TPU v7x, 32 devices: a whole 2x2x4 slice. The times are simulated.
32 devices in a mesh: proj: 8 (over z, y), band: 4 (over x, core).
Axes of the slice: x: 2, y: 2, z: 4, core: 2. Of those that a mesh axis runs over, the one named last changes fastest.
Arguments:
- intensities: bfloat16 [8, 2, 4096, 4096], P('proj', None, 'band'), may hold values from 0.1 to 700, as said below
- dist_index: int32 [8, 2], P('proj'), may hold values from 0 to 7, all different within a row
- fresnel_table: float32 [8], replicated, may hold values from 20 to 400
- proj_order: int32 [8], replicated, may hold values from 0 to 7, each once
Outputs:
- sinogram: float32 [4096, 8, 4096], P(('band', 'proj'))
Inputs may be any that keep to these rules, and one draw needn't show every extreme that they name: Positive intensities. `dist_index`: the 2 frames of one projection use 2 different settings.
All inputs are finite; a program needn't handle non-finite values.
Results may differ from a plain program's by a relative error of at most 0.0041.
Values may be sent and summed in bfloat16 or wider, within the bound.
No kernel may reach another device: no remote copies, remote signals or barrier semaphores. Data moves between devices by JAX's collectives and lax.ppermute only.
A program may use at most 256 MiB of HBM per device.

v0:
```python
import math

import jax
import jax.numpy as jnp
from jax import lax
from jax.sharding import PartitionSpec as P

alpha_reg = 0.1


def split_sizes(length, along_last):
    if along_last:
        return (length // 128, 128)
    factor_a = 1
    for candidate in range(1, length + 1):
        if candidate * candidate > length:
            break
        if length % candidate == 0:
            factor_a = candidate
    return (factor_a, length // factor_a)


def trig_table(amount, other, length):
    index_a = lax.broadcasted_iota(jnp.int32, (amount, other), 0)
    index_b = lax.broadcasted_iota(jnp.int32, (amount, other), 1)
    angle = (index_a * index_b % length).astype(jnp.float32) * (2.0 * math.pi / length)
    return (jnp.cos(angle), jnp.sin(angle))


def complex_table(size, direction):
    cosine, sine = trig_table(size, size, size)
    from_real = jnp.stack([cosine, direction * sine], axis=1)
    from_imag = jnp.stack([-direction * sine, cosine], axis=1)
    return jnp.stack([from_real, from_imag], axis=0)


def contract(pattern, values, table):
    return jnp.einsum(
        pattern, values, table, precision=lax.Precision.HIGHEST, preferred_element_type=jnp.float32
    )


def patterns(along_last):
    if along_last:
        return ("c...ab,cadk->d...kb", "c...ab,cbdk->d...ak", "c...ab,cak->...kb")
    return ("c...abl,cadk->d...kbl", "c...abl,cbdk->d...akl", "c...abl,cak->...kbl")


def transform(values, length, along_last, direction, real_only):
    factor_a, factor_b = split_sizes(length, along_last)
    if along_last:
        leading = values.shape[1:-1]
        trailing = ()
    else:
        leading = values.shape[1:-2]
        trailing = values.shape[-1:]
    values = values.reshape((2,) + leading + (factor_a, factor_b) + trailing)
    pattern_a, pattern_b, pattern_real = patterns(along_last)
    twist_cos, twist_sin = trig_table(factor_a, factor_b, length)
    if not along_last:
        twist_cos = twist_cos[:, :, None]
        twist_sin = twist_sin[:, :, None]
    table_a = complex_table(factor_a, direction)
    table_b = complex_table(factor_b, direction)
    if direction < 0:
        values = contract(pattern_a, values, table_a)
    else:
        values = contract(pattern_b, values, table_b)
    part_re = values[0]
    part_im = values[1]
    values = jnp.stack(
        [
            part_re * twist_cos - direction * part_im * twist_sin,
            part_im * twist_cos + direction * part_re * twist_sin,
        ]
    )
    full_shape = leading + (length,) + trailing
    if real_only:
        result = contract(pattern_real, values, table_a[:, :, 0, :])
        return result.reshape(full_shape) * (1.0 / length)
    if direction < 0:
        values = contract(pattern_b, values, table_b)
    else:
        values = contract(pattern_a, values, table_a)
    values = values.reshape((2,) + full_shape)
    if direction > 0:
        return values * (1.0 / length)
    return values


def freq_square(amount, length, along_last, offset):
    factor_a, factor_b = split_sizes(length, along_last)
    positions = offset + lax.broadcasted_iota(jnp.int32, (amount,), 0)
    frequency = positions // factor_b + factor_a * (positions % factor_b)
    folded = jnp.minimum(frequency, length - frequency).astype(jnp.float32) / length
    return folded * folded


def column_pass(pieces):
    shape = pieces.shape
    flat = pieces.reshape(shape[:4] + shape[5:])
    done = transform(flat, shape[3], False, -1, False)
    return done.reshape(shape)


def on_device(intensities, dist_index, fresnel_table, proj_order):
    proj_here, dist_count, band_rows, ncol_all = intensities.shape
    band_count = lax.axis_size("band")
    nrow_all = band_rows * band_count
    col_block = ncol_all // band_count
    data = intensities.astype(jnp.float32)
    totals = lax.psum(jnp.sum(data, axis=(2, 3)), "band")
    means = totals / (nrow_all * ncol_all)
    contrast = data / means[:, :, None, None] - 1.0
    packed = jnp.stack([contrast[:, 0::2], contrast[:, 1::2]])
    row_spec = transform(packed, ncol_all, True, -1, False).astype(jnp.bfloat16)
    pair_count = row_spec.shape[2]
    row_spec = row_spec.reshape((2, proj_here, pair_count, band_rows, band_count, col_block))
    pencil = lax.all_to_all(row_spec, "band", split_axis=4, concat_axis=3, tiled=True)
    spectra = column_pass(pencil)
    spectra = spectra.reshape((2, proj_here, pair_count, nrow_all, col_block))
    spec_re = spectra[0]
    spec_im = spectra[1]
    table_size = fresnel_table.shape[0]
    onehot = (
        dist_index[:, :, None] == lax.broadcasted_iota(jnp.int32, (1, 1, table_size), 2)
    ).astype(jnp.float32)
    coefficient = jnp.sum(onehot * fresnel_table[None, None, :], axis=2)
    band_index = lax.axis_index("band")
    freq_sq = (
        freq_square(nrow_all, nrow_all, False, 0)[:, None]
        + freq_square(col_block, ncol_all, True, band_index * col_block)[None, :]
    )
    sines = jnp.sin(math.pi * coefficient[:, :, None, None] * freq_sq[None, None, :, :])
    denominator = 2.0 * jnp.sum(sines * sines, axis=1) + alpha_reg
    sines_even = sines[:, 0::2]
    sines_odd = sines[:, 1::2]
    phase_re = jnp.sum(spec_re * sines_even + spec_im * sines_odd, axis=1) / denominator
    phase_im = jnp.sum(spec_im * sines_even - spec_re * sines_odd, axis=1) / denominator
    phase_spec = jnp.stack([phase_re, phase_im])
    send = transform(phase_spec, nrow_all, False, 1, False).astype(jnp.bfloat16)
    rows_back = lax.all_to_all(send, "band", split_axis=2, concat_axis=3, tiled=True)
    phase = transform(rows_back, ncol_all, True, 1, True)
    gathered = lax.all_to_all(phase, "proj", split_axis=1, concat_axis=0, tiled=True)
    proj_total = gathered.shape[0]
    placement = (
        proj_order[None, :] == lax.broadcasted_iota(jnp.int32, (proj_total, proj_total), 0)
    ).astype(jnp.float32)
    return jnp.einsum(
        "sq,qrc->rsc",
        placement,
        gathered,
        precision=lax.Precision.HIGHEST,
        preferred_element_type=jnp.float32,
    )


def solution(mesh):
    in_specs = (P("proj", None, "band", None), P("proj", None), P(), P())
    out_specs = P(("band", "proj"), None, None)
    return jax.shard_map(
        on_device, mesh=mesh, in_specs=in_specs, out_specs=out_specs, check_vma=False
    )
```

profile of v0, /device:TPU:0, one launch (start us, length us, event | category | flops | bytes accessed | tf_op | source)
XLA Modules:
  0.0 1606.2 jit_solution(9936141451648006591)
XLA Ops:
  0.3 0.3 broadcast_multiply_fusion
  0.5 0.3 fusion.79
  0.8 10.9 convert_reduce_fusion
  11.7 8.3 psum.7
  20.0 19.0 %fusion = f32[1,2,1024,4096]{3,2,1,0:T(8,128)} fusion(bf16[1,2,1024,4096]{3,2,1,0:T(8,128)(2,1)} %param.4, f32[2]{0:T(128)S(1)} %multiply_bitcast_fusion), kind=kLoop, calls=%fused_computation.2 | loop fusion | flops 25165824 | bytes 50331656 | tf_op jit(solution)/shard_map/sub | solution.py:114
  39.0 17.8 %slice_bitcast_fusion.3 = (f32[128,8,32,128]{3,1,2,0:T(8,128)}, f32[128,8,32,128]{3,1,2,0:T(8,128)S(1)}) fusion(f32[1,2,1024,4096]{3,2,1,0:T(8,128)} %fusion), kind=kLoop, calls=%fused_computation.37 | loop fusion | bytes 67108864
  56.9 14.1 copy.123
  70.9 7.0 copy.124
  78.0 0.6 fusion.59
  78.6 37.8 %fusion.17 = f32[2,1,1,1024,32,128]{5,4,3,0,2,1:T(8,128)} fusion(f32[1,1,1,1024,32,128]{5,4,0,3,2,1:T(8,128)} %bitcast.227, f32[1,1,1,1024,32,128]{5,4,0,3,2,1:T(8,128)} %bitcast.226, f32[1,32,2,32]{1,3,0,2:T(8,128)S(1)} %get-tuple-element.32, f32[1,32,2,32]{1,3,0,2:T(8,128)S(1)} %get-tuple-element.37), kind=kOutput, calls=%fused_computation.29 | convolution fusion | flops 6450843648 | bytes 67125248 | tf_op jit(solution)/shard_map/c...ab,cadk->d...kb/dot_general | solution.py:38
  116.4 18.0 %multiply_subtract_fusion.3 = (f32[1,1,1,1024,32,128]{5,4,3,0,2,1:T(8,128)S(1)}, f32[1,1,1,1024,32,128]{5,4,3,0,2,1:T(8,128)}) fusion(f32[2,1,1,1024,32,128]{5,4,3,0,2,1:T(8,128)} %fusion.17, f32[32,128]{1,0:T(8,128)S(1)} %get-tuple-element.41, f32[32,128]{1,0:T(8,128)S(1)} %get-tuple-element.42), kind=kLoop, calls=%fused_computation.60 | loop fusion | flops 25165824 | bytes 67141632 | tf_op jit(solution)/shard_map/sub | solution.py:73
  134.4 18.6 %maximum_bitcast_fusion.2 = f32[2,1024,32,128]{3,2,1,0:T(8,128)} fusion(f32[1,1,1,1024,32,128]{5,4,3,0,2,1:T(8,128)} %get-tuple-element.14, f32[1,1,1,1024,32,128]{5,4,3,0,2,1:T(8,128)S(1)} %get-tuple-element.13), kind=kLoop, calls=%fused_computation.7 | loop fusion | flops 8388608 | bytes 67108864 | tf_op jit(solution)/shard_map/reshape.13
  153.0 0.7 fusion.41
  153.7 57.7 %bitcast_convert_fusion = bf16[2,128,1024,32]{2,1,3,0:T(8,128)(2,1)} fusion(f32[2,1024,32,128]{3,2,1,0:T(8,128)} %maximum_bitcast_fusion.2, f32[1,128,2,128]{1,3,0,2:T(8,128)S(1)} %get-tuple-element.22, f32[1,128,2,128]{1,3,0,2:T(8,128)S(1)} %get-tuple-element.25), kind=kOutput, calls=%fused_computation.21 | convolution fusion | flops 25778257920 | bytes 50593792 | tf_op jit(solution)/shard_map/c...ab,cbdk->d...ak/dot_general | solution.py:38
  211.4 21.6 %copy.81 = bf16[2,1,1,1024,4,1024]{5,3,0,2,1,4:T(8,128)(2,1)} copy(bf16[2,1,1,1024,4,1024]{3,5,4,0,2,1:T(8,128)(2,1)} %bitcast.225) | data formatting | bytes 33554432 | tf_op jit(solution)/shard_map/convert_element_type | solution.py:116
  233.0 7.2 all-to-all-start
  240.4 0.7 copy.86
  241.2 0.7 copy.87
  242.1 0.2 fusion.123
  242.4 0.7 fusion.47
  243.1 7.3 broadcast_add_fusion
  250.4 122.0 %multiply_reduce_fusion = (f32[4096,1024]{1,0:T(8,128)}, f32[1,2,4096,1024]{3,2,1,0:T(8,128)}) fusion(f32[4096,1024]{1,0:T(8,128)} %broadcast_add_fusion, f32[2]{0:T(128)S(1)} %broadcast_multiply_fusion.5), kind=kLoop, calls=%fused_computation.27 | loop fusion | flops 20971520 | bytes 67108872 | tf_op jit(solution)/shard_map/reduce_sum | solution.py:135
  372.4 50.9 %all-to-all-done = bf16[2,1,1,1024,4,1024]{5,3,0,2,1,4:T(8,128)(2,1)} async-done(((bf16[2,1,1,1024,4,1024]{5,3,0,2,1,4:T(8,128)(2,1)}), bf16[2,1,1,1024,4,1024]{5,3,0,2,1,4:T(8,128)(2,1)}, u32[]{:S(2)}, u32[]{:S(2)}) %all-to-all-start) | async-done | bytes 16777248 | tf_op jit(solution)/shard_map/all_to_all | solution.py:119
  423.3 13.9 copy.82
  437.2 44.5 %convolution_bitcast_fusion.1 = f32[2,64,64,1024]{3,1,2,0:T(8,128)} fusion(bf16[2,64,64,1024]{3,2,1,0:T(8,128)(2,1)} %bitcast.222, f32[1,64,2,64]{1,3,0,2:T(8,128)S(1)} %get-tuple-element.28, f32[1,64,2,64]{1,3,0,2:T(8,128)S(1)} %get-tuple-element.35), kind=kOutput, calls=%fused_computation.31 | convolution fusion | flops 12884918272 | bytes 50397184 | tf_op jit(solution)/shard_map/c...abl,cadk->d...kbl/dot_general | solution.py:38
  481.7 17.7 %multiply_subtract_fusion.2 = (f32[1,1,1,64,64,1024]{5,3,4,2,1,0:T(8,128)S(1)}, f32[1,1,1,64,64,1024]{5,3,4,2,1,0:T(8,128)}) fusion(f32[2,64,64,1024]{3,1,2,0:T(8,128)} %convolution_bitcast_fusion.1, f32[64,64]{0,1:T(8,128)S(1)} %get-tuple-element.47, f32[64,64]{0,1:T(8,128)S(1)} %get-tuple-element.48), kind=kLoop, calls=%fused_computation.58 | loop fusion | flops 25165824 | bytes 67141632 | tf_op jit(solution)/shard_map/sub | solution.py:73
  499.4 18.6 %maximum_bitcast_fusion.3 = f32[2,64,64,1024]{3,1,2,0:T(8,128)} fusion(f32[1,1,1,64,64,1024]{5,3,4,2,1,0:T(8,128)} %get-tuple-element.10, f32[1,1,1,64,64,1024]{5,3,4,2,1,0:T(8,128)S(1)} %get-tuple-element.9), kind=kLoop, calls=%fused_computation.8 | loop fusion | flops 8388608 | bytes 67108864 | tf_op jit(solution)/shard_map/reshape.28
  518.0 58.4 %fusion.19 = f32[2,1,1,64,64,1024]{5,4,3,0,2,1:T(8,128)} fusion(f32[2,64,64,1024]{3,1,2,0:T(8,128)} %maximum_bitcast_fusion.3, f32[1,64,2,64]{1,3,0,2:T(8,128)S(1)} %get-tuple-element.28, f32[1,64,2,64]{1,3,0,2:T(8,128)S(1)} %get-tuple-element.35), kind=kOutput, calls=%fused_computation.33 | convolution fusion | flops 12884918272 | bytes 67174400 | tf_op jit(solution)/shard_map/c...abl,cbdk->d...akl/dot_general | solution.py:38
  576.4 21.9 %fusion.130 = (f32[1,1,1,64,64,1024]{5,4,3,0,2,1:T(8,128)}, f32[1,1,1,64,64,1024]{5,4,3,0,2,1:T(8,128)}) fusion(f32[2,1,1,64,64,1024]{5,4,3,0,2,1:T(8,128)} %fusion.19), kind=kLoop, calls=%fused_computation.210 | loop fusion | bytes 67108864 | tf_op jit(solution)/shard_map/slice | solution.py:122
  598.2 40.5 %bitcast_divide_fusion.1 = (f32[1,1,4096,1024]{3,2,1,0:T(8,128)}, f32[1,1,4096,1024]{3,2,1,0:T(8,128)}) fusion(f32[1,1,1,64,64,1024]{5,4,3,0,2,1:T(8,128)} %get-tuple-element.16, f32[1,1,1,64,64,1024]{5,4,3,0,2,1:T(8,128)} %get-tuple-element.15, f32[1,2,4096,1024]{3,2,1,0:T(8,128)} %get-tuple-element.20, f32[4096,1024]{1,0:T(8,128)} %get-tuple-element.19), kind=kLoop, calls=%fused_computation.41 | loop fusion | flops 41943040 | bytes 117440512 | tf_op jit(solution)/shard_map/div | solution.py:138
  638.8 37.2 %fusion.18 = f32[2,1,64,64,1024]{4,3,2,0,1:T(8,128)} fusion(f32[1,1,64,64,1024]{4,3,0,2,1:T(8,128)} %bitcast.229, f32[1,1,64,64,1024]{4,3,0,2,1:T(8,128)} %bitcast.228, f32[1,64,2,64]{1,3,2,0:T(8,128)S(1)} %copy-done.1, f32[1,64,2,64]{1,3,2,0:T(8,128)S(1)} %copy-done), kind=kOutput, calls=%fused_computation.32 | convolution fusion | flops 12893306880 | bytes 67174400 | tf_op jit(solution)/shard_map/c...abl,cbdk->d...akl/dot_general | solution.py:38
  676.0 17.6 %multiply_subtract_fusion.1 = (f32[1,1,64,64,1024]{4,3,2,0,1:T(8,128)S(1)}, f32[1,1,64,64,1024]{4,3,2,0,1:T(8,128)}) fusion(f32[2,1,64,64,1024]{4,3,2,0,1:T(8,128)} %fusion.18, f32[64,64]{1,0:T(8,128)S(1)} %copy-done.7, f32[64,64]{1,0:T(8,128)S(1)} %copy-done.6), kind=kLoop, calls=%fused_computation.55 | loop fusion | flops 25165824 | bytes 67141632 | tf_op jit(solution)/shard_map/sub | solution.py:73
  693.7 18.6 %maximum_bitcast_fusion.6 = f32[2,64,64,1024]{3,2,1,0:T(8,128)} fusion(f32[1,1,64,64,1024]{4,3,2,0,1:T(8,128)} %get-tuple-element.8, f32[1,1,64,64,1024]{4,3,2,0,1:T(8,128)S(1)} %get-tuple-element.7), kind=kLoop, calls=%fused_computation.13 | loop fusion | flops 8388608 | bytes 67108864 | tf_op jit(solution)/shard_map/reshape.47
  712.3 59.3 %fusion.7 = bf16[2,64,64,1024]{3,1,2,0:T(8,128)(2,1)} fusion(f32[2,64,64,1024]{3,2,1,0:T(8,128)} %maximum_bitcast_fusion.6, f32[1,64,2,64]{1,3,2,0:T(8,128)S(1)} %copy-done.1, f32[1,64,2,64]{1,3,2,0:T(8,128)S(1)} %copy-done), kind=kOutput, calls=%fused_computation.16 | convolution fusion | flops 12901695488 | bytes 50397184 | tf_op jit(solution)/shard_map/c...abl,cadk->d...kbl/dot_general | solution.py:38
  771.6 15.4 copy.90
  787.1 57.5 %copy.91 = bf16[2,1,4096,1024]{3,0,1,2:T(2,128)(2,1)} copy(bf16[2,1,4096,1024]{3,2,0,1:T(8,128)(2,1)S(1)} %bitcast.230) | data formatting | bytes 33554432 | tf_op jit(solution)/shard_map/convert_element_type | solution.py:141
  844.6 7.0 all-to-all-start.1
  851.6 183.0 %all-to-all-done.1 = bf16[2,1,4096,1024]{3,0,1,2:T(2,128)(2,1)} async-done(((bf16[2,1,4096,1024]{3,0,1,2:T(2,128)(2,1)}), bf16[2,1,4096,1024]{3,0,1,2:T(2,128)(2,1)}, u32[]{:S(2)}, u32[]{:S(2)}) %all-to-all-start.1) | async-done | bytes 16777248 | tf_op jit(solution)/shard_map/all_to_all | solution.py:142
  1034.6 16.4 %copy.92 = bf16[2,1,4096,1024]{3,2,0,1:T(8,128)(2,1)} copy(bf16[2,1,4096,1024]{3,0,1,2:T(2,128)(2,1)} %all-to-all-done.1) | data formatting | bytes 33554432 | tf_op jit(solution)/shard_map/all_to_all | solution.py:142
  1051.1 21.6 %copy.93 = bf16[2,1,1024,4,1024]{2,4,3,0,1:T(8,128)(2,1)} copy(bf16[2,1,1024,4,1024]{4,2,3,0,1:T(8,128)(2,1)} %bitcast.231) | data formatting | bytes 33554432 | tf_op jit(solution)/shard_map/all_to_all | solution.py:142
  1072.7 22.2 %convolution_bitcast_fusion = f32[2,1,1024,32,128]{2,4,3,0,1:T(8,128)} fusion(bf16[2,1024,32,128,1]{1,3,2,0,4:T(8,128)(2,1)} %bitcast.224, f32[1,128,2,128]{1,3,2,0:T(8,128)S(1)} %copy-done.3, f32[1,128,2,128]{1,3,2,0:T(8,128)S(1)} %copy-done.2), kind=kOutput, calls=%fused_computation.30 | convolution fusion | flops 25769869312 | bytes 50593792 | tf_op jit(solution)/shard_map/c...ab,cbdk->d...ak/dot_general | solution.py:38
  1094.9 17.7 %multiply_subtract_fusion = (f32[1,1,1024,32,128]{2,4,3,0,1:T(8,128)S(1)}, f32[1,1,1024,32,128]{2,4,3,0,1:T(8,128)}) fusion(f32[2,1,1024,32,128]{2,4,3,0,1:T(8,128)} %convolution_bitcast_fusion, f32[32,128]{1,0:T(8,128)S(1)} %fusion.106, f32[32,128]{1,0:T(8,128)S(1)} %copy-done.5), kind=kLoop, calls=%fused_computation.53 | loop fusion | flops 25165824 | bytes 67141632 | tf_op jit(solution)/shard_map/sub | solution.py:73
  1112.6 18.6 %maximum_bitcast_fusion.7 = f32[2,1024,32,128]{1,3,2,0:T(8,128)} fusion(f32[1,1,1024,32,128]{2,4,3,0,1:T(8,128)} %get-tuple-element.12, f32[1,1,1024,32,128]{2,4,3,0,1:T(8,128)S(1)} %get-tuple-element.11), kind=kLoop, calls=%fused_computation.14 | loop fusion | flops 8388608 | bytes 67108864 | tf_op jit(solution)/shard_map/reshape.57
  1131.2 33.9 %copy.96 = f32[2,1024,32,128]{3,2,0,1:T(8,128)} copy(f32[2,1024,32,128]{1,3,2,0:T(8,128)} %maximum_bitcast_fusion.7) | data formatting | bytes 67108864 | tf_op jit(solution)/shard_map/reshape.57
  1165.2 23.7 %bitcast_multiply_fusion.1 = f32[32,1024,128]{2,0,1:T(8,128)S(1)} fusion(f32[2,1024,32,128]{3,2,0,1:T(8,128)} %copy.96, f32[1,32,2,32]{1,3,2,0:T(8,128)S(1)} %copy-done.9, f32[1,32,2,32]{1,3,2,0:T(8,128)S(1)} %copy-done.8), kind=kOutput, calls=%fused_computation.38 | convolution fusion | flops 3225421824 | bytes 50348032 | tf_op jit(solution)/shard_map/c...ab,cak->...kb/dot_general | solution.py:38
  1188.9 369.0 %all_to_all.42 = f32[1,1024,4096]{2,0,1:T(1,128)S(1)} all-to-all(f32[1,1024,4096]{2,0,1:T(1,128)S(1)} %bitcast.223), channel_id=1, replica_groups=mesh['proj'=8,'band'=4] {'proj'}, dimensions={1} | all-to-all | bytes 33554432 | tf_op jit(solution)/shard_map/all_to_all | solution.py:144
  1557.9 19.0 %copy.122 = f32[1,1024,4096]{2,1,0:T(8,128)} copy(f32[1,1024,4096]{2,0,1:T(1,128)S(1)} %all_to_all.42) | data formatting | bytes 33554432
  1576.9 28.9 %fusion.33 = f32[128,8,4096]{2,1,0:T(8,128)} fusion(f32[8,128,4096]{2,1,0:T(8,128)} %bitcast.232, s32[8]{0:T(128)S(1)} %copy-done.10), kind=kOutput, calls=%fused_computation.61 | convolution fusion | flops 402653248 | bytes 33554464 | tf_op jit(solution)/shard_map/sq,qrc->rsc/dot_general | solution.py:149
  (38 shorter events, 1.0 us)
Async XLA Ops:
  0.3 116.2 %copy-start.4 = (f32[32,128]{1,0:T(8,128)}, f32[32,128]{1,0:T(8,128)S(1)}, u32[]{:S(2)}) copy-start(f32[32,128]{1,0:T(8,128)S(1)} %get-tuple-element.42) | copy-start | bytes 49156
  233.0 9.1 copy-start.11
  233.0 9.1 copy-start.12
  233.0 190.3 %all-to-all-start = ((bf16[2,1,1,1024,4,1024]{5,3,0,2,1,4:T(8,128)(2,1)}), bf16[2,1,1,1024,4,1024]{5,3,0,2,1,4:T(8,128)(2,1)}, u32[]{:S(2)}, u32[]{:S(2)}) async-start(bf16[2,1,1,1024,4,1024]{5,3,0,2,1,4:T(8,128)(2,1)} %copy.81), calls=%async_computation | async-start | bytes 33554432 | tf_op jit(solution)/shard_map/all_to_all | solution.py:119
  598.2 40.5 %copy-start = (f32[1,64,2,64]{1,3,2,0:T(8,128)S(1)}, f32[1,64,2,64]{1,3,2,0:T(8,128)}, u32[]{:S(2)}) copy-start(f32[1,64,2,64]{1,3,2,0:T(8,128)} %get-tuple-element.27) | copy-start | bytes 98308
  598.2 40.5 %copy-start.1 = (f32[1,64,2,64]{1,3,2,0:T(8,128)S(1)}, f32[1,64,2,64]{1,3,2,0:T(8,128)}, u32[]{:S(2)}) copy-start(f32[1,64,2,64]{1,3,2,0:T(8,128)} %get-tuple-element.36) | copy-start | bytes 98308
  638.8 37.2 %copy-start.6 = (f32[64,64]{1,0:T(8,128)S(1)}, f32[64,64]{1,0:T(8,128)}, u32[]{:S(2)}) copy-start(f32[64,64]{1,0:T(8,128)} %copy.86) | copy-start | bytes 49156
  638.8 37.2 %copy-start.7 = (f32[64,64]{1,0:T(8,128)S(1)}, f32[64,64]{1,0:T(8,128)}, u32[]{:S(2)}) copy-start(f32[64,64]{1,0:T(8,128)} %copy.87) | copy-start | bytes 49156
  844.6 190.0 %all-to-all-start.1 = ((bf16[2,1,4096,1024]{3,0,1,2:T(2,128)(2,1)}), bf16[2,1,4096,1024]{3,0,1,2:T(2,128)(2,1)}, u32[]{:S(2)}, u32[]{:S(2)}) async-start(bf16[2,1,4096,1024]{3,0,1,2:T(2,128)(2,1)} %copy.91), calls=%async_computation.1 | async-start | bytes 33554432 | tf_op jit(solution)/shard_map/all_to_all | solution.py:142
  1051.1 21.6 %copy-start.2 = (f32[1,128,2,128]{1,3,2,0:T(8,128)S(1)}, f32[1,128,2,128]{1,3,2,0:T(8,128)}, u32[]{:S(2)}) copy-start(f32[1,128,2,128]{1,3,2,0:T(8,128)} %get-tuple-element.21) | copy-start | bytes 393220
  1051.1 21.6 %copy-start.3 = (f32[1,128,2,128]{1,3,2,0:T(8,128)S(1)}, f32[1,128,2,128]{1,3,2,0:T(8,128)}, u32[]{:S(2)}) copy-start(f32[1,128,2,128]{1,3,2,0:T(8,128)} %get-tuple-element.26) | copy-start | bytes 393220
  1072.7 22.2 %copy-start.5 = (f32[32,128]{1,0:T(8,128)S(1)}, f32[32,128]{1,0:T(8,128)}, u32[]{:S(2)}) copy-start(f32[32,128]{1,0:T(8,128)} %copy-done.4) | copy-start | bytes 49156
  1131.2 33.9 %copy-start.8 = (f32[1,32,2,32]{1,3,2,0:T(8,128)S(1)}, f32[1,32,2,32]{1,3,2,0:T(8,128)}, u32[]{:S(2)}) copy-start(f32[1,32,2,32]{1,3,2,0:T(8,128)} %get-tuple-element.31) | copy-start | bytes 24580
  1131.2 33.9 %copy-start.9 = (f32[1,32,2,32]{1,3,2,0:T(8,128)S(1)}, f32[1,32,2,32]{1,3,2,0:T(8,128)}, u32[]{:S(2)}) copy-start(f32[1,32,2,32]{1,3,2,0:T(8,128)} %get-tuple-element.38) | copy-start | bytes 24580
  1557.9 19.0 %copy-start.10 = (s32[8]{0:T(128)S(1)}, s32[8]{0:T(128)}, u32[]{:S(2)}) copy-start(s32[8]{0:T(128)} %param.7) | copy-start | bytes 100
where the time goes:
time: 1620 us; the launch traced here: 1610 us
  blocking collectives  377 us (23%)
  matrix products  370 us (23%)
  other arithmetic  349 us (22%)
  local copies, waits for them, and re-layouts  262 us (16%)
  waiting for transfers between devices  234 us (14%)
    all_to_all x1, blocking collectives, on_device(): lax.all_to_all(phase, 'proj', split_axis=1, concat_axis=0, tiled=True)  369 us
    dot_general x8, matrix products, contract(): jnp.einsum(pattern, values, table, precision=lax.Precision.HIGHEST, prefe...  341 us
    all_to_all x1, waiting for transfers between devices, on_device(): lax.all_to_all(send, 'band', split_axis=2, concat_axis=3, tiled=True)  183 us
    reduce_sum x1, other arithmetic, on_device(): denominator = 2.0 * jnp.sum(sines * sines, axis=1) + alpha_reg  122 us
    another operation x4, other arithmetic  74.4 us
    convert_element_type x2, local copies, waits for them, and re-layouts, on_device(): send = transform(phase_spec, nrow_all, False, 1, False).astype(jnp.bfloat16)  72.9 us
    sub x4, other arithmetic, transform(): part_re * twist_cos - direction * part_im * twist_sin  71 us
    unnamed x30, local copies, waits for them, and re-layouts  58 us
  transfers between devices with their start and end apart: 2, of which 2 were waited for; matrix products, arithmetic and copies ran while one was open for 8% of the time, Pallas kernels for 0%

commit v1 on v0

v1 whole, which is shorter than its diff:
```python
import functools
import math

import jax
import jax.numpy as jnp
import numpy as np
from jax import lax
from jax.experimental import pallas as pl
from jax.experimental.pallas import tpu as pltpu
from jax.sharding import PartitionSpec as P

alpha_reg = 0.1
LENGTH = 4096
MAJOR = 32
MINOR = 128
HALF = MAJOR // 2
F32 = jnp.float32
BF16 = jnp.bfloat16
MIB = 1 << 20


def split_table(table):
    high = table.astype(np.float32).astype(jnp.bfloat16)
    low = (table - high.astype(np.float64)).astype(np.float32).astype(jnp.bfloat16)
    return high, low


def as_real(table):
    return np.block([[table.real, table.imag], [-table.imag, table.real]])


@functools.lru_cache(maxsize=None)
def step_tables():
    k = np.arange(MAJOR)[:, None, None]
    b = np.arange(MINOR)[None, :, None]
    s = np.arange(MINOR)[None, None, :]
    return np.exp(-2j * math.pi * ((b * (k + MAJOR * s)) % LENGTH) / LENGTH)


@functools.lru_cache(maxsize=None)
def row_tables():
    step = step_tables()
    out = np.zeros((34, 2 * MINOR, 2 * MINOR))
    for t in range(1, HALF):
        out[2 * t] = as_real(step[t])
        out[2 * t + 1] = as_real(step[MAJOR - t][:, ::-1])
    half = MINOR // 2
    zero = np.zeros((MINOR, half), np.complex128)
    negative = step[0][:, (-np.arange(half)) % MINOR].copy()
    negative[:, 0] = step[0][:, half]
    out[0] = as_real(np.concatenate([step[0][:, :half], zero], 1))
    out[1] = as_real(np.concatenate([negative, zero], 1))
    out[32] = as_real(np.concatenate([zero, step[HALF][:, :half]], 1))
    out[33] = as_real(np.concatenate([zero, step[HALF][:, ::-1][:, :half]], 1))
    return split_table(out)


@functools.lru_cache(maxsize=None)
def column_tables():
    inverse = np.stack([as_real(table) for table in step_tables()])
    return split_table(inverse.transpose(0, 2, 1)), split_table(inverse)


@functools.lru_cache(maxsize=None)
def final_tables():
    step = step_tables()
    out = np.zeros((HALF, 4 * MINOR, 2 * MINOR))
    eye = np.eye(MINOR)
    conjugate = np.diag(np.concatenate([np.ones(MINOR), -np.ones(MINOR)]))
    for t in range(1, HALF):
        turn = np.exp(2j * math.pi * t / MAJOR)
        out[t, : 2 * MINOR] = as_real((1 + 1j * turn) * np.conj(step[t]).T)
        partner = as_real(np.conj(step[HALF - t]).T)
        out[t, 2 * MINOR :] = partner @ conjugate @ as_real((1 - 1j * turn) * eye)
    half = MINOR // 2
    b = np.arange(MINOR)[None, :]
    s = np.arange(half)[:, None]
    even = 2 * math.pi * (b * s) / MINOR
    odd = 2 * math.pi * (b * (HALF + MAJOR * s)) / LENGTH
    first_re, first_im = 2 * np.cos(even), -2 * np.sin(even)
    first_re[0] = 1.0
    first_im[0] = (-1.0) ** np.arange(MINOR)
    second_re, second_im = 2 * np.cos(odd), -2 * np.sin(odd)
    first = np.concatenate([first_re, 0 * second_re, first_im, 0 * second_im], 0)
    second = np.concatenate([0 * first_re, second_re, 0 * first_im, second_im], 0)
    out[0, : 2 * MINOR] = np.concatenate([first + second, first - second], 1)
    return split_table(out / float(LENGTH * LENGTH))


def add(x, y):
    return (x[0] + y[0], x[1] + y[1])


def sub(x, y):
    return (x[0] - y[0], x[1] - y[1])


def turn(x, index, length):
    index = index % length
    re, im = x
    if index == 0:
        return x
    if 4 * index == length:
        return (im, -re)
    if 2 * index == length:
        return (-re, -im)
    if 4 * index == 3 * length:
        return (-im, re)
    angle = 2.0 * math.pi * index / length
    cosine, sine = math.cos(angle), math.sin(angle)
    if 8 * index == length:
        return ((re + im) * cosine, (im - re) * cosine)
    if 8 * index == 3 * length:
        return ((im - re) * sine, (re + im) * (-sine))
    return (re * cosine + im * sine, im * cosine - re * sine)


def dft4(x):
    a, b = add(x[0], x[2]), sub(x[0], x[2])
    c, d = add(x[1], x[3]), sub(x[1], x[3])
    return [add(a, c), (b[0] + d[1], b[1] - d[0]), sub(a, c), (b[0] - d[1], b[1] + d[0])]


def dft8(x):
    even, odd = dft4(x[0::2]), dft4(x[1::2])
    odd = [turn(value, index, 8) for index, value in enumerate(odd)]
    return [add(e, o) for e, o in zip(even, odd)] + [sub(e, o) for e, o in zip(even, odd)]


def dft16(x):
    middle = [dft4([x[4 * a + b] for a in range(4)]) for b in range(4)]
    out = [None] * 16
    for k in range(4):
        part = dft4([turn(middle[b][k], b * k, 16) for b in range(4)])
        for m in range(4):
            out[k + 4 * m] = part[m]
    return out


def dft32(load, store, mid_ref):
    for b in range(8):
        part = dft4([load(8 * a + b) for a in range(4)])
        for k in range(4):
            re, im = turn(part[k], b * k, 32)
            mid_ref[2 * (8 * k + b)] = re
            mid_ref[2 * (8 * k + b) + 1] = im
    for k in range(4):
        part = dft8([(mid_ref[2 * (8 * k + b)], mid_ref[2 * (8 * k + b) + 1]) for b in range(8)])
        for m in range(8):
            store(k + 4 * m, *part[m])


def dot(x, y):
    return jnp.dot(x, y, preferred_element_type=F32)


def row_kernel(chunks, bands, scale_ref, x_ref, high_ref, low_ref, *rest):
    outs, (mid_ref, xs_ref) = rest[:chunks], rest[chunks:]
    rows_here = x_ref.shape[2]
    scale_even, scale_odd = scale_ref[0, 0], scale_ref[0, 1]

    def group(index, carry):
        rows = pl.ds(pl.multiple_of(index * 16, 16), 16)

        def load(a):
            lanes = slice(MINOR * a, MINOR * (a + 1))
            even = x_ref[0, 0, rows, lanes].astype(F32) * scale_even - 1.0
            odd = x_ref[0, 1, rows, lanes].astype(F32) * scale_odd - 1.0
            return even, odd

        def store(k, re, im):
            for place, value in enumerate((re, im)):
                high = value.astype(BF16)
                low = (value - high.astype(F32)).astype(BF16)
                xs_ref[k, rows, MINOR * place : MINOR * (place + 1)] = high
                xs_ref[k, rows, MINOR * (2 + place) : MINOR * (3 + place)] = low

        dft32(load, store, mid_ref)
        return carry

    lax.fori_loop(0, rows_here // 16, group, 0)

    def apply(k, table):
        values = xs_ref[k]
        high = high_ref[table]
        whole = jnp.concatenate([values, values[:, : 2 * MINOR]], axis=1)
        return dot(whole, jnp.concatenate([high, high, low_ref[table]], axis=0))

    width = 2 * MINOR
    outs[0][0, :, :width] = (apply(0, 0) + apply(HALF, 32)).astype(BF16)
    outs[0][0, :, width:] = (apply(0, 1) + apply(HALF, 33)).astype(BF16)
    for chunk in range(chunks):

        def tile(band, carry, chunk=chunk):
            t = chunk * bands + band
            outs[chunk][band, :, :width] = apply(t, 2 * t).astype(BF16)
            outs[chunk][band, :, width:] = apply(MAJOR - t, 2 * t + 1).astype(BF16)
            return carry

        lax.fori_loop(1 if chunk == 0 else 0, bands, tile, 0)


def whole_spec():
    return pl.BlockSpec(memory_space=pltpu.VMEM)


def fixed_spec(shape):
    return pl.BlockSpec(shape, lambda *_: (0,) * len(shape), pipeline_mode=pl.Buffered(1))


def rows_forward(intensities, scale, bands, chunks):
    rows = intensities.shape[2]
    block = min(256, rows)
    high, low = row_tables()
    width = 4 * MINOR
    return pl.pallas_call(
        functools.partial(row_kernel, chunks, bands),
        grid=(rows // block,),
        in_specs=[
            pl.BlockSpec(memory_space=pltpu.SMEM),
            pl.BlockSpec((1, 2, block, LENGTH), lambda i: (0, 0, i, 0)),
            fixed_spec(high.shape),
            fixed_spec(low.shape),
        ],
        out_specs=[pl.BlockSpec((bands, block, width), lambda i: (0, i, 0))] * chunks,
        out_shape=[jax.ShapeDtypeStruct((bands, rows, width), BF16)] * chunks,
        scratch_shapes=[
            pltpu.VMEM((64, 16, MINOR), F32),
            pltpu.VMEM((MAJOR, block, 4 * MINOR), BF16),
        ],
        compiler_params=pltpu.CompilerParams(vmem_limit_bytes=48 * MIB),
        cost_estimate=pl.CostEstimate(
            flops=rows * 34 * 6 * 256 * 256, bytes_accessed=4 * rows * LENGTH * 2 + 9 * MIB, transcendentals=0
        ),
        name="rows_forward",
    )(scale, intensities, jnp.asarray(high), jnp.asarray(low))


def column_kernel(special, first_ref, x_ref, u_ref, v_ref, fh_ref, fl_ref, ih_ref, il_ref, *rest):
    if special:
        nyquist_ref, out_ref, mid_ref, xs_ref, ys_ref = rest
        lane = lax.broadcasted_iota(jnp.int32, (16, MINOR), 1)
        own = (lane == 0) & (first_ref[0] == 1)
    else:
        out_ref, mid_ref, xs_ref, ys_ref = rest

    def forward(index, carry):
        start = pl.multiple_of(index * 16, 16)
        rows = pl.ds(start, 16)
        below = pl.ds(pl.multiple_of(start + MINOR, 16), 16)
        for frame in range(2):

            def load(a, frame=frame):
                pos_re, pos_im, neg_re, neg_im = [
                    x_ref[a, rows, MINOR * i : MINOR * (i + 1)].astype(F32) for i in range(4)
                ]
                if special:
                    neg_re = jnp.where(own, pos_re, neg_re)
                    neg_im = jnp.where(own, pos_im, neg_im)
                if frame == 0:
                    return pos_re + neg_re, pos_im - neg_im
                return pos_im + neg_im, neg_re - pos_re

            def store(k, re, im, frame=frame):
                lanes = slice(MINOR * frame, MINOR * (frame + 1))
                xs_ref[k, rows, lanes] = re.astype(BF16)
                xs_ref[k, below, lanes] = im.astype(BF16)

            dft32(load, store, mid_ref)
        return carry

    lax.fori_loop(0, MINOR // 16, forward, 0)

    sin_even_v, cos_even_v, sin_odd_v, cos_odd_v = [v_ref[i : i + 1, :] for i in range(4)]

    def middle(k, carry):
        values = xs_ref[k]
        table = jnp.concatenate([fh_ref[k], fl_ref[k]], axis=1)
        spectra = dot(table, jnp.concatenate([values, values], axis=0))
        column = u_ref[k]
        sin_even = column[:, 0:1] * cos_even_v + column[:, 1:2] * sin_even_v
        sin_odd = column[:, 2:3] * cos_odd_v + column[:, 3:4] * sin_odd_v
        scale = 1.0 / (4.0 * (sin_even * sin_even + sin_odd * sin_odd) + 2.0 * alpha_reg)
        sin_even = sin_even * scale
        sin_odd = sin_odd * scale
        phase_re = sin_even * spectra[:MINOR, :MINOR] + sin_odd * spectra[:MINOR, MINOR:]
        phase_im = sin_even * spectra[MINOR:, :MINOR] + sin_odd * spectra[MINOR:, MINOR:]
        phase = jnp.concatenate([phase_re.astype(BF16), phase_im.astype(BF16)], axis=0)
        table = jnp.concatenate([ih_ref[k], il_ref[k]], axis=1)
        ys_ref[k] = dot(table, jnp.concatenate([phase, phase], axis=0))
        return carry

    lax.fori_loop(0, MAJOR, middle, 0)

    def inverse(index, carry):
        start = pl.multiple_of(index * 16, 16)
        rows = pl.ds(start, 16)
        below = pl.ds(pl.multiple_of(start + MINOR, 16), 16)

        def load(k):
            return ys_ref[k, below, :], ys_ref[k, rows, :]

        def store(a, im, re):
            if special:
                im = jnp.where(own, nyquist_ref[rows, a : a + 1], im)
            out_ref[a, rows, :MINOR] = re.astype(BF16)
            out_ref[a, rows, MINOR:] = im.astype(BF16)

        dft32(load, store, mid_ref)
        return carry

    lax.fori_loop(0, MINOR // 16, inverse, 0)


def columns(received, first, along_u, along_v, nyquist):
    (fh, fl), (ih, il) = column_tables()
    special = nyquist is not None
    operands = [first, received, along_u, along_v] + [jnp.asarray(t) for t in (fh, fl, ih, il)]
    if special:
        operands.append(nyquist)
    return pl.pallas_call(
        functools.partial(column_kernel, special),
        in_specs=[pl.BlockSpec(memory_space=pltpu.SMEM)] + [whole_spec()] * (len(operands) - 1),
        out_specs=whole_spec(),
        out_shape=jax.ShapeDtypeStruct((MAJOR, MINOR, 2 * MINOR), BF16),
        scratch_shapes=[
            pltpu.VMEM((64, 16, MINOR), F32),
            pltpu.VMEM((MAJOR, 2 * MINOR, 2 * MINOR), BF16),
            pltpu.VMEM((MAJOR, 2 * MINOR, MINOR), F32),
        ],
        compiler_params=pltpu.CompilerParams(vmem_limit_bytes=48 * MIB),
        cost_estimate=pl.CostEstimate(
            flops=32 * 8 * 256 * 256 * 256, bytes_accessed=24 * MIB, transcendentals=0
        ),
        name="columns",
    )(*operands)


def final_kernel(chunks, bands, place_ref, *rest):
    ins, (high_ref, low_ref, out_ref, xs_ref, zs_ref) = rest[:chunks], rest[chunks:]
    place = place_ref[...]
    count = place.shape[0]
    for chunk in range(chunks):

        def arrange(band, carry, chunk=chunk):
            values = ins[chunk][band].reshape(count, 2 * MINOR)
            xs_ref[chunk * bands + band] = dot(place, values).astype(BF16)
            return carry

        lax.fori_loop(0, bands, arrange, 0)

    def tile(t, carry):
        partner = lax.rem(HALF - t, HALF)
        pair = jnp.concatenate([xs_ref[t], xs_ref[partner]], axis=1)
        pair = jnp.concatenate([pair, pair], axis=1)
        zs_ref[t] = dot(pair, jnp.concatenate([high_ref[t], low_ref[t]], axis=0))
        return carry

    lax.fori_loop(0, HALF, tile, 0)

    def group(index, carry):
        rows = pl.ds(pl.multiple_of(index * 8, 8), 8)
        values = [(zs_ref[t, rows, MINOR:], zs_ref[t, rows, :MINOR]) for t in range(HALF)]
        for n, (odd, even) in enumerate(dft16(values)):
            out_ref[rows, MINOR * 2 * n : MINOR * (2 * n + 1)] = even
            out_ref[rows, MINOR * (2 * n + 1) : MINOR * (2 * n + 2)] = odd
        return carry

    lax.fori_loop(0, count // 8, group, 0)


def rows_inverse(received, proj_order, bands):
    chunks = len(received)
    _, projections, rows, width = received[0].shape
    block = min(256 // projections, rows)
    count = block * projections
    high, low = final_tables()
    to = jnp.arange(count, dtype=jnp.int32)
    slot = proj_order[to // block]
    place = (to[:, None] == ((to % block) * projections + slot)[None, :]).astype(BF16)
    result = pl.pallas_call(
        functools.partial(final_kernel, chunks, bands),
        grid=(rows // block,),
        in_specs=[fixed_spec((count, count))]
        + [pl.BlockSpec((bands, projections, block, width), lambda i: (0, 0, i, 0))] * chunks
        + [fixed_spec(high.shape), fixed_spec(low.shape)],
        out_specs=pl.BlockSpec((count, LENGTH), lambda i: (i, 0)),
        out_shape=jax.ShapeDtypeStruct((rows * projections, LENGTH), F32),
        scratch_shapes=[
            pltpu.VMEM((HALF, count, 2 * MINOR), BF16),
            pltpu.VMEM((HALF, count, 2 * MINOR), F32),
        ],
        compiler_params=pltpu.CompilerParams(vmem_limit_bytes=48 * MIB),
        cost_estimate=pl.CostEstimate(
            flops=rows * projections * 16 * 10 * 256 * 256,
            bytes_accessed=rows * projections * LENGTH * 6 + 8 * MIB,
            transcendentals=0,
        ),
        name="rows_inverse",
    )(place, *received, jnp.asarray(high), jnp.asarray(low))
    return result.reshape(rows, projections, LENGTH)


def folded_square(position, length):
    folded = jnp.minimum(position, length - position).astype(F32) / length
    return folded * folded


def nyquist_column(re, im, coefficient):
    side = 64
    index = np.arange(side)
    angle = 2 * math.pi * np.outer(index, index) / side
    cosine, sine = np.cos(angle), np.sin(angle)
    forward = np.stack([np.stack([cosine, -sine], 1), np.stack([sine, cosine], 1)]).astype(np.float32)
    inverse = np.stack([np.stack([cosine, sine], 1), np.stack([-sine, cosine], 1)]).astype(np.float32)
    twist = 2 * math.pi * np.outer(index, index) / LENGTH
    twist_cos, twist_sin = np.cos(twist).astype(np.float32), np.sin(twist).astype(np.float32)
    contract = functools.partial(jnp.einsum, precision=lax.Precision.HIGHEST, preferred_element_type=F32)
    values = jnp.stack([re, im]).reshape(2, side, side)
    values = contract("cab,cadk->dkb", values, forward)
    values = jnp.stack(
        [values[0] * twist_cos + values[1] * twist_sin, values[1] * twist_cos - values[0] * twist_sin]
    )
    values = contract("ckb,cbdm->dkm", values, forward)
    position = (
        lax.broadcasted_iota(jnp.int32, (side, side), 0) + side * lax.broadcasted_iota(jnp.int32, (side, side), 1)
    )
    freq_sq = folded_square(position, LENGTH) + 0.25
    sines = jnp.sin(math.pi * coefficient[:, None, None] * freq_sq)
    scale = 1.0 / (2.0 * (sines[0] * sines[0] + sines[1] * sines[1]) + alpha_reg)
    values = jnp.stack(
        [
            (sines[0] * values[0] + sines[1] * values[1]) * scale,
            (sines[0] * values[1] - sines[1] * values[0]) * scale,
        ]
    )
    values = contract("ckm,cmdb->dkb", values, inverse)
    values = jnp.stack(
        [values[0] * twist_cos - values[1] * twist_sin, values[1] * twist_cos + values[0] * twist_sin]
    )
    column = contract("ckb,cka->ab", values, inverse[:, :, 0, :])
    return column.reshape(MAJOR, MINOR).T


def on_device(intensities, dist_index, fresnel_table, proj_order):
    rows = intensities.shape[2]
    bands = lax.axis_size("band")
    projections = lax.axis_size("proj")
    band = lax.axis_index("band")
    chunks = HALF // bands
    totals = lax.psum(jnp.sum(intensities.astype(F32), axis=(2, 3)), "band")
    scale = (rows * bands * LENGTH) / totals

    spectra = rows_forward(intensities, scale, bands, chunks)

    table_size = fresnel_table.shape[0]
    onehot = (dist_index[0][:, None] == jnp.arange(table_size, dtype=jnp.int32)[None, :]).astype(F32)
    coefficient = jnp.sum(onehot * fresnel_table[None, :], axis=1)
    k_index = lax.broadcasted_iota(jnp.int32, (MAJOR, MINOR), 0)
    s_index = lax.broadcasted_iota(jnp.int32, (MAJOR, MINOR), 1)
    angle_u = math.pi * coefficient[:, None, None] * folded_square(k_index + MAJOR * s_index, LENGTH)
    along_u = jnp.stack([jnp.sin(angle_u[0]), jnp.cos(angle_u[0]), jnp.sin(angle_u[1]), jnp.cos(angle_u[1])], axis=-1)
    tile = jnp.arange(chunks, dtype=jnp.int32)[:, None] * bands + band
    lane = jnp.arange(MINOR, dtype=jnp.int32)[None, :]
    first_tile = jnp.where(lane < MINOR // 2, MAJOR * lane, HALF + MAJOR * (lane - MINOR // 2))
    position_v = jnp.where(tile == 0, first_tile, tile + MAJOR * lane)
    angle_v = math.pi * coefficient[:, None, None] * folded_square(position_v, LENGTH)
    along_v = jnp.stack([jnp.sin(angle_v[0]), jnp.cos(angle_v[0]), jnp.sin(angle_v[1]), jnp.cos(angle_v[1])], axis=1)
    first = (band == 0).astype(jnp.int32).reshape(1)

    received = []
    for chunk in range(chunks):
        pencil = lax.all_to_all(spectra[chunk], "band", split_axis=0, concat_axis=0, tiled=True)
        pencil = pencil.reshape(LENGTH, 4 * MINOR)
        nyquist = None
        if chunk == 0:
            nyquist = nyquist_column(
                pencil[:, 2 * MINOR].astype(F32), pencil[:, 3 * MINOR].astype(F32), coefficient
            )
        phase = columns(
            pencil.reshape(MAJOR, MINOR, 4 * MINOR), first, along_u, along_v[chunk], nyquist
        )
        rows_to = LENGTH // (bands * projections)
        phase = phase.reshape(bands * projections, rows_to, 2 * MINOR)
        back = lax.all_to_all(phase, ("band", "proj"), split_axis=0, concat_axis=0, tiled=True)
        received.append(back.reshape(bands, projections, rows_to, 2 * MINOR))

    return rows_inverse(received, proj_order, bands)


def solution(mesh):
    in_specs = (P("proj", None, "band", None), P("proj", None), P(), P())
    out_specs = P(("band", "proj"), None, None)
    return jax.shard_map(
        on_device, mesh=mesh, in_specs=in_specs, out_specs=out_specs, check_vma=False
    )
```

time: 1620 us -> 535 us (0.33)
  matrix products: 370 us -> 1.04 us
  other arithmetic: 349 us -> 16.8 us
  local copies, waits for them, and re-layouts: 262 us -> 9.41 us
  blocking collectives: 377 us -> 164 us
  Pallas kernels: 0 us -> 207 us
  waiting for transfers between devices: 234 us -> 116 us
    dot_general x9 -> x4, matrix products: 370 us -> 1.04 us  [the longest x1 0.32 us: nyquist_column(): values = contract('ckb,cbdm->dkm', values, forward)]
    all_to_all x1 -> x3, blocking collectives: 369 us -> 155 us  [on_device(): lax.all_to_all(spectra[chunk], 'band', split_axis=0, concat_axis=0, tiled...]
    pallas_call x0 -> x6, Pallas kernels: none -> 207 us  [the longest x4 116 us: columns(): pl.pallas_call(functools.partial(column_kernel, special), in_specs=[pl.Bl...]
    reduce_sum x3 -> x2, other arithmetic: 133 us -> 11.1 us  [the longest x1 10.9 us: on_device(): totals = lax.psum(jnp.sum(intensities.astype(F32), axis=(2, 3)), 'band')]
    all_to_all x2 -> x5, waiting for transfers between devices: 234 us -> 116 us  [the longest x4 99.5 us: on_device(): lax.all_to_all(phase, ('band', 'proj'), split_axis=0, concat_axis=0, tile...]
    convert_element_type x3 -> x2, local copies, waits for them, and re-layouts: 94.5 us -> 0.16 us  [the longest x1 0.08 us: on_device(): pencil[:, 2 * MINOR].astype(F32)]
    sub x5 -> x1, other arithmetic: 90.1 us -> 0.01 us  [nyquist_column(): values[0] * twist_cos - values[1] * twist_sin]
    another operation x7 -> x2, other arithmetic: 76.5 us -> 0.02 us  [the longest x1 0.02 us: on_device(): jnp.stack([jnp.sin(angle_v[0]), jnp.cos(angle_v[0]), jnp.sin(angle_v[1]),...]
  transfers between devices with their start and end apart: 2 -> 5, of which waited for: 2 -> 5; matrix products, arithmetic and copies ran while one was open for 8% -> 2% of each run, Pallas kernels for 0% -> 22%
where the time goes in v1:
time: 535 us
  Pallas kernels  207 us (39%)
  blocking collectives  164 us (31%)
  waiting for transfers between devices  116 us (22%)
  starting transfers between devices  19.7 us (4%)
  other arithmetic  16.8 us (3%)
  local copies, waits for them, and re-layouts  9.41 us (2%)
    all_to_all x3, blocking collectives, on_device(): lax.all_to_all(spectra[chunk], 'band', split_axis=0, concat_axis=0, tiled...  155 us
    pallas_call x4, Pallas kernels, columns(): pl.pallas_call(functools.partial(column_kernel, special), in_specs=[pl.Bl...  116 us
    all_to_all x4, waiting for transfers between devices, on_device(): lax.all_to_all(phase, ('band', 'proj'), split_axis=0, concat_axis=0, tile...  99.5 us
    pallas_call x1, Pallas kernels, rows_forward(): pl.pallas_call(functools.partial(row_kernel, chunks, bands), grid=(rows /...  49.5 us
    pallas_call x1, Pallas kernels, rows_inverse(): pl.pallas_call(functools.partial(final_kernel, chunks, bands), grid=(rows...  42.3 us
    all_to_all x1, waiting for transfers between devices, on_device(): lax.all_to_all(spectra[chunk], 'band', split_axis=0, concat_axis=0, tiled...  16.8 us
    all_to_all x4, starting transfers between devices, on_device(): lax.all_to_all(phase, ('band', 'proj'), split_axis=0, concat_axis=0, tile...  14.7 us
    reduce_sum x1, other arithmetic, on_device(): totals = lax.psum(jnp.sum(intensities.astype(F32), axis=(2, 3)), 'band')  10.9 us
  transfers between devices with their start and end apart: 5, of which 5 were waited for; matrix products, arithmetic and copies ran while one was open for 2% of the time, Pallas kernels for 22%

profile of v1, /device:TPU:0, one launch (start us, length us, event | category | flops | bytes accessed | tf_op | source)
XLA Modules:
  0.0 534.6 jit_solution(4380455750044479480)
XLA Ops:
  0.0 10.9 %convert_reduce_fusion = f32[2]{0:T(128)S(1)} fusion(bf16[1,2,1024,4096]{3,2,1,0:T(8,128)(2,1)} %x_ref.1), kind=kLoop, calls=%fused_computation | loop fusion | flops 16777214 | bytes 16777224 | tf_op jit(solution)/shard_map/reduce_sum | solution.py:451
  10.9 8.3 %psum.7 = f32[1,2]{1,0:T(1,128)S(1)} all-reduce(f32[1,2]{1,0:T(1,128)S(1)} %bitcast.88), channel_id=1, replica_groups=mesh['proj'=8,'band'=4] {'band'}, use_global_device_ids=true, to_apply=%region_1.0 | all-reduce | flops 2 | bytes 16 | tf_op jit(solution)/shard_map/psum | solution.py:451
  19.2 49.5 %rows_forward.1 = (bf16[4,1024,512]{2,1,0:T(8,128)(2,1)S(1)}, bf16[4,1024,512]{2,1,0:T(8,128)(2,1)}, bf16[4,1024,512]{2,1,0:T(8,128)(2,1)}, bf16[4,1024,512]{2,1,0:T(8,128)(2,1)}) custom-call(f32[1,2]{1,0:T(1,128)S(1)} %broadcast_divide_fusion.scale_ref, bf16[1,2,1024,4096]{3,2,1,0:T(8,128)(2,1)} %x_ref.1, bf16[34,256,256]{2,1,0:T(8,128)(2,1)} %constant.103.clone.high_ref, ...), custom_call_target="tpu_custom_call" | custom-call | flops 13690208256 | bytes 42991616 | tf_op jit(solution)/shard_map/rows_forward/pallas_call | solution.py:216
  68.7 51.8 %all_to_all.40 = bf16[4,1024,512]{2,1,0:T(8,128)(2,1)} all-to-all(bf16[4,1024,512]{2,1,0:T(8,128)(2,1)S(1)} %get-tuple-element.9), channel_id=1, replica_groups=mesh['proj'=8,'band'=4] {'band'}, dimensions={0} | all-to-all | bytes 8388608 | tf_op jit(solution)/shard_map/all_to_all | solution.py:473
  120.5 51.8 %all_to_all.41 = bf16[4,1024,512]{2,1,0:T(8,128)(2,1)} all-to-all(bf16[4,1024,512]{2,1,0:T(8,128)(2,1)S(1)} %copy-done.5), channel_id=1, replica_groups=mesh['proj'=8,'band'=4] {'band'}, dimensions={0} | all-to-all | bytes 8388608 | tf_op jit(solution)/shard_map/all_to_all | solution.py:473
  172.4 51.6 %all_to_all.42 = bf16[4,1024,512]{2,1,0:T(8,128)(2,1)} all-to-all(bf16[4,1024,512]{2,1,0:T(8,128)(2,1)S(1)} %copy-done.4), channel_id=1, replica_groups=mesh['proj'=8,'band'=4] {'band'}, dimensions={0} | all-to-all | bytes 8388608 | tf_op jit(solution)/shard_map/all_to_all | solution.py:473
  224.0 5.0 all-to-all-start.6
  229.1 0.2 fusion.23
  229.3 0.1 broadcast_multiply_fusion
  229.3 0.1 sine_bitcast_fusion.1
  229.5 0.6 copy.85.u_ref
  230.2 0.1 fusion.20
  230.2 0.1 broadcast_multiply_fusion.1
  230.3 0.1 slice_sine_fusion.1
  230.4 28.7 %columns.5 = bf16[32,128,256]{2,1,0:T(8,128)(2,1)S(1)} custom-call(s32[1]{0:T(128)} %bitcast.9.first_ref, bf16[32,128,512]{2,1,0:T(8,128)(2,1)} %bitcast.82, f32[32,128,4]{2,1,0:T(8,128)S(1)} %copy.85.u_ref, f32[4,128]{1,0:T(4,128)S(1)} %get-tuple-element.27.v_ref, bf16[32,256,256]{2,1,0:T(8,128)(2,1)} %constant.110.clone.fh_ref, ...), custom_call_target="tpu_custom_call" | custom-call | flops 4294967296 | bytes 25165824 | tf_op jit(solution)/shard_map/columns/pallas_call | solution.py:321
  259.1 0.0 copy-start.2
  259.1 1.3 copy-done.2
  260.5 16.8 %all-to-all-done.6 = bf16[4,1024,512]{2,1,0:T(8,128)(2,1)} async-done(((bf16[4,1024,512]{2,1,0:T(8,128)(2,1)}), bf16[4,1024,512]{2,1,0:T(8,128)(2,1)}, u32[]{:S(2)}, u32[]{:S(2)}) %all-to-all-start.6) | async-done | bytes 4194336 | tf_op jit(solution)/shard_map/all_to_all | solution.py:473
  277.3 5.1 all-to-all-start.3
  282.3 28.7 %columns.6 = bf16[32,128,256]{2,1,0:T(8,128)(2,1)S(1)} custom-call(s32[1]{0:T(128)} %bitcast.9.first_ref, bf16[32,128,512]{2,1,0:T(8,128)(2,1)} %bitcast.81, f32[32,128,4]{2,1,0:T(8,128)S(1)} %copy.85.u_ref, f32[4,128]{1,0:T(4,128)S(1)} %get-tuple-element.26.v_ref, bf16[32,256,256]{2,1,0:T(8,128)(2,1)} %constant.110.clone.fh_ref, ...), custom_call_target="tpu_custom_call" | custom-call | flops 4294967296 | bytes 25165824 | tf_op jit(solution)/shard_map/columns/pallas_call | solution.py:321
  311.0 1.3 copy-done.3
  312.4 20.0 %all-to-all-done.3 = bf16[32,128,256]{2,1,0:T(8,128)(2,1)} async-done(((bf16[32,128,256]{2,1,0:T(8,128)(2,1)}), bf16[32,128,256]{2,1,0:T(8,128)(2,1)}, u32[]{:S(2)}, u32[]{:S(2)}) %all-to-all-start.3) | async-done | bytes 2097184 | tf_op jit(solution)/shard_map/all_to_all | solution.py:485
  332.4 3.5 all-to-all-start.5
  335.9 28.7 %columns.7 = bf16[32,128,256]{2,1,0:T(8,128)(2,1)S(1)} custom-call(s32[1]{0:T(128)} %bitcast.9.first_ref, bf16[32,128,512]{2,1,0:T(8,128)(2,1)} %bitcast.48.x_ref, f32[32,128,4]{2,1,0:T(8,128)S(1)} %copy.85.u_ref, f32[4,128]{1,0:T(4,128)S(1)} %get-tuple-element.25.v_ref, bf16[32,256,256]{2,1,0:T(8,128)(2,1)} %constant.110.clone.fh_ref, ...), custom_call_target="tpu_custom_call" | custom-call | flops 4294967296 | bytes 25165824 | tf_op jit(solution)/shard_map/columns/pallas_call | solution.py:321
  364.6 1.3 copy-done
  366.0 0.0 copy-start.10
  366.0 20.0 %all-to-all-done.5 = bf16[32,128,256]{2,1,0:T(8,128)(2,1)} async-done(((bf16[32,128,256]{2,1,0:T(8,128)(2,1)}), bf16[32,128,256]{2,1,0:T(8,128)(2,1)}, u32[]{:S(2)}, u32[]{:S(2)}) %all-to-all-start.5) | async-done | bytes 2097184 | tf_op jit(solution)/shard_map/all_to_all | solution.py:485
  385.9 3.5 all-to-all-start.7
  389.4 0.3 multiply_sine_fusion
  389.7 2.2 slice_reduce_fusion.1
  391.9 0.1 convert_element_type.58
  392.0 0.1 convert_element_type.59
  392.1 0.2 convolution_bitcast_fusion.2
  392.4 0.3 convolution_bitcast_fusion.1
  392.8 0.3 convolution_bitcast_fusion
  393.1 0.2 convolution_bitcast_fusion.3
  393.3 0.1 reshape.343
  393.4 0.1 copy.84
  393.5 29.4 %columns.4 = bf16[32,128,256]{2,1,0:T(8,128)(2,1)S(1)} custom-call(s32[1]{0:T(128)} %bitcast.9.first_ref, bf16[32,128,512]{2,1,0:T(8,128)(2,1)} %bitcast.80, f32[32,128,4]{2,1,0:T(8,128)S(1)} %copy.85.u_ref, f32[4,128]{1,0:T(4,128)S(1)} %get-tuple-element.28.v_ref, bf16[32,256,256]{2,1,0:T(8,128)(2,1)} %constant.110.clone.fh_ref, ...), custom_call_target="tpu_custom_call" | custom-call | flops 4294967296 | bytes 25165824 | tf_op jit(solution)/shard_map/columns/pallas_call | solution.py:321
  422.9 0.0 copy-start.1
  422.9 1.3 copy-done.1
  424.2 15.2 %all-to-all-done.7 = bf16[32,128,256]{2,1,0:T(8,128)(2,1)} async-done(((bf16[32,128,256]{2,1,0:T(8,128)(2,1)}), bf16[32,128,256]{2,1,0:T(8,128)(2,1)}, u32[]{:S(2)}, u32[]{:S(2)}) %all-to-all-start.7) | async-done | bytes 2097184 | tf_op jit(solution)/shard_map/all_to_all | solution.py:485
  439.5 2.7 all-to-all-start.1
  442.3 0.7 fusion.30
  442.9 4.4 compare_select_fusion.1
  447.4 0.6 fusion.22
  448.0 44.3 %all-to-all-done.1 = bf16[32,128,256]{2,1,0:T(8,128)(2,1)S(1)} async-done(((bf16[32,128,256]{2,1,0:T(8,128)(2,1)}), bf16[32,128,256]{2,1,0:T(8,128)(2,1)S(1)}, u32[]{:S(2)}, u32[]{:S(2)}) %all-to-all-start.1) | async-done | bytes 2097184 | tf_op jit(solution)/shard_map/all_to_all | solution.py:485
  492.3 42.3 %rows_inverse.1 = f32[1024,4096]{1,0:T(8,128)} custom-call(bf16[256,256]{1,0:T(8,128)(2,1)S(1)} %fusion.place_ref, bf16[4,8,128,256]{3,2,1,0:T(8,128)(2,1)S(1)} %bitcast.77, bf16[4,8,128,256]{3,2,1,0:T(8,128)(2,1)} %bitcast.44.rest_1_, bf16[4,8,128,256]{3,2,1,0:T(8,128)(2,1)} %bitcast.47.rest_2_, bf16[4,8,128,256]{3,2,1,0:T(8,128)(2,1)} %bitcast.50.rest_3_, ...), custom_call_target="tpu_custom_call" | custom-call | flops 10737418240 | bytes 33554432 | tf_op jit(solution)/shard_map/rows_inverse/pallas_call | solution.py:381
  (37 shorter events, 0.2 us)
Async XLA Ops:
  68.7 51.8 %copy-start.5 = (bf16[4,1024,512]{2,1,0:T(8,128)(2,1)S(1)}, bf16[4,1024,512]{2,1,0:T(8,128)(2,1)}, u32[]{:S(2)}) copy-start(bf16[4,1024,512]{2,1,0:T(8,128)(2,1)} %get-tuple-element.10) | copy-start | bytes 12582916
  120.5 51.8 %copy-start.4 = (bf16[4,1024,512]{2,1,0:T(8,128)(2,1)S(1)}, bf16[4,1024,512]{2,1,0:T(8,128)(2,1)}, u32[]{:S(2)}) copy-start(bf16[4,1024,512]{2,1,0:T(8,128)(2,1)} %get-tuple-element.11) | copy-start | bytes 12582916
  224.0 5.0 copy-start.12
  224.0 5.0 copy-start.13
  224.0 53.2 %all-to-all-start.6 = ((bf16[4,1024,512]{2,1,0:T(8,128)(2,1)}), bf16[4,1024,512]{2,1,0:T(8,128)(2,1)}, u32[]{:S(2)}, u32[]{:S(2)}) async-start(bf16[4,1024,512]{2,1,0:T(8,128)(2,1)} %get-tuple-element.12), calls=%async_computation.6 | async-start | bytes 8388608 | tf_op jit(solution)/shard_map/all_to_all | solution.py:473
  259.1 1.3 copy-start.2
  277.3 55.1 %all-to-all-start.3 = ((bf16[32,128,256]{2,1,0:T(8,128)(2,1)}), bf16[32,128,256]{2,1,0:T(8,128)(2,1)}, u32[]{:S(2)}, u32[]{:S(2)}) async-start(bf16[32,128,256]{2,1,0:T(8,128)(2,1)} %copy-done.2), calls=%async_computation.3 | async-start | bytes 4194304 | tf_op jit(solution)/shard_map/all_to_all | solution.py:485
  311.0 1.4 copy-start.3
  332.4 53.5 %all-to-all-start.5 = ((bf16[32,128,256]{2,1,0:T(8,128)(2,1)}), bf16[32,128,256]{2,1,0:T(8,128)(2,1)}, u32[]{:S(2)}, u32[]{:S(2)}) async-start(bf16[32,128,256]{2,1,0:T(8,128)(2,1)} %copy-done.3), calls=%async_computation.5 | async-start | bytes 4194304 | tf_op jit(solution)/shard_map/all_to_all | solution.py:485
  364.6 1.4 copy-start
  365.9 26.2 %copy-start.6 = (f32[2,64,2,64]{1,3,0,2:T(8,128)S(1)}, f32[2,64,2,64]{1,3,0,2:T(8,128)}, u32[]{:S(2)}) copy-start(f32[2,64,2,64]{1,3,0,2:T(8,128)} %constant.105.clone) | copy-start | bytes 196612
  365.9 26.4 %copy-start.8 = (f32[1,64,64]{2,1,0:T(8,128)S(1)}, f32[1,64,64]{2,1,0:T(8,128)}, u32[]{:S(2)}) copy-start(f32[1,64,64]{2,1,0:T(8,128)} %constant.119) | copy-start | bytes 49156
  365.9 26.4 %copy-start.9 = (f32[1,64,64]{2,1,0:T(8,128)S(1)}, f32[1,64,64]{2,1,0:T(8,128)}, u32[]{:S(2)}) copy-start(f32[1,64,64]{2,1,0:T(8,128)} %constant.118) | copy-start | bytes 49156
  365.9 26.8 %copy-start.7 = (f32[2,64,2,64]{3,1,0,2:T(8,128)S(1)}, f32[2,64,2,64]{3,1,0,2:T(8,128)}, u32[]{:S(2)}) copy-start(f32[2,64,2,64]{3,1,0,2:T(8,128)} %constant.108.clone) | copy-start | bytes 196612
  366.0 27.1 %copy-start.10 = (f32[2,64,64]{1,2,0:T(8,128)S(1)}, f32[2,64,64]{1,2,0:T(8,128)}, u32[]{:S(2)}) copy-start(f32[2,64,64]{1,2,0:T(8,128)} %constant.109.clone) | copy-start | bytes 98308
  385.9 53.6 %all-to-all-start.7 = ((bf16[32,128,256]{2,1,0:T(8,128)(2,1)}), bf16[32,128,256]{2,1,0:T(8,128)(2,1)}, u32[]{:S(2)}, u32[]{:S(2)}) async-start(bf16[32,128,256]{2,1,0:T(8,128)(2,1)} %copy-done), calls=%async_computation.7 | async-start | bytes 4194304 | tf_op jit(solution)/shard_map/all_to_all | solution.py:485
  422.9 1.3 copy-start.1
  424.2 18.0 %copy-start.11 = (s32[8]{0:T(128)S(1)}, s32[8]{0:T(128)}, u32[]{:S(2)}) copy-start(s32[8]{0:T(128)} %param.21) | copy-start | bytes 100
  439.5 52.8 %all-to-all-start.1 = ((bf16[32,128,256]{2,1,0:T(8,128)(2,1)}), bf16[32,128,256]{2,1,0:T(8,128)(2,1)S(1)}, u32[]{:S(2)}, u32[]{:S(2)}) async-start(bf16[32,128,256]{2,1,0:T(8,128)(2,1)} %copy-done.1), calls=%async_computation.1 | async-start | bytes 4194304 | tf_op jit(solution)/shard_map/all_to_all | solution.py:485

commit v2 on v1

--- a/solution.py
+++ b/solution.py
@@ -154,10 +154,23 @@
     return jnp.dot(x, y, preferred_element_type=F32)
 
 
-def row_kernel(chunks, bands, scale_ref, x_ref, high_ref, low_ref, *rest):
-    outs, (mid_ref, xs_ref) = rest[:chunks], rest[chunks:]
+def row_kernel(chunks, bands, band_ref, scale_ref, x_ref, high_hbm, low_hbm, *rest):
+    outs = rest[: chunks * bands]
+    mid_ref, xs_ref, high_ref, low_ref, sems = rest[chunks * bands :]
     rows_here = x_ref.shape[2]
+    band = band_ref[0]
     scale_even, scale_odd = scale_ref[0, 0], scale_ref[0, 1]
+
+    def fetches():
+        return [
+            pltpu.make_async_copy(high_hbm, high_ref, sems.at[0]),
+            pltpu.make_async_copy(low_hbm, low_ref, sems.at[1]),
+        ]
+
+    @pl.when(pl.program_id(0) == 0)
+    def _():
+        for fetch in fetches():
+            fetch.start()
 
     def group(index, carry):
         rows = pl.ds(pl.multiple_of(index * 16, 16), 16)
@@ -180,6 +193,11 @@
 
     lax.fori_loop(0, rows_here // 16, group, 0)
 
+    @pl.when(pl.program_id(0) == 0)
+    def _():
+        for fetch in fetches():
+            fetch.wait()
+
     def apply(k, table):
         values = xs_ref[k]
         high = high_ref[table]
@@ -187,62 +205,97 @@
         return dot(whole, jnp.concatenate([high, high, low_ref[table]], axis=0))
 
     width = 2 * MINOR
-    outs[0][0, :, :width] = (apply(0, 0) + apply(HALF, 32)).astype(BF16)
-    outs[0][0, :, width:] = (apply(0, 1) + apply(HALF, 33)).astype(BF16)
     for chunk in range(chunks):
-
-        def tile(band, carry, chunk=chunk):
-            t = chunk * bands + band
-            outs[chunk][band, :, :width] = apply(t, 2 * t).astype(BF16)
-            outs[chunk][band, :, width:] = apply(MAJOR - t, 2 * t + 1).astype(BF16)
-            return carry
-
-        lax.fori_loop(1 if chunk == 0 else 0, bands, tile, 0)
+        for offset in range(bands):
+            t = chunk * bands + (band ^ offset)
+            out_ref = outs[chunk * bands + offset]
+            out_ref[:, :width] = apply(t, 2 * t).astype(BF16)
+            out_ref[:, width:] = apply(lax.rem(MAJOR - t, MAJOR), 2 * t + 1).astype(BF16)
+    for offset in range(bands):
+
+        @pl.when(band == offset)
+        def _(offset=offset):
+            outs[offset][:, :width] = (apply(0, 0) + apply(HALF, 32)).astype(BF16)
+            outs[offset][:, width:] = (apply(0, 1) + apply(HALF, 33)).astype(BF16)
 
 
 def whole_spec():
     return pl.BlockSpec(memory_space=pltpu.VMEM)
 
 
+def any_spec():
+    return pl.BlockSpec(memory_space=pl.ANY)
+
+
 def fixed_spec(shape):
     return pl.BlockSpec(shape, lambda *_: (0,) * len(shape), pipeline_mode=pl.Buffered(1))
 
 
-def rows_forward(intensities, scale, bands, chunks):
-    rows = intensities.shape[2]
+def rows_forward(intensities, scale, band, bands, chunks, part, parts):
+    rows = intensities.shape[2] // parts
     block = min(256, rows)
+    blocks = rows // block
     high, low = row_tables()
     width = 4 * MINOR
-    return pl.pallas_call(
+    count = chunks * bands
+    outs = pl.pallas_call(
         functools.partial(row_kernel, chunks, bands),
-        grid=(rows // block,),
+        grid=(blocks,),
         in_specs=[
             pl.BlockSpec(memory_space=pltpu.SMEM),
-            pl.BlockSpec((1, 2, block, LENGTH), lambda i: (0, 0, i, 0)),
-            fixed_spec(high.shape),
-            fixed_spec(low.shape),
+            pl.BlockSpec(memory_space=pltpu.SMEM),
+            pl.BlockSpec((1, 2, block, LENGTH), lambda i: (0, 0, i + part * blocks, 0)),
+            any_spec(),
+            any_spec(),
         ],
-        out_specs=[pl.BlockSpec((bands, block, width), lambda i: (0, i, 0))] * chunks,
-        out_shape=[jax.ShapeDtypeStruct((bands, rows, width), BF16)] * chunks,
+        out_specs=[pl.BlockSpec((block, width), lambda i: (i, 0))] * count,
+        out_shape=[jax.ShapeDtypeStruct((rows, width), BF16)] * count,
         scratch_shapes=[
             pltpu.VMEM((64, 16, MINOR), F32),
             pltpu.VMEM((MAJOR, block, 4 * MINOR), BF16),
+            pltpu.VMEM(high.shape, BF16),
+            pltpu.VMEM(low.shape, BF16),
+            pltpu.SemaphoreType.DMA((2,)),
         ],
         compiler_params=pltpu.CompilerParams(vmem_limit_bytes=48 * MIB),
         cost_estimate=pl.CostEstimate(
             flops=rows * 34 * 6 * 256 * 256, bytes_accessed=4 * rows * LENGTH * 2 + 9 * MIB, transcendentals=0
         ),
         name="rows_forward",
-    )(scale, intensities, jnp.asarray(high), jnp.asarray(low))
-
-
-def column_kernel(special, first_ref, x_ref, u_ref, v_ref, fh_ref, fl_ref, ih_ref, il_ref, *rest):
+    )(band, scale, intensities, jnp.asarray(high), jnp.asarray(low))
+    return [outs[bands * chunk : bands * (chunk + 1)] for chunk in range(chunks)]
+
+
+def column_kernel(special, bands, parts, band_ref, v_ref, *rest):
+    blocks = rest[: bands * parts]
+    u_hbm, *table_hbms = rest[bands * parts : bands * parts + 5]
+    rest = rest[bands * parts + 5 :]
+    band = band_ref[0]
     if special:
-        nyquist_ref, out_ref, mid_ref, xs_ref, ys_ref = rest
+        nyquist_ref, out_ref, mid_ref, xs_ref, ys_ref, x_ref, u_ref, fh_ref, fl_ref, ih_ref, il_ref, sems = rest
         lane = lax.broadcasted_iota(jnp.int32, (16, MINOR), 1)
-        own = (lane == 0) & (first_ref[0] == 1)
+        own = (lane == 0) & (band == 0)
     else:
-        out_ref, mid_ref, xs_ref, ys_ref = rest
+        out_ref, mid_ref, xs_ref, ys_ref, x_ref, u_ref, fh_ref, fl_ref, ih_ref, il_ref, sems = rest
+
+    fetches = []
+    height = MAJOR // (bands * parts)
+    for offset in range(bands):
+        for part in range(parts):
+            index = offset * parts + part
+            start = (band ^ offset) * (height * parts) + part * height
+            fetches.append(
+                pltpu.make_async_copy(blocks[index], x_ref.at[pl.ds(start, height)], sems.at[index])
+            )
+    late = []
+    for index, (source, target) in enumerate(
+        zip([u_hbm] + table_hbms, (u_ref, fh_ref, fl_ref, ih_ref, il_ref))
+    ):
+        late.append(pltpu.make_async_copy(source, target, sems.at[bands * parts + index]))
+    for fetch in fetches + late:
+        fetch.start()
+    for fetch in fetches:
+        fetch.wait()
 
     def forward(index, carry):
         start = pl.multiple_of(index * 16, 16)
@@ -270,10 +323,12 @@
         return carry
 
     lax.fori_loop(0, MINOR // 16, forward, 0)
+    for fetch in late:
+        fetch.wait()
 
     sin_even_v, cos_even_v, sin_odd_v, cos_odd_v = [v_ref[i : i + 1, :] for i in range(4)]
 
-    def middle(k, carry):
+    def middle(k):
         values = xs_ref[k]
         table = jnp.concatenate([fh_ref[k], fl_ref[k]], axis=1)
         spectra = dot(table, jnp.concatenate([values, values], axis=0))
@@ -288,9 +343,13 @@
         phase = jnp.concatenate([phase_re.astype(BF16), phase_im.astype(BF16)], axis=0)
         table = jnp.concatenate([ih_ref[k], il_ref[k]], axis=1)
         ys_ref[k] = dot(table, jnp.concatenate([phase, phase], axis=0))
+
+    def middles(index, carry):
+        for step in range(4):
+            middle(4 * index + step)
         return carry
 
-    lax.fori_loop(0, MAJOR, middle, 0)
+    lax.fori_loop(0, MAJOR // 4, middles, 0)
 
     def inverse(index, carry):
         start = pl.multiple_of(index * 16, 16)
@@ -312,22 +371,29 @@
     lax.fori_loop(0, MINOR // 16, inverse, 0)
 
 
-def columns(received, first, along_u, along_v, nyquist):
+def columns(blocks, band, along_u, along_v, nyquist, bands, parts):
     (fh, fl), (ih, il) = column_tables()
     special = nyquist is not None
-    operands = [first, received, along_u, along_v] + [jnp.asarray(t) for t in (fh, fl, ih, il)]
+    count = bands * parts
+    operands = [band, along_v, *blocks, along_u] + [jnp.asarray(t) for t in (fh, fl, ih, il)]
+    in_specs = [pl.BlockSpec(memory_space=pltpu.SMEM), whole_spec()] + [any_spec()] * (count + 5)
     if special:
         operands.append(nyquist)
+        in_specs.append(whole_spec())
     return pl.pallas_call(
-        functools.partial(column_kernel, special),
-        in_specs=[pl.BlockSpec(memory_space=pltpu.SMEM)] + [whole_spec()] * (len(operands) - 1),
+        functools.partial(column_kernel, special, bands, parts),
+        in_specs=in_specs,
         out_specs=whole_spec(),
         out_shape=jax.ShapeDtypeStruct((MAJOR, MINOR, 2 * MINOR), BF16),
         scratch_shapes=[
             pltpu.VMEM((64, 16, MINOR), F32),
             pltpu.VMEM((MAJOR, 2 * MINOR, 2 * MINOR), BF16),
             pltpu.VMEM((MAJOR, 2 * MINOR, MINOR), F32),
-        ],
+            pltpu.VMEM((MAJOR, MINOR, 4 * MINOR), BF16),
+            pltpu.VMEM(along_u.shape, F32),
+        ]
+        + [pltpu.VMEM(fh.shape, BF16)] * 4
+        + [pltpu.SemaphoreType.DMA((count + 5,))],
         compiler_params=pltpu.CompilerParams(vmem_limit_bytes=48 * MIB),
         cost_estimate=pl.CostEstimate(
             flops=32 * 8 * 256 * 256 * 256, bytes_accessed=24 * MIB, transcendentals=0
@@ -341,32 +407,26 @@
     place = place_ref[...]
     count = place.shape[0]
     for chunk in range(chunks):
-
-        def arrange(band, carry, chunk=chunk):
+        for band in range(bands):
             values = ins[chunk][band].reshape(count, 2 * MINOR)
             xs_ref[chunk * bands + band] = dot(place, values).astype(BF16)
-            return carry
-
-        lax.fori_loop(0, bands, arrange, 0)
-
-    def tile(t, carry):
-        partner = lax.rem(HALF - t, HALF)
+
+    for t in range(HALF):
+        partner = (HALF - t) % HALF
         pair = jnp.concatenate([xs_ref[t], xs_ref[partner]], axis=1)
         pair = jnp.concatenate([pair, pair], axis=1)
         zs_ref[t] = dot(pair, jnp.concatenate([high_ref[t], low_ref[t]], axis=0))
+
+    def group(index, carry):
+        for half in range(2):
+            rows = pl.ds(pl.multiple_of(index * 16 + 8 * half, 8), 8)
+            values = [(zs_ref[t, rows, MINOR:], zs_ref[t, rows, :MINOR]) for t in range(HALF)]
+            for n, (odd, even) in enumerate(dft16(values)):
+                out_ref[rows, MINOR * 2 * n : MINOR * (2 * n + 1)] = even
+                out_ref[rows, MINOR * (2 * n + 1) : MINOR * (2 * n + 2)] = odd
         return carry
 
-    lax.fori_loop(0, HALF, tile, 0)
-
-    def group(index, carry):
-        rows = pl.ds(pl.multiple_of(index * 8, 8), 8)
-        values = [(zs_ref[t, rows, MINOR:], zs_ref[t, rows, :MINOR]) for t in range(HALF)]
-        for n, (odd, even) in enumerate(dft16(values)):
-            out_ref[rows, MINOR * 2 * n : MINOR * (2 * n + 1)] = even
-            out_ref[rows, MINOR * (2 * n + 1) : MINOR * (2 * n + 2)] = odd
-        return carry
-
-    lax.fori_loop(0, count // 8, group, 0)
+    lax.fori_loop(0, count // 16, group, 0)
 
 
 def rows_inverse(received, proj_order, bands):
@@ -451,7 +511,9 @@
     totals = lax.psum(jnp.sum(intensities.astype(F32), axis=(2, 3)), "band")
     scale = (rows * bands * LENGTH) / totals
 
-    spectra = rows_forward(intensities, scale, bands, chunks)
+    here = jnp.asarray(band, jnp.int32).reshape(1)
+    parts = 2
+    spectra = [rows_forward(intensities, scale, here, bands, chunks, part, parts) for part in range(parts)]
 
     table_size = fresnel_table.shape[0]
     onehot = (dist_index[0][:, None] == jnp.arange(table_size, dtype=jnp.int32)[None, :]).astype(F32)
@@ -466,20 +528,24 @@
     position_v = jnp.where(tile == 0, first_tile, tile + MAJOR * lane)
     angle_v = math.pi * coefficient[:, None, None] * folded_square(position_v, LENGTH)
     along_v = jnp.stack([jnp.sin(angle_v[0]), jnp.cos(angle_v[0]), jnp.sin(angle_v[1]), jnp.cos(angle_v[1])], axis=1)
-    first = (band == 0).astype(jnp.int32).reshape(1)
 
     received = []
     for chunk in range(chunks):
-        pencil = lax.all_to_all(spectra[chunk], "band", split_axis=0, concat_axis=0, tiled=True)
-        pencil = pencil.reshape(LENGTH, 4 * MINOR)
+        blocks = []
+        for offset in range(bands):
+            pairs = [(source, source ^ offset) for source in range(bands)]
+            for part in range(parts):
+                block = spectra[part][chunk][offset]
+                if offset:
+                    block = lax.ppermute(block, "band", pairs)
+                blocks.append(block)
         nyquist = None
         if chunk == 0:
-            nyquist = nyquist_column(
-                pencil[:, 2 * MINOR].astype(F32), pencil[:, 3 * MINOR].astype(F32), coefficient
-            )
-        phase = columns(
-            pencil.reshape(MAJOR, MINOR, 4 * MINOR), first, along_u, along_v[chunk], nyquist
-        )
+            sent = jnp.stack([block[:, 2 * MINOR :: MINOR] for block in blocks]).astype(F32)
+            sent = sent.reshape(bands, rows, 2)[jnp.arange(bands, dtype=jnp.int32) ^ band]
+            nyquist = nyquist_column(sent[:, :, 0], sent[:, :, 1], coefficient)
+        blocks = [block.reshape(-1, MINOR, 4 * MINOR) for block in blocks]
+        phase = columns(blocks, here, along_u, along_v[chunk], nyquist, bands, parts)
         rows_to = LENGTH // (bands * projections)
         phase = phase.reshape(bands * projections, rows_to, 2 * MINOR)
         back = lax.all_to_all(phase, ("band", "proj"), split_axis=0, concat_axis=0, tiled=True)

time: 535 us -> 489 us (0.914)
  blocking collectives: 164 us -> 8.31 us
  waiting for transfers between devices: 116 us -> 252 us
  Pallas kernels: 207 us -> 139 us
  starting transfers between devices: 19.7 us -> 39.7 us
  local copies, waits for them, and re-layouts: 9.41 us -> 27 us
    ppermute x0 -> x24, waiting for transfers between devices: none -> 208 us  [on_device(): block = lax.ppermute(block, 'band', pairs)]
    all_to_all x3 -> x0, blocking collectives: 155 us -> none  [on_device(): lax.all_to_all(spectra[chunk], 'band', split_axis=0, concat_axis=0, tiled...]
    all_to_all x4, waiting for transfers between devices: 99.5 us -> 44.1 us  [on_device(): lax.all_to_all(phase, ('band', 'proj'), split_axis=0, concat_axis=0, tile...]
    pallas_call x5 -> x6, Pallas kernels: 165 us -> 117 us  [the longest x4 76.3 us: columns(): pl.pallas_call(functools.partial(column_kernel, special, bands, parts), i...]
    pallas_call x1, Pallas kernels: 42.3 us -> 21.4 us  [rows_inverse(): pl.pallas_call(functools.partial(final_kernel, chunks, bands), grid=(rows...]
    all_to_all x1 -> x0, waiting for transfers between devices: 16.8 us -> none  [on_device(): lax.all_to_all(spectra[chunk], 'band', split_axis=0, concat_axis=0, tiled...]
    ppermute x0 -> x24, starting transfers between devices: none -> 16.1 us  [on_device(): block = lax.ppermute(block, 'band', pairs)]
    all_to_all x4, starting transfers between devices: 14.7 us -> 23.6 us  [on_device(): lax.all_to_all(phase, ('band', 'proj'), split_axis=0, concat_axis=0, tile...]
  transfers between devices with their start and end apart: 5 -> 28, of which waited for: 5 -> 15; matrix products, arithmetic and copies ran while one was open for 2% -> 4% of each run, Pallas kernels for 22% -> 16%
where the time goes in v2:
time: 489 us; the launch traced here: 488 us
  waiting for transfers between devices  252 us (52%)
  Pallas kernels  139 us (28%)
  starting transfers between devices  39.7 us (8%)
  local copies, waits for them, and re-layouts  27 us (6%)
  other arithmetic  19 us (4%)
  blocking collectives  8.31 us (2%)
    ppermute x24, waiting for transfers between devices, on_device(): block = lax.ppermute(block, 'band', pairs)  208 us
    pallas_call x4, Pallas kernels, columns(): pl.pallas_call(functools.partial(column_kernel, special, bands, parts), i...  76.3 us
    all_to_all x4, waiting for transfers between devices, on_device(): lax.all_to_all(phase, ('band', 'proj'), split_axis=0, concat_axis=0, tile...  44.1 us
    pallas_call x2, Pallas kernels, rows_forward(): pl.pallas_call(functools.partial(row_kernel, chunks, bands), grid=(blocks...  41.2 us
    all_to_all x4, starting transfers between devices, on_device(): lax.all_to_all(phase, ('band', 'proj'), split_axis=0, concat_axis=0, tile...  23.6 us
    pallas_call x1, Pallas kernels, rows_inverse(): pl.pallas_call(functools.partial(final_kernel, chunks, bands), grid=(rows...  21.4 us
    ppermute x24, starting transfers between devices, on_device(): block = lax.ppermute(block, 'band', pairs)  16.1 us
    unnamed x52, local copies, waits for them, and re-layouts  11.3 us
  transfers between devices with their start and end apart: 28, of which 15 were waited for; matrix products, arithmetic and copies ran while one was open for 4% of the time, Pallas kernels for 16%

profile of v2, /device:TPU:0, one launch (start us, length us, event | category | flops | bytes accessed | tf_op | source)
XLA Modules:
  0.0 488.3 jit_solution(11843446574366563758)
XLA Ops:
  0.0 10.9 %convert_reduce_fusion = f32[2]{0:T(128)S(1)} fusion(bf16[1,2,1024,4096]{3,2,1,0:T(8,128)(2,1)} %x_ref.3), kind=kLoop, calls=%fused_computation.1 | loop fusion | flops 16777214 | bytes 16777224 | tf_op jit(solution)/shard_map/reduce_sum | solution.py:511
  10.9 8.3 %psum.7 = f32[1,2]{1,0:T(1,128)S(1)} all-reduce(f32[1,2]{1,0:T(1,128)S(1)} %bitcast.161), channel_id=1, replica_groups=mesh['proj'=8,'band'=4] {'band'}, use_global_device_ids=true, to_apply=%region_2.0 | all-reduce | flops 2 | bytes 16 | tf_op jit(solution)/shard_map/psum | solution.py:511
  19.2 20.7 %rows_forward.3 = (bf16[512,512]{1,0:T(8,128)(2,1)S(1)}, bf16[512,512]{1,0:T(8,128)(2,1)}, bf16[512,512]{1,0:T(8,128)(2,1)}, bf16[512,512]{1,0:T(8,128)(2,1)}, b...) custom-call(s32[1]{0:T(128)} %bitcast.9.band_ref, ...), custom_call_target="tpu_custom_call" | custom-call | flops 6845104128 | bytes 26214400 | tf_op jit(solution)/shard_map/rows_forward/pallas_call | solution.py:241
  45.1 1.5 collective-permute-start.5
  46.6 20.5 %rows_forward.2 = (bf16[512,512]{1,0:T(8,128)(2,1)S(1)}, bf16[512,512]{1,0:T(8,128)(2,1)}, bf16[512,512]{1,0:T(8,128)(2,1)}, bf16[512,512]{1,0:T(8,128)(2,1)S(1)...) custom-call(s32[1]{0:T(128)} %bitcast.9.band_ref, ...), custom_call_target="tpu_custom_call" | custom-call | flops 6845104128 | bytes 26214400 | tf_op jit(solution)/shard_map/rows_forward/pallas_call | solution.py:241
  69.5 0.8 copy-done.13
  75.5 2.0 copy.111.rest_8_
  78.5 0.9 slice.100
  79.6 1.2 collective-permute-start.4
  81.1 0.9 slice.103
  82.2 0.9 slice.105
  83.2 0.9 slice.107
  84.2 0.9 slice.102
  85.2 3.7 collective-permute-done.2
  88.9 2.0 slice.104
  91.0 7.6 %collective-permute-done.4 = bf16[512,512]{1,0:T(8,128)(2,1)} collective-permute-done((bf16[512,512]{1,0:T(8,128)(2,1)}, bf16[512,512]{1,0:T(8,128)(2,1)}, u32[]{:S(2)}, u32[]{:S(2)}) %collective-permute-start.4) | collective-permute-done | bytes 524320 | tf_op jit(solution)/shard_map/ppermute | solution.py:540
  98.7 2.1 slice.106
  103.3 1.1 convolution_bitcast_fusion.2
  106.6 1.1 convolution_bitcast_fusion.3
  107.8 19.5 %columns.4 = bf16[32,128,256]{2,1,0:T(8,128)(2,1)} custom-call(s32[1]{0:T(128)} %bitcast.9.band_ref, f32[4,128]{1,0:T(4,128)S(1)} %get-tuple-element.84.v_ref, bf16[4,128,512]{2,1,0:T(8,128)(2,1)S(1)} %bitcast.121, bf16[4,128,512]{2,1,0:T(8,128)(2,1)S(1)} %bitcast.117, bf16[4,128,512]{2,1,0:T(8,128)(2,1)S(1)} %bitcast.122, ...), custom_call_target="tpu_custom_call" | custom-call | flops 4294967296 | bytes 25165824 | tf_op jit(solution)/shard_map/columns/pallas_call | solution.py:383
  127.4 5.1 %all-to-all-start = ((bf16[32,128,256]{2,1,0:T(8,128)(2,1)}), bf16[32,128,256]{2,1,0:T(8,128)(2,1)S(1)}, u32[]{:S(2)}, u32[]{:S(2)}) async-start(bf16[32,128,256]{2,1,0:T(8,128)(2,1)} %columns.4), calls=%async_computation | async-start | bytes 4194304 | tf_op jit(solution)/shard_map/all_to_all | solution.py:551
  132.8 1.7 collective-permute-start.9
  134.9 1.7 collective-permute-start.8
  136.6 28.5 %collective-permute-done.9 = bf16[512,512]{1,0:T(8,128)(2,1)S(1)} collective-permute-done((bf16[512,512]{1,0:T(8,128)(2,1)}, bf16[512,512]{1,0:T(8,128)(2,1)S(1)}, u32[]{:S(2)}, u32[]{:S(2)}) %collective-permute-start.9) | collective-permute-done | bytes 524320 | tf_op jit(solution)/shard_map/ppermute | solution.py:540
  165.2 12.5 %collective-permute-done.11 = bf16[512,512]{1,0:T(8,128)(2,1)S(1)} collective-permute-done((bf16[512,512]{1,0:T(8,128)(2,1)}, bf16[512,512]{1,0:T(8,128)(2,1)S(1)}, u32[]{:S(2)}, u32[]{:S(2)}) %collective-permute-start.11) | collective-permute-done | bytes 524320 | tf_op jit(solution)/shard_map/ppermute | solution.py:540
  177.7 14.3 %collective-permute-done.8 = bf16[512,512]{1,0:T(8,128)(2,1)S(1)} collective-permute-done((bf16[512,512]{1,0:T(8,128)(2,1)}, bf16[512,512]{1,0:T(8,128)(2,1)S(1)}, u32[]{:S(2)}, u32[]{:S(2)}) %collective-permute-start.8) | collective-permute-done | bytes 524320 | tf_op jit(solution)/shard_map/ppermute | solution.py:540
  192.0 10.3 %collective-permute-done.10 = bf16[512,512]{1,0:T(8,128)(2,1)S(1)} collective-permute-done((bf16[512,512]{1,0:T(8,128)(2,1)}, bf16[512,512]{1,0:T(8,128)(2,1)S(1)}, u32[]{:S(2)}, u32[]{:S(2)}) %collective-permute-start.10) | collective-permute-done | bytes 524320 | tf_op jit(solution)/shard_map/ppermute | solution.py:540
  202.3 18.9 %columns.5 = bf16[32,128,256]{2,1,0:T(8,128)(2,1)} custom-call(s32[1]{0:T(128)} %bitcast.9.band_ref, f32[4,128]{1,0:T(4,128)S(1)} %get-tuple-element.83.v_ref, bf16[4,128,512]{2,1,0:T(8,128)(2,1)S(1)} %bitcast.128, bf16[4,128,512]{2,1,0:T(8,128)(2,1)S(1)} %bitcast.127, bf16[4,128,512]{2,1,0:T(8,128)(2,1)S(1)} %bitcast.140, ...), custom_call_target="tpu_custom_call" | custom-call | flops 4294967296 | bytes 25165824 | tf_op jit(solution)/shard_map/columns/pallas_call | solution.py:383
  221.2 6.1 %all-to-all-start.1 = ((bf16[32,128,256]{2,1,0:T(8,128)(2,1)}), bf16[32,128,256]{2,1,0:T(8,128)(2,1)}, u32[]{:S(2)}, u32[]{:S(2)}) async-start(bf16[32,128,256]{2,1,0:T(8,128)(2,1)} %columns.5), calls=%async_computation.1 | async-start | bytes 4194304 | tf_op jit(solution)/shard_map/all_to_all | solution.py:551
  227.6 1.7 collective-permute-start.15
  229.7 1.7 collective-permute-start.14
  231.4 28.5 %collective-permute-done.15 = bf16[512,512]{1,0:T(8,128)(2,1)S(1)} collective-permute-done((bf16[512,512]{1,0:T(8,128)(2,1)}, bf16[512,512]{1,0:T(8,128)(2,1)S(1)}, u32[]{:S(2)}, u32[]{:S(2)}) %collective-permute-start.15) | collective-permute-done | bytes 524320 | tf_op jit(solution)/shard_map/ppermute | solution.py:540
  259.9 12.5 %collective-permute-done.17 = bf16[512,512]{1,0:T(8,128)(2,1)S(1)} collective-permute-done((bf16[512,512]{1,0:T(8,128)(2,1)}, bf16[512,512]{1,0:T(8,128)(2,1)S(1)}, u32[]{:S(2)}, u32[]{:S(2)}) %collective-permute-start.17) | collective-permute-done | bytes 524320 | tf_op jit(solution)/shard_map/ppermute | solution.py:540
  272.4 14.3 %collective-permute-done.14 = bf16[512,512]{1,0:T(8,128)(2,1)S(1)} collective-permute-done((bf16[512,512]{1,0:T(8,128)(2,1)}, bf16[512,512]{1,0:T(8,128)(2,1)S(1)}, u32[]{:S(2)}, u32[]{:S(2)}) %collective-permute-start.14) | collective-permute-done | bytes 524320 | tf_op jit(solution)/shard_map/ppermute | solution.py:540
  286.7 10.3 %collective-permute-done.16 = bf16[512,512]{1,0:T(8,128)(2,1)S(1)} collective-permute-done((bf16[512,512]{1,0:T(8,128)(2,1)}, bf16[512,512]{1,0:T(8,128)(2,1)S(1)}, u32[]{:S(2)}, u32[]{:S(2)}) %collective-permute-start.16) | collective-permute-done | bytes 524320 | tf_op jit(solution)/shard_map/ppermute | solution.py:540
  297.0 18.9 %columns.6 = bf16[32,128,256]{2,1,0:T(8,128)(2,1)} custom-call(s32[1]{0:T(128)} %bitcast.9.band_ref, f32[4,128]{1,0:T(4,128)S(1)} %get-tuple-element.82.v_ref, bf16[4,128,512]{2,1,0:T(8,128)(2,1)S(1)} %bitcast.126, bf16[4,128,512]{2,1,0:T(8,128)(2,1)S(1)} %bitcast.125, bf16[4,128,512]{2,1,0:T(8,128)(2,1)S(1)} %bitcast.141, ...), custom_call_target="tpu_custom_call" | custom-call | flops 4294967296 | bytes 25165824 | tf_op jit(solution)/shard_map/columns/pallas_call | solution.py:383
  316.0 6.1 %all-to-all-start.2 = ((bf16[32,128,256]{2,1,0:T(8,128)(2,1)}), bf16[32,128,256]{2,1,0:T(8,128)(2,1)}, u32[]{:S(2)}, u32[]{:S(2)}) async-start(bf16[32,128,256]{2,1,0:T(8,128)(2,1)} %columns.6), calls=%async_computation.2 | async-start | bytes 4194304 | tf_op jit(solution)/shard_map/all_to_all | solution.py:551
  322.3 1.7 collective-permute-start.21
  324.5 1.7 collective-permute-start.20
  326.2 28.5 %collective-permute-done.21 = bf16[512,512]{1,0:T(8,128)(2,1)S(1)} collective-permute-done((bf16[512,512]{1,0:T(8,128)(2,1)}, bf16[512,512]{1,0:T(8,128)(2,1)S(1)}, u32[]{:S(2)}, u32[]{:S(2)}) %collective-permute-start.21) | collective-permute-done | bytes 524320 | tf_op jit(solution)/shard_map/ppermute | solution.py:540
  354.6 12.5 %collective-permute-done.23 = bf16[512,512]{1,0:T(8,128)(2,1)S(1)} collective-permute-done((bf16[512,512]{1,0:T(8,128)(2,1)}, bf16[512,512]{1,0:T(8,128)(2,1)S(1)}, u32[]{:S(2)}, u32[]{:S(2)}) %collective-permute-start.23) | collective-permute-done | bytes 524320 | tf_op jit(solution)/shard_map/ppermute | solution.py:540
  367.2 14.3 %collective-permute-done.20 = bf16[512,512]{1,0:T(8,128)(2,1)S(1)} collective-permute-done((bf16[512,512]{1,0:T(8,128)(2,1)}, bf16[512,512]{1,0:T(8,128)(2,1)S(1)}, u32[]{:S(2)}, u32[]{:S(2)}) %collective-permute-start.20) | collective-permute-done | bytes 524320 | tf_op jit(solution)/shard_map/ppermute | solution.py:540
  381.5 10.3 %collective-permute-done.22 = bf16[512,512]{1,0:T(8,128)(2,1)S(1)} collective-permute-done((bf16[512,512]{1,0:T(8,128)(2,1)}, bf16[512,512]{1,0:T(8,128)(2,1)S(1)}, u32[]{:S(2)}, u32[]{:S(2)}) %collective-permute-start.22) | collective-permute-done | bytes 524320 | tf_op jit(solution)/shard_map/ppermute | solution.py:540
  391.8 18.9 %columns.7 = bf16[32,128,256]{2,1,0:T(8,128)(2,1)} custom-call(s32[1]{0:T(128)} %bitcast.9.band_ref, f32[4,128]{1,0:T(4,128)S(1)} %get-tuple-element.81.v_ref, bf16[4,128,512]{2,1,0:T(8,128)(2,1)S(1)} %bitcast.124, bf16[4,128,512]{2,1,0:T(8,128)(2,1)S(1)} %bitcast.123, bf16[4,128,512]{2,1,0:T(8,128)(2,1)S(1)} %bitcast.134, ...), custom_call_target="tpu_custom_call" | custom-call | flops 4294967296 | bytes 25165824 | tf_op jit(solution)/shard_map/columns/pallas_call | solution.py:383
  410.7 6.3 %all-to-all-start.3 = ((bf16[32,128,256]{2,1,0:T(8,128)(2,1)}), bf16[32,128,256]{2,1,0:T(8,128)(2,1)}, u32[]{:S(2)}, u32[]{:S(2)}) async-start(bf16[32,128,256]{2,1,0:T(8,128)(2,1)} %columns.7), calls=%async_computation.3 | async-start | bytes 4194304 | tf_op jit(solution)/shard_map/all_to_all | solution.py:551
  417.8 4.4 compare_select_fusion.1
  422.8 44.1 %all-to-all-done.3 = bf16[32,128,256]{2,1,0:T(8,128)(2,1)} async-done(((bf16[32,128,256]{2,1,0:T(8,128)(2,1)}), bf16[32,128,256]{2,1,0:T(8,128)(2,1)}, u32[]{:S(2)}, u32[]{:S(2)}) %all-to-all-start.3) | async-done | bytes 2097184 | tf_op jit(solution)/shard_map/all_to_all | solution.py:551
  466.9 21.4 %rows_inverse.1 = f32[1024,4096]{1,0:T(8,128)} custom-call(bf16[256,256]{1,0:T(8,128)(2,1)S(1)} %fusion.place_ref, bf16[4,8,128,256]{3,2,1,0:T(8,128)(2,1)S(1)} %bitcast.116, bf16[4,8,128,256]{3,2,1,0:T(8,128)(2,1)} %bitcast.66.rest_1_, bf16[4,8,128,256]{3,2,1,0:T(8,128)(2,1)} %bitcast.76.rest_2_, bf16[4,8,128,256]{3,2,1,0:T(8,128)(2,1)} %bitcast.86.rest_3_, ...), custom_call_target="tpu_custom_call" | custom-call | flops 10737418240 | bytes 33554432 | tf_op jit(solution)/shard_map/rows_inverse/pallas_call | solution.py:441
  (127 shorter events, 23.3 us)
Async XLA Ops:
  40.7 0.8 copy-start.10
  41.5 0.8 copy-start.11
  44.7 22.4 %copy-start.2 = (bf16[512,512]{1,0:T(8,128)(2,1)}, bf16[512,512]{1,0:T(8,128)(2,1)S(1)}, u32[]{:S(2)}) copy-start(bf16[512,512]{1,0:T(8,128)(2,1)S(1)} %get-tuple-element.54) | copy-start | bytes 1572868
  44.7 34.9 %collective-permute-start.1 = (bf16[512,512]{1,0:T(8,128)(2,1)}, bf16[512,512]{1,0:T(8,128)(2,1)S(1)}, u32[]{:S(2)}, u32[]{:S(2)}) collective-permute-start(bf16[512,512]{1,0:T(8,128)(2,1)} %get-tuple-element.40), channel_id=1, source_target_pairs={{0,1},{1,0},{2,3},{3,2},{4,5},{5,4},{6,7},{7,6},{8,9},{9,8},{10,11... | collective-permute-start | bytes 1572872 | tf_op jit(solution)/shard_map/ppermute | solution.py:540
  44.7 37.5 %collective-permute-start.3 = (bf16[512,512]{1,0:T(8,128)(2,1)}, bf16[512,512]{1,0:T(8,128)(2,1)S(1)}, u32[]{:S(2)}, u32[]{:S(2)}) collective-permute-start(bf16[512,512]{1,0:T(8,128)(2,1)} %get-tuple-element.42), channel_id=1, source_target_pairs={{0,2},{1,3},{2,0},{3,1},{4,6},{5,7},{6,4},{7,5},{8,10},{9,11},{10,... | collective-permute-start | bytes 1572872 | tf_op jit(solution)/shard_map/ppermute | solution.py:540
  45.1 29.2 %copy-start.24 = (f32[8]{0:T(128)S(1)}, f32[8]{0:T(128)}, u32[]{:S(2)}) copy-start(f32[8]{0:T(128)} %param.20) | copy-start | bytes 100
  45.1 29.2 %copy-start.25 = (s32[1,2]{1,0:T(1,128)S(1)}, s32[1,2]{1,0:T(1,128)}, u32[]{:S(2)}) copy-start(s32[1,2]{1,0:T(1,128)} %param.19) | copy-start | bytes 28
  45.1 38.1 %collective-permute-start.5 = (bf16[512,512]{1,0:T(8,128)(2,1)}, bf16[512,512]{1,0:T(8,128)(2,1)S(1)}, u32[]{:S(2)}, u32[]{:S(2)}) collective-permute-start(bf16[512,512]{1,0:T(8,128)(2,1)} %get-tuple-element.44), channel_id=1, source_target_pairs={{0,3},{1,2},{2,1},{3,0},{4,7},{5,6},{6,5},{7,4},{8,11},{9,10},{10,... | collective-permute-start | bytes 1572872 | tf_op jit(solution)/shard_map/ppermute | solution.py:540
  67.9 0.8 copy-start.8
  68.7 0.8 copy-start.12
  69.5 0.8 copy-start.13
  70.3 0.8 copy-start.17
  71.1 0.8 copy-start.18
  72.7 0.8 copy-start.20
  73.5 10.7 %collective-permute-start = (bf16[512,512]{1,0:T(8,128)(2,1)}, bf16[512,512]{1,0:T(8,128)(2,1)S(1)}, u32[]{:S(2)}, u32[]{:S(2)}) collective-permute-start(bf16[512,512]{1,0:T(8,128)(2,1)} %get-tuple-element.39), channel_id=1, source_target_pairs={{0,1},{1,0},{2,3},{3,2},{4,5},{5,4},{6,7},{7,6},{8,9},{9,8},{10,11... | collective-permute-start | bytes 1572872 | tf_op jit(solution)/shard_map/ppermute | solution.py:540
  73.9 15.1 %collective-permute-start.2 = (bf16[512,512]{1,0:T(8,128)(2,1)}, bf16[512,512]{1,0:T(8,128)(2,1)}, u32[]{:S(2)}, u32[]{:S(2)}) collective-permute-start(bf16[512,512]{1,0:T(8,128)(2,1)} %get-tuple-element.41), channel_id=1, source_target_pairs={{0,2},{1,3},{2,0},{3,1},{4,6},{5,7},{6,4},{7,5},{8,10},{9,11},{10,... | collective-permute-start | bytes 1572872 | tf_op jit(solution)/shard_map/ppermute | solution.py:540
  77.5 25.8 %copy-start.21 = (f32[2,64,2,64]{1,3,0,2:T(8,128)S(1)}, f32[2,64,2,64]{1,3,0,2:T(8,128)}, u32[]{:S(2)}) copy-start(f32[2,64,2,64]{1,3,0,2:T(8,128)} %constant.106.clone) | copy-start | bytes 196612
  79.6 19.1 %collective-permute-start.4 = (bf16[512,512]{1,0:T(8,128)(2,1)}, bf16[512,512]{1,0:T(8,128)(2,1)}, u32[]{:S(2)}, u32[]{:S(2)}) collective-permute-start(bf16[512,512]{1,0:T(8,128)(2,1)} %copy-done.20), channel_id=1, source_target_pairs={{0,3},{1,2},{2,1},{3,0},{4,7},{5,6},{6,5},{7,4},{8,11},{9,10},{10,... | collective-permute-start | bytes 1572872 | tf_op jit(solution)/shard_map/ppermute | solution.py:540
  101.0 4.5 copy-start.22
  127.3 74.9 %copy-start.7 = (bf16[512,512]{1,0:T(8,128)(2,1)S(1)}, bf16[512,512]{1,0:T(8,128)(2,1)}, u32[]{:S(2)}) copy-start(bf16[512,512]{1,0:T(8,128)(2,1)} %copy-done.6) | copy-start | bytes 1572868
  127.4 74.9 %copy-start.9 = (bf16[512,512]{1,0:T(8,128)(2,1)S(1)}, bf16[512,512]{1,0:T(8,128)(2,1)}, u32[]{:S(2)}) copy-start(bf16[512,512]{1,0:T(8,128)(2,1)} %copy-done.8) | copy-start | bytes 1572868
  127.4 93.9 %all-to-all-start = ((bf16[32,128,256]{2,1,0:T(8,128)(2,1)}), bf16[32,128,256]{2,1,0:T(8,128)(2,1)S(1)}, u32[]{:S(2)}, u32[]{:S(2)}) async-start(bf16[32,128,256]{2,1,0:T(8,128)(2,1)} %columns.4), calls=%async_computation | async-start | bytes 4194304 | tf_op jit(solution)/shard_map/all_to_all | solution.py:551
  132.5 4.1 collective-permute-start.7
  132.8 32.4 %collective-permute-start.9 = (bf16[512,512]{1,0:T(8,128)(2,1)}, bf16[512,512]{1,0:T(8,128)(2,1)S(1)}, u32[]{:S(2)}, u32[]{:S(2)}) collective-permute-start(bf16[512,512]{1,0:T(8,128)(2,1)} %copy-done.15), channel_id=1, source_target_pairs={{0,2},{1,3},{2,0},{3,1},{4,6},{5,7},{6,4},{7,5},{8,10},{9,11},{10,... | collective-permute-start | bytes 1572872 | tf_op jit(solution)/shard_map/ppermute | solution.py:540
  134.5 43.2 %collective-permute-start.11 = (bf16[512,512]{1,0:T(8,128)(2,1)}, bf16[512,512]{1,0:T(8,128)(2,1)S(1)}, u32[]{:S(2)}, u32[]{:S(2)}) collective-permute-start(bf16[512,512]{1,0:T(8,128)(2,1)} %copy-done.14), channel_id=1, source_target_pairs={{0,3},{1,2},{2,1},{3,0},{4,7},{5,6},{6,5},{7,4},{8,11},{9,10},{10,... | collective-permute-start | bytes 1572872 | tf_op jit(solution)/shard_map/ppermute | solution.py:540
  134.5 43.2 %collective-permute-start.6 = (bf16[512,512]{1,0:T(8,128)(2,1)}, bf16[512,512]{1,0:T(8,128)(2,1)S(1)}, u32[]{:S(2)}, u32[]{:S(2)}) collective-permute-start(bf16[512,512]{1,0:T(8,128)(2,1)} %copy-done.19), channel_id=1, source_target_pairs={{0,1},{1,0},{2,3},{3,2},{4,5},{5,4},{6,7},{7,6},{8,9},{9,8},{10,11... | collective-permute-start | bytes 1572872 | tf_op jit(solution)/shard_map/ppermute | solution.py:540
  134.9 57.1 %collective-permute-start.8 = (bf16[512,512]{1,0:T(8,128)(2,1)}, bf16[512,512]{1,0:T(8,128)(2,1)S(1)}, u32[]{:S(2)}, u32[]{:S(2)}) collective-permute-start(bf16[512,512]{1,0:T(8,128)(2,1)} %copy-done.18), channel_id=1, source_target_pairs={{0,2},{1,3},{2,0},{3,1},{4,6},{5,7},{6,4},{7,5},{8,10},{9,11},{10,... | collective-permute-start | bytes 1572872 | tf_op jit(solution)/shard_map/ppermute | solution.py:540
  136.6 65.7 %collective-permute-start.10 = (bf16[512,512]{1,0:T(8,128)(2,1)}, bf16[512,512]{1,0:T(8,128)(2,1)S(1)}, u32[]{:S(2)}, u32[]{:S(2)}) collective-permute-start(bf16[512,512]{1,0:T(8,128)(2,1)} %copy-done.17), channel_id=1, source_target_pairs={{0,3},{1,2},{2,1},{3,0},{4,7},{5,6},{6,5},{7,4},{8,11},{9,10},{10,... | collective-permute-start | bytes 1572872 | tf_op jit(solution)/shard_map/ppermute | solution.py:540
  221.2 75.8 %copy-start.3 = (bf16[512,512]{1,0:T(8,128)(2,1)S(1)}, bf16[512,512]{1,0:T(8,128)(2,1)}, u32[]{:S(2)}) copy-start(bf16[512,512]{1,0:T(8,128)(2,1)} %copy-done.2) | copy-start | bytes 1572868
  221.2 75.8 %copy-start.5 = (bf16[512,512]{1,0:T(8,128)(2,1)S(1)}, bf16[512,512]{1,0:T(8,128)(2,1)}, u32[]{:S(2)}) copy-start(bf16[512,512]{1,0:T(8,128)(2,1)} %copy-done.4) | copy-start | bytes 1572868
  221.2 94.7 %all-to-all-start.1 = ((bf16[32,128,256]{2,1,0:T(8,128)(2,1)}), bf16[32,128,256]{2,1,0:T(8,128)(2,1)}, u32[]{:S(2)}, u32[]{:S(2)}) async-start(bf16[32,128,256]{2,1,0:T(8,128)(2,1)} %columns.5), calls=%async_computation.1 | async-start | bytes 4194304 | tf_op jit(solution)/shard_map/all_to_all | solution.py:551
  227.3 4.1 collective-permute-start.13
  227.6 32.3 %collective-permute-start.15 = (bf16[512,512]{1,0:T(8,128)(2,1)}, bf16[512,512]{1,0:T(8,128)(2,1)S(1)}, u32[]{:S(2)}, u32[]{:S(2)}) collective-permute-start(bf16[512,512]{1,0:T(8,128)(2,1)} %copy-done.10), channel_id=1, source_target_pairs={{0,2},{1,3},{2,0},{3,1},{4,6},{5,7},{6,4},{7,5},{8,10},{9,11},{10,... | collective-permute-start | bytes 1572872 | tf_op jit(solution)/shard_map/ppermute | solution.py:540
  229.3 43.2 %collective-permute-start.17 = (bf16[512,512]{1,0:T(8,128)(2,1)}, bf16[512,512]{1,0:T(8,128)(2,1)S(1)}, u32[]{:S(2)}, u32[]{:S(2)}) collective-permute-start(bf16[512,512]{1,0:T(8,128)(2,1)} %get-tuple-element.60), channel_id=1, source_target_pairs={{0,3},{1,2},{2,1},{3,0},{4,7},{5,6},{6,5},{7,4},{8,11},{9,10},{10,... | collective-permute-start | bytes 1572872 | tf_op jit(solution)/shard_map/ppermute | solution.py:540
  229.3 43.2 %collective-permute-start.12 = (bf16[512,512]{1,0:T(8,128)(2,1)}, bf16[512,512]{1,0:T(8,128)(2,1)S(1)}, u32[]{:S(2)}, u32[]{:S(2)}) collective-permute-start(bf16[512,512]{1,0:T(8,128)(2,1)} %copy-done.13), channel_id=1, source_target_pairs={{0,1},{1,0},{2,3},{3,2},{4,5},{5,4},{6,7},{7,6},{8,9},{9,8},{10,11... | collective-permute-start | bytes 1572872 | tf_op jit(solution)/shard_map/ppermute | solution.py:540
  229.7 57.0 %collective-permute-start.14 = (bf16[512,512]{1,0:T(8,128)(2,1)}, bf16[512,512]{1,0:T(8,128)(2,1)S(1)}, u32[]{:S(2)}, u32[]{:S(2)}) collective-permute-start(bf16[512,512]{1,0:T(8,128)(2,1)} %copy-done.12), channel_id=1, source_target_pairs={{0,2},{1,3},{2,0},{3,1},{4,6},{5,7},{6,4},{7,5},{8,10},{9,11},{10,... | collective-permute-start | bytes 1572872 | tf_op jit(solution)/shard_map/ppermute | solution.py:540
  231.4 65.6 %collective-permute-start.16 = (bf16[512,512]{1,0:T(8,128)(2,1)}, bf16[512,512]{1,0:T(8,128)(2,1)S(1)}, u32[]{:S(2)}, u32[]{:S(2)}) collective-permute-start(bf16[512,512]{1,0:T(8,128)(2,1)} %get-tuple-element.59), channel_id=1, source_target_pairs={{0,3},{1,2},{2,1},{3,0},{4,7},{5,6},{6,5},{7,4},{8,11},{9,10},{10,... | collective-permute-start | bytes 1572872 | tf_op jit(solution)/shard_map/ppermute | solution.py:540
  315.9 75.8 %copy-start = (bf16[512,512]{1,0:T(8,128)(2,1)S(1)}, bf16[512,512]{1,0:T(8,128)(2,1)}, u32[]{:S(2)}) copy-start(bf16[512,512]{1,0:T(8,128)(2,1)} %get-tuple-element.62) | copy-start | bytes 1572868
  316.0 75.8 %copy-start.1 = (bf16[512,512]{1,0:T(8,128)(2,1)S(1)}, bf16[512,512]{1,0:T(8,128)(2,1)}, u32[]{:S(2)}) copy-start(bf16[512,512]{1,0:T(8,128)(2,1)} %get-tuple-element.61) | copy-start | bytes 1572868
  316.0 94.8 %all-to-all-start.2 = ((bf16[32,128,256]{2,1,0:T(8,128)(2,1)}), bf16[32,128,256]{2,1,0:T(8,128)(2,1)}, u32[]{:S(2)}, u32[]{:S(2)}) async-start(bf16[32,128,256]{2,1,0:T(8,128)(2,1)} %columns.6), calls=%async_computation.2 | async-start | bytes 4194304 | tf_op jit(solution)/shard_map/all_to_all | solution.py:551
  322.1 4.1 collective-permute-start.19
  322.3 32.3 %collective-permute-start.21 = (bf16[512,512]{1,0:T(8,128)(2,1)}, bf16[512,512]{1,0:T(8,128)(2,1)S(1)}, u32[]{:S(2)}, u32[]{:S(2)}) collective-permute-start(bf16[512,512]{1,0:T(8,128)(2,1)} %get-tuple-element.66), channel_id=1, source_target_pairs={{0,2},{1,3},{2,0},{3,1},{4,6},{5,7},{6,4},{7,5},{8,10},{9,11},{10,... | collective-permute-start | bytes 1572872 | tf_op jit(solution)/shard_map/ppermute | solution.py:540
  324.0 43.2 %collective-permute-start.23 = (bf16[512,512]{1,0:T(8,128)(2,1)}, bf16[512,512]{1,0:T(8,128)(2,1)S(1)}, u32[]{:S(2)}, u32[]{:S(2)}) collective-permute-start(bf16[512,512]{1,0:T(8,128)(2,1)} %get-tuple-element.68), channel_id=1, source_target_pairs={{0,3},{1,2},{2,1},{3,0},{4,7},{5,6},{6,5},{7,4},{8,11},{9,10},{10,... | collective-permute-start | bytes 1572872 | tf_op jit(solution)/shard_map/ppermute | solution.py:540
  324.0 43.2 %collective-permute-start.18 = (bf16[512,512]{1,0:T(8,128)(2,1)}, bf16[512,512]{1,0:T(8,128)(2,1)S(1)}, u32[]{:S(2)}, u32[]{:S(2)}) collective-permute-start(bf16[512,512]{1,0:T(8,128)(2,1)} %get-tuple-element.63), channel_id=1, source_target_pairs={{0,1},{1,0},{2,3},{3,2},{4,5},{5,4},{6,7},{7,6},{8,9},{9,8},{10,11... | collective-permute-start | bytes 1572872 | tf_op jit(solution)/shard_map/ppermute | solution.py:540
  324.5 57.0 %collective-permute-start.20 = (bf16[512,512]{1,0:T(8,128)(2,1)}, bf16[512,512]{1,0:T(8,128)(2,1)S(1)}, u32[]{:S(2)}, u32[]{:S(2)}) collective-permute-start(bf16[512,512]{1,0:T(8,128)(2,1)} %get-tuple-element.65), channel_id=1, source_target_pairs={{0,2},{1,3},{2,0},{3,1},{4,6},{5,7},{6,4},{7,5},{8,10},{9,11},{10,... | collective-permute-start | bytes 1572872 | tf_op jit(solution)/shard_map/ppermute | solution.py:540
  326.2 65.6 %collective-permute-start.22 = (bf16[512,512]{1,0:T(8,128)(2,1)}, bf16[512,512]{1,0:T(8,128)(2,1)S(1)}, u32[]{:S(2)}, u32[]{:S(2)}) collective-permute-start(bf16[512,512]{1,0:T(8,128)(2,1)} %get-tuple-element.67), channel_id=1, source_target_pairs={{0,3},{1,2},{2,1},{3,0},{4,7},{5,6},{6,5},{7,4},{8,11},{9,10},{10,... | collective-permute-start | bytes 1572872 | tf_op jit(solution)/shard_map/ppermute | solution.py:540
  410.7 6.4 %copy-start.23 = (s32[8]{0:T(128)S(1)}, s32[8]{0:T(128)}, u32[]{:S(2)}) copy-start(s32[8]{0:T(128)} %param.21) | copy-start | bytes 100
  410.7 56.2 %all-to-all-start.3 = ((bf16[32,128,256]{2,1,0:T(8,128)(2,1)}), bf16[32,128,256]{2,1,0:T(8,128)(2,1)}, u32[]{:S(2)}, u32[]{:S(2)}) async-start(bf16[32,128,256]{2,1,0:T(8,128)(2,1)} %columns.7), calls=%async_computation.3 | async-start | bytes 4194304 | tf_op jit(solution)/shard_map/all_to_all | solution.py:551
  (6 other events, 4.8 us)

commit v3 on v2

--- a/solution.py
+++ b/solution.py
@@ -154,7 +154,39 @@
     return jnp.dot(x, y, preferred_element_type=F32)
 
 
-def row_kernel(chunks, bands, band_ref, scale_ref, x_ref, high_hbm, low_hbm, *rest):
+def sum_kernel(x_ref, out_ref, total_ref):
+    @pl.when(pl.program_id(0) == 0)
+    def _():
+        total_ref[...] = jnp.zeros_like(total_ref)
+
+    rows = x_ref.shape[2]
+    for frame in range(2):
+        values = x_ref[0, frame].astype(F32).reshape(rows // 8, 8, LENGTH)
+        total_ref[frame] += jnp.sum(values, axis=0)
+
+    @pl.when(pl.program_id(0) == pl.num_programs(0) - 1)
+    def _():
+        for frame in range(2):
+            out_ref[0, frame] = jnp.sum(total_ref[frame])
+
+
+def frame_sums(intensities):
+    rows = intensities.shape[2]
+    block = 128
+    return pl.pallas_call(
+        sum_kernel,
+        grid=(rows // block,),
+        in_specs=[pl.BlockSpec((1, 2, block, LENGTH), lambda i: (0, 0, i, 0))],
+        out_specs=pl.BlockSpec(memory_space=pltpu.SMEM),
+        out_shape=jax.ShapeDtypeStruct((1, 2), F32),
+        scratch_shapes=[pltpu.VMEM((2, 8, LENGTH), F32)],
+        compiler_params=pltpu.CompilerParams(vmem_limit_bytes=58 * MIB),
+        name="frame_sums",
+    )(intensities)
+
+
+def row_kernel(chunks, bands, kept, band_ref, scale_ref, x_ref, high_hbm, low_hbm, *rest):
+    rest = rest[kept:]
     outs = rest[: chunks * bands]
     mid_ref, xs_ref, high_ref, low_ref, sems = rest[chunks * bands :]
     rows_here = x_ref.shape[2]
@@ -231,15 +263,18 @@
     return pl.BlockSpec(shape, lambda *_: (0,) * len(shape), pipeline_mode=pl.Buffered(1))
 
 
-def rows_forward(intensities, scale, band, bands, chunks, part, parts):
-    rows = intensities.shape[2] // parts
+def rows_forward(intensities, scale, band, bands, chunks, part, parts, earlier):
+    total = intensities.shape[2]
+    rows = total // parts
     block = min(256, rows)
     blocks = rows // block
     high, low = row_tables()
     width = 4 * MINOR
-    count = chunks * bands
+    later = (chunks - 1) * bands
+    alone = pl.BlockSpec((block, width), lambda i: (i, 0))
+    shared = pl.BlockSpec((block, width), lambda i: (i + part * blocks, 0))
     outs = pl.pallas_call(
-        functools.partial(row_kernel, chunks, bands),
+        functools.partial(row_kernel, chunks, bands, len(earlier)),
         grid=(blocks,),
         in_specs=[
             pl.BlockSpec(memory_space=pltpu.SMEM),
@@ -247,9 +282,11 @@
             pl.BlockSpec((1, 2, block, LENGTH), lambda i: (0, 0, i + part * blocks, 0)),
             any_spec(),
             any_spec(),
-        ],
-        out_specs=[pl.BlockSpec((block, width), lambda i: (i, 0))] * count,
-        out_shape=[jax.ShapeDtypeStruct((rows, width), BF16)] * count,
+        ]
+        + [any_spec()] * len(earlier),
+        out_specs=[alone] * bands + [shared] * later,
+        out_shape=[jax.ShapeDtypeStruct((rows, width), BF16)] * bands
+        + [jax.ShapeDtypeStruct((total, width), BF16)] * later,
         scratch_shapes=[
             pltpu.VMEM((64, 16, MINOR), F32),
             pltpu.VMEM((MAJOR, block, 4 * MINOR), BF16),
@@ -257,13 +294,14 @@
             pltpu.VMEM(low.shape, BF16),
             pltpu.SemaphoreType.DMA((2,)),
         ],
-        compiler_params=pltpu.CompilerParams(vmem_limit_bytes=48 * MIB),
+        input_output_aliases={5 + index: bands + index for index in range(len(earlier))},
+        compiler_params=pltpu.CompilerParams(vmem_limit_bytes=58 * MIB),
         cost_estimate=pl.CostEstimate(
-            flops=rows * 34 * 6 * 256 * 256, bytes_accessed=4 * rows * LENGTH * 2 + 9 * MIB, transcendentals=0
+            flops=64 * rows * 34 * 6 * 256 * 256, bytes_accessed=4 * rows * LENGTH * 2 + 9 * MIB, transcendentals=0
         ),
         name="rows_forward",
-    )(band, scale, intensities, jnp.asarray(high), jnp.asarray(low))
-    return [outs[bands * chunk : bands * (chunk + 1)] for chunk in range(chunks)]
+    )(band, scale, intensities, jnp.asarray(high), jnp.asarray(low), *earlier)
+    return outs
 
 
 def column_kernel(special, bands, parts, band_ref, v_ref, *rest):
@@ -394,9 +432,9 @@
         ]
         + [pltpu.VMEM(fh.shape, BF16)] * 4
         + [pltpu.SemaphoreType.DMA((count + 5,))],
-        compiler_params=pltpu.CompilerParams(vmem_limit_bytes=48 * MIB),
+        compiler_params=pltpu.CompilerParams(vmem_limit_bytes=58 * MIB),
         cost_estimate=pl.CostEstimate(
-            flops=32 * 8 * 256 * 256 * 256, bytes_accessed=24 * MIB, transcendentals=0
+            flops=64 * 32 * 8 * 256 * 256 * 256, bytes_accessed=24 * MIB, transcendentals=0
         ),
         name="columns",
     )(*operands)
@@ -450,7 +488,7 @@
             pltpu.VMEM((HALF, count, 2 * MINOR), BF16),
             pltpu.VMEM((HALF, count, 2 * MINOR), F32),
         ],
-        compiler_params=pltpu.CompilerParams(vmem_limit_bytes=48 * MIB),
+        compiler_params=pltpu.CompilerParams(vmem_limit_bytes=56 * MIB),
         cost_estimate=pl.CostEstimate(
             flops=rows * projections * 16 * 10 * 256 * 256,
             bytes_accessed=rows * projections * LENGTH * 6 + 8 * MIB,
@@ -508,12 +546,16 @@
     projections = lax.axis_size("proj")
     band = lax.axis_index("band")
     chunks = HALF // bands
-    totals = lax.psum(jnp.sum(intensities.astype(F32), axis=(2, 3)), "band")
+    totals = lax.psum(frame_sums(intensities), "band")
     scale = (rows * bands * LENGTH) / totals
 
     here = jnp.asarray(band, jnp.int32).reshape(1)
     parts = 2
-    spectra = [rows_forward(intensities, scale, here, bands, chunks, part, parts) for part in range(parts)]
+    firsts, others = [], []
+    for part in range(parts):
+        outs = rows_forward(intensities, scale, here, bands, chunks, part, parts, others)
+        firsts.append(outs[:bands])
+        others = outs[bands:]
 
     table_size = fresnel_table.shape[0]
     onehot = (dist_index[0][:, None] == jnp.arange(table_size, dtype=jnp.int32)[None, :]).astype(F32)
@@ -534,18 +576,19 @@
         blocks = []
         for offset in range(bands):
             pairs = [(source, source ^ offset) for source in range(bands)]
-            for part in range(parts):
-                block = spectra[part][chunk][offset]
-                if offset:
-                    block = lax.ppermute(block, "band", pairs)
-                blocks.append(block)
+            if chunk == 0:
+                sources = [first[offset] for first in firsts]
+            else:
+                sources = [others[(chunk - 1) * bands + offset]]
+            for block in sources:
+                blocks.append(lax.ppermute(block, "band", pairs) if offset else block)
         nyquist = None
         if chunk == 0:
             sent = jnp.stack([block[:, 2 * MINOR :: MINOR] for block in blocks]).astype(F32)
             sent = sent.reshape(bands, rows, 2)[jnp.arange(bands, dtype=jnp.int32) ^ band]
             nyquist = nyquist_column(sent[:, :, 0], sent[:, :, 1], coefficient)
         blocks = [block.reshape(-1, MINOR, 4 * MINOR) for block in blocks]
-        phase = columns(blocks, here, along_u, along_v[chunk], nyquist, bands, parts)
+        phase = columns(blocks, here, along_u, along_v[chunk], nyquist, bands, len(blocks) // bands)
         rows_to = LENGTH // (bands * projections)
         phase = phase.reshape(bands * projections, rows_to, 2 * MINOR)
         back = lax.all_to_all(phase, ("band", "proj"), split_axis=0, concat_axis=0, tiled=True)

time: 489 us -> 421 us (0.86)
  waiting for transfers between devices: 252 us -> 199 us
  Pallas kernels: 139 us -> 156 us
  other arithmetic: 19 us -> 6.99 us
  starting transfers between devices: 39.7 us -> 30.1 us
  local copies, waits for them, and re-layouts: 27 us -> 17.9 us
    ppermute x24 -> x15, waiting for transfers between devices: 208 us -> 74.3 us  [on_device(): blocks.append(lax.ppermute(block, 'band', pairs) if offset else block)]
    all_to_all x4, waiting for transfers between devices: 44.1 us -> 125 us  [on_device(): lax.all_to_all(phase, ('band', 'proj'), split_axis=0, concat_axis=0, tile...]
    reduce_sum x1 -> x0, other arithmetic: 10.9 us -> none  [on_device(): totals = lax.psum(jnp.sum(intensities.astype(F32), axis=(2, 3)), 'band')]
    pallas_call x2 -> x3, Pallas kernels: 41.2 us -> 52 us  [the longest x2 42.7 us: rows_forward(): pl.pallas_call(functools.partial(row_kernel, chunks, bands, len(earlier))...]
    unnamed x52 -> x28, local copies, waits for them, and re-layouts: 11.3 us -> 1.47 us
    pallas_call x4, Pallas kernels: 76.3 us -> 82.7 us  [columns(): pl.pallas_call(functools.partial(column_kernel, special, bands, parts), i...]
    ppermute x24 -> x15, starting transfers between devices: 16.1 us -> 11.2 us  [on_device(): blocks.append(lax.ppermute(block, 'band', pairs) if offset else block)]
  transfers between devices with their start and end apart: 28 -> 19, of which waited for: 15 -> 10; matrix products, arithmetic and copies ran while one was open for 4% -> 6% of each run, Pallas kernels for 16% -> 20%
where the time goes in v3:
time: 421 us; the launch traced here: 420 us
  waiting for transfers between devices  199 us (47%)
  Pallas kernels  156 us (37%)
  starting transfers between devices  30.1 us (7%)
  local copies, waits for them, and re-layouts  17.9 us (4%)
  blocking collectives  8.48 us (2%)
  other arithmetic  6.99 us (2%)
    all_to_all x4, waiting for transfers between devices, on_device(): lax.all_to_all(phase, ('band', 'proj'), split_axis=0, concat_axis=0, tile...  125 us
    pallas_call x4, Pallas kernels, columns(): pl.pallas_call(functools.partial(column_kernel, special, bands, parts), i...  82.7 us
    ppermute x15, waiting for transfers between devices, on_device(): blocks.append(lax.ppermute(block, 'band', pairs) if offset else block)  74.3 us
    pallas_call x2, Pallas kernels, rows_forward(): pl.pallas_call(functools.partial(row_kernel, chunks, bands, len(earlier))...  42.7 us
    pallas_call x1, Pallas kernels, rows_inverse(): pl.pallas_call(functools.partial(final_kernel, chunks, bands), grid=(rows...  21.4 us
    all_to_all x4, starting transfers between devices, on_device(): lax.all_to_all(phase, ('band', 'proj'), split_axis=0, concat_axis=0, tile...  19 us
    ppermute x15, starting transfers between devices, on_device(): blocks.append(lax.ppermute(block, 'band', pairs) if offset else block)  11.2 us
    slice x8, local copies, waits for them, and re-layouts, on_device(): block[:, 2 * MINOR::MINOR]  10.1 us
  transfers between devices with their start and end apart: 19, of which 10 were waited for; matrix products, arithmetic and copies ran while one was open for 6% of the time, Pallas kernels for 20%

profile of v3, /device:TPU:0, one launch (start us, length us, event | category | flops | bytes accessed | tf_op | source)
XLA Modules:
  0.0 420.0 jit_solution(11734249094060530732)
XLA Ops:
  0.0 9.3 %frame_sums.1 = f32[1,2]{1,0:T(1,128)} custom-call(bf16[1,2,1024,4096]{3,2,1,0:T(8,128)(2,1)} %x_ref.5), custom_call_target="tpu_custom_call" | custom-call | tf_op jit(solution)/shard_map/frame_sums/pallas_call | solution.py:176
  9.3 8.5 %psum.7 = f32[1,2]{1,0:T(1,128)S(1)} all-reduce(f32[1,2]{1,0:T(1,128)} %frame_sums.1), channel_id=1, replica_groups=mesh['proj'=8,'band'=4] {'band'}, use_global_device_ids=true, to_apply=%region_1.0 | all-reduce | flops 2 | bytes 16 | tf_op jit(solution)/shard_map/psum | solution.py:549
  17.8 0.5 broadcast_divide_fusion.scale_ref
  18.3 21.3 %rows_forward.2 = (bf16[512,512]{1,0:T(8,128)(2,1)}, bf16[512,512]{1,0:T(8,128)(2,1)}, bf16[512,512]{1,0:T(8,128)(2,1)}, bf16[512,512]{1,0:T(8,128)(2,1)}, bf16[...) custom-call(s32[1]{0:T(128)} %bitcast.9.band_ref, ...), custom_call_target="tpu_custom_call" | custom-call | flops 438086664192 | bytes 26214400 | tf_op jit(solution)/shard_map/rows_forward/pallas_call | solution.py:276
  39.6 21.4 %rows_forward.3 = (bf16[512,512]{1,0:T(8,128)(2,1)}, bf16[512,512]{1,0:T(8,128)(2,1)}, bf16[512,512]{1,0:T(8,128)(2,1)}, bf16[512,512]{1,0:T(8,128)(2,1)}, bf16[...) custom-call(s32[1]{0:T(128)} %bitcast.9.band_ref, ...), custom_call_target="tpu_custom_call", output_to_operand_aliasing={{4}: (5, {}), {5}: (6, {}), {6}: (7, {}), {7}: (8, {}), {8}... | custom-call | flops 438086664192 | bytes 26214400 | tf_op jit(solution)/shard_map/rows_forward/pallas_call | solution.py:276
  61.6 1.4 collective-permute-start.5
  64.4 2.0 copy.123.rest_8_.rest_4_
  66.3 2.0 slice.101
  68.4 2.0 slice.100
  70.6 0.6 slice_bitcast_fusion
  71.3 1.2 collective-permute-start.4
  72.7 0.9 slice.103
  73.8 2.3 collective-permute-done.3
  76.1 0.9 slice.105
  77.1 9.3 %collective-permute-done.5 = bf16[512,512]{1,0:T(8,128)(2,1)S(1)} collective-permute-done((bf16[512,512]{1,0:T(8,128)(2,1)}, bf16[512,512]{1,0:T(8,128)(2,1)S(1)}, u32[]{:S(2)}, u32[]{:S(2)}) %collective-permute-start.5) | collective-permute-done | bytes 524320 | tf_op jit(solution)/shard_map/ppermute | solution.py:584
  86.4 0.6 collective-permute-start.13
  87.0 0.8 slice.107
  88.0 1.6 collective-permute-start.14
  89.6 0.8 slice.102
  90.5 8.0 %collective-permute-done.2 = bf16[512,512]{1,0:T(8,128)(2,1)S(1)} collective-permute-done((bf16[512,512]{1,0:T(8,128)(2,1)}, bf16[512,512]{1,0:T(8,128)(2,1)S(1)}, u32[]{:S(2)}, u32[]{:S(2)}) %collective-permute-start.2) | collective-permute-done | bytes 524320 | tf_op jit(solution)/shard_map/ppermute | solution.py:584
  98.6 0.9 slice.104
  99.6 9.4 %collective-permute-done.4 = bf16[512,512]{1,0:T(8,128)(2,1)} collective-permute-done((bf16[512,512]{1,0:T(8,128)(2,1)}, bf16[512,512]{1,0:T(8,128)(2,1)}, u32[]{:S(2)}, u32[]{:S(2)}) %collective-permute-start.4) | collective-permute-done | bytes 524320 | tf_op jit(solution)/shard_map/ppermute | solution.py:584
  109.5 2.0 slice.106
  111.8 0.6 gather_fusion
  114.0 0.7 copy.122
  114.7 21.1 %columns.4 = bf16[32,128,256]{2,1,0:T(8,128)(2,1)} custom-call(s32[1]{0:T(128)} %bitcast.9.band_ref, f32[4,128]{1,0:T(4,128)} %get-tuple-element.84.v_ref, bf16[4,128,512]{2,1,0:T(8,128)(2,1)} %bitcast.113, bf16[4,128,512]{2,1,0:T(8,128)(2,1)} %bitcast.114, bf16[4,128,512]{2,1,0:T(8,128)(2,1)} %bitcast.118, bf16[4,128,512]{2,1,0:T(8,128)(2,1)} %bitcast.115, ...), custom_call_target="tpu_custom_call" | custom-call | flops 274877906944 | bytes 25165824 | tf_op jit(solution)/shard_map/columns/pallas_call | solution.py:421
  135.8 6.1 %all-to-all-start = ((bf16[32,128,256]{2,1,0:T(8,128)(2,1)}), bf16[32,128,256]{2,1,0:T(8,128)(2,1)}, u32[]{:S(2)}, u32[]{:S(2)}) async-start(bf16[32,128,256]{2,1,0:T(8,128)(2,1)} %columns.4), calls=%async_computation | async-start | bytes 4194304 | tf_op jit(solution)/shard_map/all_to_all | solution.py:594
  141.9 1.5 collective-permute-start.11
  143.8 18.2 %collective-permute-done.14 = bf16[1024,512]{1,0:T(8,128)(2,1)} collective-permute-done((bf16[1024,512]{1,0:T(8,128)(2,1)}, bf16[1024,512]{1,0:T(8,128)(2,1)}, u32[]{:S(2)}, u32[]{:S(2)}) %collective-permute-start.14) | collective-permute-done | bytes 1048608 | tf_op jit(solution)/shard_map/ppermute | solution.py:584
  162.0 0.6 collective-permute-start.7
  162.6 20.5 %columns.7 = bf16[32,128,256]{2,1,0:T(8,128)(2,1)} custom-call(s32[1]{0:T(128)} %bitcast.9.band_ref, f32[4,128]{1,0:T(4,128)} %get-tuple-element.81.v_ref, bf16[8,128,512]{2,1,0:T(8,128)(2,1)} %bitcast.128, bf16[8,128,512]{2,1,0:T(8,128)(2,1)} %bitcast.70.rest_1_, bf16[8,128,512]{2,1,0:T(8,128)(2,1)} %bitcast.71.rest_2_, ...), custom_call_target="tpu_custom_call" | custom-call | flops 274877906944 | bytes 25165824 | tf_op jit(solution)/shard_map/columns/pallas_call | solution.py:421
  183.1 2.2 collective-permute-start.8
  185.4 14.4 %all-to-all-done = bf16[32,128,256]{2,1,0:T(8,128)(2,1)} async-done(((bf16[32,128,256]{2,1,0:T(8,128)(2,1)}), bf16[32,128,256]{2,1,0:T(8,128)(2,1)}, u32[]{:S(2)}, u32[]{:S(2)}) %all-to-all-start) | async-done | bytes 2097184 | tf_op jit(solution)/shard_map/all_to_all | solution.py:594
  199.8 5.1 %all-to-all-start.3 = ((bf16[32,128,256]{2,1,0:T(8,128)(2,1)}), bf16[32,128,256]{2,1,0:T(8,128)(2,1)}, u32[]{:S(2)}, u32[]{:S(2)}) async-start(bf16[32,128,256]{2,1,0:T(8,128)(2,1)} %columns.7), calls=%async_computation.3 | async-start | bytes 4194304 | tf_op jit(solution)/shard_map/all_to_all | solution.py:594
  204.9 27.0 %collective-permute-done.11 = bf16[1024,512]{1,0:T(8,128)(2,1)} collective-permute-done((bf16[1024,512]{1,0:T(8,128)(2,1)}, bf16[1024,512]{1,0:T(8,128)(2,1)}, u32[]{:S(2)}, u32[]{:S(2)}) %collective-permute-start.11) | collective-permute-done | bytes 1048608 | tf_op jit(solution)/shard_map/ppermute | solution.py:584
  231.9 20.5 %columns.6 = bf16[32,128,256]{2,1,0:T(8,128)(2,1)} custom-call(s32[1]{0:T(128)} %bitcast.9.band_ref, f32[4,128]{1,0:T(4,128)} %get-tuple-element.82.v_ref, bf16[8,128,512]{2,1,0:T(8,128)(2,1)} %bitcast.127, bf16[8,128,512]{2,1,0:T(8,128)(2,1)} %bitcast.64.rest_1_, bf16[8,128,512]{2,1,0:T(8,128)(2,1)} %bitcast.65.rest_2_, ...), custom_call_target="tpu_custom_call" | custom-call | flops 274877906944 | bytes 25165824 | tf_op jit(solution)/shard_map/columns/pallas_call | solution.py:421
  252.4 36.9 %all-to-all-done.3 = bf16[32,128,256]{2,1,0:T(8,128)(2,1)} async-done(((bf16[32,128,256]{2,1,0:T(8,128)(2,1)}), bf16[32,128,256]{2,1,0:T(8,128)(2,1)}, u32[]{:S(2)}, u32[]{:S(2)}) %all-to-all-start.3) | async-done | bytes 2097184 | tf_op jit(solution)/shard_map/all_to_all | solution.py:594
  289.2 5.1 %all-to-all-start.2 = ((bf16[32,128,256]{2,1,0:T(8,128)(2,1)}), bf16[32,128,256]{2,1,0:T(8,128)(2,1)}, u32[]{:S(2)}, u32[]{:S(2)}) async-start(bf16[32,128,256]{2,1,0:T(8,128)(2,1)} %columns.6), calls=%async_computation.2 | async-start | bytes 4194304 | tf_op jit(solution)/shard_map/all_to_all | solution.py:594
  294.3 20.5 %columns.5 = bf16[32,128,256]{2,1,0:T(8,128)(2,1)} custom-call(s32[1]{0:T(128)} %bitcast.9.band_ref, f32[4,128]{1,0:T(4,128)} %get-tuple-element.83.v_ref, bf16[8,128,512]{2,1,0:T(8,128)(2,1)} %bitcast.126, bf16[8,128,512]{2,1,0:T(8,128)(2,1)} %bitcast.58.rest_1_, bf16[8,128,512]{2,1,0:T(8,128)(2,1)} %bitcast.59.rest_2_, ...), custom_call_target="tpu_custom_call" | custom-call | flops 274877906944 | bytes 25165824 | tf_op jit(solution)/shard_map/columns/pallas_call | solution.py:421
  314.9 29.5 %all-to-all-done.2 = bf16[32,128,256]{2,1,0:T(8,128)(2,1)} async-done(((bf16[32,128,256]{2,1,0:T(8,128)(2,1)}), bf16[32,128,256]{2,1,0:T(8,128)(2,1)}, u32[]{:S(2)}, u32[]{:S(2)}) %all-to-all-start.2) | async-done | bytes 2097184 | tf_op jit(solution)/shard_map/all_to_all | solution.py:594
  344.4 2.7 all-to-all-start.1
  347.1 0.7 fusion.31
  347.8 4.3 %compare_select_fusion.1 = s32[256,1]{0,1:T(1,128)S(1)} fusion(s32[]{:T(128)} %bitcast.1, s32[]{:T(128)} %bitcast.2, s32[]{:T(128)} %bitcast.3, s32[]{:T(128)} %bitcast.4, s32[]{:T(128)} %bitcast.5, s32[]{:T(128)} %bitcast.7, s32[]{:T(128)} %bitcast.6), kind=kLoop, calls=%fused_computation.48 | loop fusion | flops 5888 | bytes 1052 | tf_op jit(solution)/shard_map/gather | solution.py:477
  352.1 0.7 fusion.22
  352.7 0.7 fusion.place_ref
  353.4 43.7 %all-to-all-done.1 = bf16[32,128,256]{2,1,0:T(8,128)(2,1)S(1)} async-done(((bf16[32,128,256]{2,1,0:T(8,128)(2,1)}), bf16[32,128,256]{2,1,0:T(8,128)(2,1)S(1)}, u32[]{:S(2)}, u32[]{:S(2)}) %all-to-all-start.1) | async-done | bytes 2097184 | tf_op jit(solution)/shard_map/all_to_all | solution.py:594
  397.2 1.4 copy-done
  398.6 21.4 %rows_inverse.1 = f32[1024,4096]{1,0:T(8,128)} custom-call(bf16[256,256]{1,0:T(8,128)(2,1)} %fusion.place_ref, bf16[4,8,128,256]{3,2,1,0:T(8,128)(2,1)} %bitcast.55.rest_0_, bf16[4,8,128,256]{3,2,1,0:T(8,128)(2,1)} %bitcast.103, bf16[4,8,128,256]{3,2,1,0:T(8,128)(2,1)} %bitcast.67.rest_2_, bf16[4,8,128,256]{3,2,1,0:T(8,128)(2,1)} %bitcast.73.rest_3_, ...), custom_call_target="tpu_custom_call" | custom-call | flops 10737418240 | bytes 33554432 | tf_op jit(solution)/shard_map/rows_inverse/pallas_call | solution.py:479
  (85 shorter events, 6.0 us)
Async XLA Ops:
  39.6 24.2 %copy-start.12 = (f32[8]{0:T(128)S(1)}, f32[8]{0:T(128)}, u32[]{:S(2)}) copy-start(f32[8]{0:T(128)} %param.20) | copy-start | bytes 100
  39.6 24.2 %copy-start.13 = (s32[1,2]{1,0:T(1,128)S(1)}, s32[1,2]{1,0:T(1,128)}, u32[]{:S(2)}) copy-start(s32[1,2]{1,0:T(1,128)} %param.19) | copy-start | bytes 28
  61.0 10.2 %collective-permute-start.1 = (bf16[512,512]{1,0:T(8,128)(2,1)}, bf16[512,512]{1,0:T(8,128)(2,1)S(1)}, u32[]{:S(2)}, u32[]{:S(2)}) collective-permute-start(bf16[512,512]{1,0:T(8,128)(2,1)} %get-tuple-element.52), channel_id=1, source_target_pairs={{0,1},{1,0},{2,3},{3,2},{4,5},{5,4},{6,7},{7,6},{8,9},{9,8},{10,11... | collective-permute-start | bytes 1572872 | tf_op jit(solution)/shard_map/ppermute | solution.py:584
  61.1 15.0 %collective-permute-start.3 = (bf16[512,512]{1,0:T(8,128)(2,1)}, bf16[512,512]{1,0:T(8,128)(2,1)S(1)}, u32[]{:S(2)}, u32[]{:S(2)}) collective-permute-start(bf16[512,512]{1,0:T(8,128)(2,1)} %get-tuple-element.54), channel_id=1, source_target_pairs={{0,2},{1,3},{2,0},{3,1},{4,6},{5,7},{6,4},{7,5},{8,10},{9,11},{10,... | collective-permute-start | bytes 1572872 | tf_op jit(solution)/shard_map/ppermute | solution.py:584
  61.6 24.8 %collective-permute-start.5 = (bf16[512,512]{1,0:T(8,128)(2,1)}, bf16[512,512]{1,0:T(8,128)(2,1)S(1)}, u32[]{:S(2)}, u32[]{:S(2)}) collective-permute-start(bf16[512,512]{1,0:T(8,128)(2,1)} %get-tuple-element.56), channel_id=1, source_target_pairs={{0,3},{1,2},{2,1},{3,0},{4,7},{5,6},{6,5},{7,4},{8,11},{9,10},{10,... | collective-permute-start | bytes 1572872 | tf_op jit(solution)/shard_map/ppermute | solution.py:584
  63.0 25.0 %collective-permute-start = (bf16[512,512]{1,0:T(8,128)(2,1)}, bf16[512,512]{1,0:T(8,128)(2,1)S(1)}, u32[]{:S(2)}, u32[]{:S(2)}) collective-permute-start(bf16[512,512]{1,0:T(8,128)(2,1)} %get-tuple-element.51), channel_id=1, source_target_pairs={{0,1},{1,0},{2,3},{3,2},{4,5},{5,4},{6,7},{7,6},{8,9},{9,8},{10,11... | collective-permute-start | bytes 1572872 | tf_op jit(solution)/shard_map/ppermute | solution.py:584
  63.3 35.3 %collective-permute-start.2 = (bf16[512,512]{1,0:T(8,128)(2,1)}, bf16[512,512]{1,0:T(8,128)(2,1)S(1)}, u32[]{:S(2)}, u32[]{:S(2)}) collective-permute-start(bf16[512,512]{1,0:T(8,128)(2,1)} %get-tuple-element.53), channel_id=1, source_target_pairs={{0,2},{1,3},{2,0},{3,1},{4,6},{5,7},{6,4},{7,5},{8,10},{9,11},{10,... | collective-permute-start | bytes 1572872 | tf_op jit(solution)/shard_map/ppermute | solution.py:584
  71.3 41.1 %copy-start.6 = (bf16[512,512]{1,0:T(8,128)(2,1)}, bf16[512,512]{1,0:T(8,128)(2,1)S(1)}, u32[]{:S(2)}) copy-start(bf16[512,512]{1,0:T(8,128)(2,1)S(1)} %collective-permute-done.1) | copy-start | bytes 1572868
  71.3 37.8 %collective-permute-start.4 = (bf16[512,512]{1,0:T(8,128)(2,1)}, bf16[512,512]{1,0:T(8,128)(2,1)}, u32[]{:S(2)}, u32[]{:S(2)}) collective-permute-start(bf16[512,512]{1,0:T(8,128)(2,1)} %get-tuple-element.55), channel_id=1, source_target_pairs={{0,3},{1,2},{2,1},{3,0},{4,7},{5,6},{6,5},{7,4},{8,11},{9,10},{10,... | collective-permute-start | bytes 1572872 | tf_op jit(solution)/shard_map/ppermute | solution.py:584
  76.1 36.3 %copy-start.7 = (bf16[512,512]{1,0:T(8,128)(2,1)}, bf16[512,512]{1,0:T(8,128)(2,1)S(1)}, u32[]{:S(2)}) copy-start(bf16[512,512]{1,0:T(8,128)(2,1)S(1)} %collective-permute-done.3) | copy-start | bytes 1572868
  76.1 65.8 %collective-permute-start.12 = (bf16[1024,512]{1,0:T(8,128)(2,1)}, bf16[1024,512]{1,0:T(8,128)(2,1)}, u32[]{:S(2)}, u32[]{:S(2)}) collective-permute-start(bf16[1024,512]{1,0:T(8,128)(2,1)} %get-tuple-element.66), channel_id=1, source_target_pairs={{0,1},{1,0},{2,3},{3,2},{4,5},{5,4},{6,7},{7,6},{8,9},{9,8},{10,11... | collective-permute-start | bytes 3145736 | tf_op jit(solution)/shard_map/ppermute | solution.py:584
  86.4 25.9 %copy-start.8 = (bf16[512,512]{1,0:T(8,128)(2,1)}, bf16[512,512]{1,0:T(8,128)(2,1)S(1)}, u32[]{:S(2)}) copy-start(bf16[512,512]{1,0:T(8,128)(2,1)S(1)} %collective-permute-done.5) | copy-start | bytes 1572868
  86.4 57.0 %collective-permute-start.13 = (bf16[1024,512]{1,0:T(8,128)(2,1)}, bf16[1024,512]{1,0:T(8,128)(2,1)}, u32[]{:S(2)}, u32[]{:S(2)}) collective-permute-start(bf16[1024,512]{1,0:T(8,128)(2,1)} %get-tuple-element.67), channel_id=1, source_target_pairs={{0,2},{1,3},{2,0},{3,1},{4,6},{5,7},{6,4},{7,5},{8,10},{9,11},{10,... | collective-permute-start | bytes 3145736 | tf_op jit(solution)/shard_map/ppermute | solution.py:584
  88.0 24.4 %copy-start.9 = (bf16[512,512]{1,0:T(8,128)(2,1)}, bf16[512,512]{1,0:T(8,128)(2,1)S(1)}, u32[]{:S(2)}) copy-start(bf16[512,512]{1,0:T(8,128)(2,1)S(1)} %collective-permute-done) | copy-start | bytes 1572868
  88.0 74.0 %collective-permute-start.14 = (bf16[1024,512]{1,0:T(8,128)(2,1)}, bf16[1024,512]{1,0:T(8,128)(2,1)}, u32[]{:S(2)}, u32[]{:S(2)}) collective-permute-start(bf16[1024,512]{1,0:T(8,128)(2,1)} %get-tuple-element.68), channel_id=1, source_target_pairs={{0,3},{1,2},{2,1},{3,0},{4,7},{5,6},{6,5},{7,4},{8,11},{9,10},{10,... | collective-permute-start | bytes 3145736 | tf_op jit(solution)/shard_map/ppermute | solution.py:584
  98.6 13.8 %copy-start.10 = (bf16[512,512]{1,0:T(8,128)(2,1)}, bf16[512,512]{1,0:T(8,128)(2,1)S(1)}, u32[]{:S(2)}) copy-start(bf16[512,512]{1,0:T(8,128)(2,1)S(1)} %collective-permute-done.2) | copy-start | bytes 1572868
  98.6 84.6 %collective-permute-start.9 = (bf16[1024,512]{1,0:T(8,128)(2,1)}, bf16[1024,512]{1,0:T(8,128)(2,1)}, u32[]{:S(2)}, u32[]{:S(2)}) collective-permute-start(bf16[1024,512]{1,0:T(8,128)(2,1)} %get-tuple-element.62), channel_id=1, source_target_pairs={{0,1},{1,0},{2,3},{3,2},{4,5},{5,4},{6,7},{7,6},{8,9},{9,8},{10,11... | collective-permute-start | bytes 3145736 | tf_op jit(solution)/shard_map/ppermute | solution.py:584
  109.0 95.8 %collective-permute-start.10 = (bf16[1024,512]{1,0:T(8,128)(2,1)}, bf16[1024,512]{1,0:T(8,128)(2,1)}, u32[]{:S(2)}, u32[]{:S(2)}) collective-permute-start(bf16[1024,512]{1,0:T(8,128)(2,1)} %get-tuple-element.63), channel_id=1, source_target_pairs={{0,2},{1,3},{2,0},{3,1},{4,6},{5,7},{6,4},{7,5},{8,10},{9,11},{10,... | collective-permute-start | bytes 3145736 | tf_op jit(solution)/shard_map/ppermute | solution.py:584
  111.7 1.0 copy-start.1
  111.7 1.3 copy-start.3
  111.7 1.3 copy-start.4
  111.7 1.6 copy-start.2
  111.7 1.9 copy-start.5
  135.8 64.0 %all-to-all-start = ((bf16[32,128,256]{2,1,0:T(8,128)(2,1)}), bf16[32,128,256]{2,1,0:T(8,128)(2,1)}, u32[]{:S(2)}, u32[]{:S(2)}) async-start(bf16[32,128,256]{2,1,0:T(8,128)(2,1)} %columns.4), calls=%async_computation | async-start | bytes 4194304 | tf_op jit(solution)/shard_map/all_to_all | solution.py:594
  141.9 89.9 %collective-permute-start.11 = (bf16[1024,512]{1,0:T(8,128)(2,1)}, bf16[1024,512]{1,0:T(8,128)(2,1)}, u32[]{:S(2)}, u32[]{:S(2)}) collective-permute-start(bf16[1024,512]{1,0:T(8,128)(2,1)} %get-tuple-element.64), channel_id=1, source_target_pairs={{0,3},{1,2},{2,1},{3,0},{4,7},{5,6},{6,5},{7,4},{8,11},{9,10},{10,... | collective-permute-start | bytes 3145736 | tf_op jit(solution)/shard_map/ppermute | solution.py:584
  143.4 150.8 %collective-permute-start.6 = (bf16[1024,512]{1,0:T(8,128)(2,1)}, bf16[1024,512]{1,0:T(8,128)(2,1)}, u32[]{:S(2)}, u32[]{:S(2)}) collective-permute-start(bf16[1024,512]{1,0:T(8,128)(2,1)} %get-tuple-element.58), channel_id=1, source_target_pairs={{0,1},{1,0},{2,3},{3,2},{4,5},{5,4},{6,7},{7,6},{8,9},{9,8},{10,11... | collective-permute-start | bytes 3145736 | tf_op jit(solution)/shard_map/ppermute | solution.py:584
  162.0 132.3 %collective-permute-start.7 = (bf16[1024,512]{1,0:T(8,128)(2,1)}, bf16[1024,512]{1,0:T(8,128)(2,1)}, u32[]{:S(2)}, u32[]{:S(2)}) collective-permute-start(bf16[1024,512]{1,0:T(8,128)(2,1)} %get-tuple-element.59), channel_id=1, source_target_pairs={{0,2},{1,3},{2,0},{3,1},{4,6},{5,7},{6,4},{7,5},{8,10},{9,11},{10,... | collective-permute-start | bytes 3145736 | tf_op jit(solution)/shard_map/ppermute | solution.py:584
  183.1 111.2 %collective-permute-start.8 = (bf16[1024,512]{1,0:T(8,128)(2,1)}, bf16[1024,512]{1,0:T(8,128)(2,1)}, u32[]{:S(2)}, u32[]{:S(2)}) collective-permute-start(bf16[1024,512]{1,0:T(8,128)(2,1)} %get-tuple-element.60), channel_id=1, source_target_pairs={{0,3},{1,2},{2,1},{3,0},{4,7},{5,6},{6,5},{7,4},{8,11},{9,10},{10,... | collective-permute-start | bytes 3145736 | tf_op jit(solution)/shard_map/ppermute | solution.py:584
  199.8 89.4 %all-to-all-start.3 = ((bf16[32,128,256]{2,1,0:T(8,128)(2,1)}), bf16[32,128,256]{2,1,0:T(8,128)(2,1)}, u32[]{:S(2)}, u32[]{:S(2)}) async-start(bf16[32,128,256]{2,1,0:T(8,128)(2,1)} %columns.7), calls=%async_computation.3 | async-start | bytes 4194304 | tf_op jit(solution)/shard_map/all_to_all | solution.py:594
  289.2 55.1 %all-to-all-start.2 = ((bf16[32,128,256]{2,1,0:T(8,128)(2,1)}), bf16[32,128,256]{2,1,0:T(8,128)(2,1)}, u32[]{:S(2)}, u32[]{:S(2)}) async-start(bf16[32,128,256]{2,1,0:T(8,128)(2,1)} %columns.6), calls=%async_computation.2 | async-start | bytes 4194304 | tf_op jit(solution)/shard_map/all_to_all | solution.py:594
  314.9 32.3 %copy-start.11 = (s32[8]{0:T(128)S(1)}, s32[8]{0:T(128)}, u32[]{:S(2)}) copy-start(s32[8]{0:T(128)} %param.21) | copy-start | bytes 100
  344.4 52.8 %all-to-all-start.1 = ((bf16[32,128,256]{2,1,0:T(8,128)(2,1)}), bf16[32,128,256]{2,1,0:T(8,128)(2,1)S(1)}, u32[]{:S(2)}, u32[]{:S(2)}) async-start(bf16[32,128,256]{2,1,0:T(8,128)(2,1)} %columns.5), calls=%async_computation.1 | async-start | bytes 4194304 | tf_op jit(solution)/shard_map/all_to_all | solution.py:594
  397.2 1.4 copy-start

commit v4 on v3

--- a/solution.py
+++ b/solution.py
@@ -14,6 +14,7 @@
 MAJOR = 32
 MINOR = 128
 HALF = MAJOR // 2
+TILES = 2
 F32 = jnp.float32
 BF16 = jnp.bfloat16
 MIB = 1 << 20
@@ -137,17 +138,28 @@
     return out
 
 
-def dft32(load, store, mid_ref):
-    for b in range(8):
-        part = dft4([load(8 * a + b) for a in range(4)])
-        for k in range(4):
-            re, im = turn(part[k], b * k, 32)
-            mid_ref[2 * (8 * k + b)] = re
-            mid_ref[2 * (8 * k + b) + 1] = im
+def dft4_half(x):
+    return [add(x[0], x[1]), (x[0][0] + x[1][1], x[0][1] - x[1][0]), sub(x[0], x[1]), (x[0][0] - x[1][1], x[0][1] + x[1][0])]
+
+
+def dft32_first(part, b, mid_ref):
+    for k in range(4):
+        re, im = turn(part[k], b * k, 32)
+        mid_ref[2 * (8 * k + b)] = re
+        mid_ref[2 * (8 * k + b) + 1] = im
+
+
+def dft32_last(store, mid_ref):
     for k in range(4):
         part = dft8([(mid_ref[2 * (8 * k + b)], mid_ref[2 * (8 * k + b) + 1]) for b in range(8)])
         for m in range(8):
             store(k + 4 * m, *part[m])
+
+
+def dft32(load, store, mid_ref):
+    for b in range(8):
+        dft32_first(dft4([load(8 * a + b) for a in range(4)]), b, mid_ref)
+    dft32_last(store, mid_ref)
 
 
 def dot(x, y):
@@ -185,8 +197,7 @@
     )(intensities)
 
 
-def row_kernel(chunks, bands, kept, band_ref, scale_ref, x_ref, high_hbm, low_hbm, *rest):
-    rest = rest[kept:]
+def row_kernel(chunks, bands, band_ref, scale_ref, x_ref, high_hbm, low_hbm, *rest):
     outs = rest[: chunks * bands]
     mid_ref, xs_ref, high_ref, low_ref, sems = rest[chunks * bands :]
     rows_here = x_ref.shape[2]
@@ -238,17 +249,21 @@
 
     width = 2 * MINOR
     for chunk in range(chunks):
-        for offset in range(bands):
-            t = chunk * bands + (band ^ offset)
-            out_ref = outs[chunk * bands + offset]
-            out_ref[:, :width] = apply(t, 2 * t).astype(BF16)
-            out_ref[:, width:] = apply(lax.rem(MAJOR - t, MAJOR), 2 * t + 1).astype(BF16)
+        for place in range(TILES):
+            start = 2 * width * place
+            for offset in range(bands):
+                t = (chunk * TILES + place) * bands + (band ^ offset)
+                out_ref = outs[chunk * bands + offset]
+                out_ref[:, start : start + width] = apply(t, 2 * t).astype(BF16)
+                out_ref[:, start + width : start + 2 * width] = apply(
+                    lax.rem(MAJOR - t, MAJOR), 2 * t + 1
+                ).astype(BF16)
     for offset in range(bands):
 
         @pl.when(band == offset)
         def _(offset=offset):
             outs[offset][:, :width] = (apply(0, 0) + apply(HALF, 32)).astype(BF16)
-            outs[offset][:, width:] = (apply(0, 1) + apply(HALF, 33)).astype(BF16)
+            outs[offset][:, width : 2 * width] = (apply(0, 1) + apply(HALF, 33)).astype(BF16)
 
 
 def whole_spec():
@@ -263,30 +278,24 @@
     return pl.BlockSpec(shape, lambda *_: (0,) * len(shape), pipeline_mode=pl.Buffered(1))
 
 
-def rows_forward(intensities, scale, band, bands, chunks, part, parts, earlier):
-    total = intensities.shape[2]
-    rows = total // parts
+def rows_forward(intensities, scale, band, bands, chunks):
+    rows = intensities.shape[2]
     block = min(256, rows)
-    blocks = rows // block
     high, low = row_tables()
-    width = 4 * MINOR
-    later = (chunks - 1) * bands
-    alone = pl.BlockSpec((block, width), lambda i: (i, 0))
-    shared = pl.BlockSpec((block, width), lambda i: (i + part * blocks, 0))
-    outs = pl.pallas_call(
-        functools.partial(row_kernel, chunks, bands, len(earlier)),
-        grid=(blocks,),
+    width = TILES * 4 * MINOR
+    count = chunks * bands
+    return pl.pallas_call(
+        functools.partial(row_kernel, chunks, bands),
+        grid=(rows // block,),
         in_specs=[
             pl.BlockSpec(memory_space=pltpu.SMEM),
             pl.BlockSpec(memory_space=pltpu.SMEM),
-            pl.BlockSpec((1, 2, block, LENGTH), lambda i: (0, 0, i + part * blocks, 0)),
+            pl.BlockSpec((1, 2, block, LENGTH), lambda i: (0, 0, i, 0)),
             any_spec(),
             any_spec(),
-        ]
-        + [any_spec()] * len(earlier),
-        out_specs=[alone] * bands + [shared] * later,
-        out_shape=[jax.ShapeDtypeStruct((rows, width), BF16)] * bands
-        + [jax.ShapeDtypeStruct((total, width), BF16)] * later,
+        ],
+        out_specs=[pl.BlockSpec((block, width), lambda i: (i, 0))] * count,
+        out_shape=[jax.ShapeDtypeStruct((rows, width), BF16)] * count,
         scratch_shapes=[
             pltpu.VMEM((64, 16, MINOR), F32),
             pltpu.VMEM((MAJOR, block, 4 * MINOR), BF16),
@@ -294,42 +303,35 @@
             pltpu.VMEM(low.shape, BF16),
             pltpu.SemaphoreType.DMA((2,)),
         ],
-        input_output_aliases={5 + index: bands + index for index in range(len(earlier))},
         compiler_params=pltpu.CompilerParams(vmem_limit_bytes=58 * MIB),
         cost_estimate=pl.CostEstimate(
             flops=64 * rows * 34 * 6 * 256 * 256, bytes_accessed=4 * rows * LENGTH * 2 + 9 * MIB, transcendentals=0
         ),
         name="rows_forward",
-    )(band, scale, intensities, jnp.asarray(high), jnp.asarray(low), *earlier)
-    return outs
-
-
-def column_kernel(special, bands, parts, band_ref, v_ref, *rest):
-    blocks = rest[: bands * parts]
-    u_hbm, *table_hbms = rest[bands * parts : bands * parts + 5]
-    rest = rest[bands * parts + 5 :]
+    )(band, scale, intensities, jnp.asarray(high), jnp.asarray(low))
+
+
+def column_kernel(special, bands, band_ref, v_ref, *rest):
+    blocks = rest[:bands]
+    u_hbm, *table_hbms = rest[bands : bands + 5]
+    rest = rest[bands + 5 :]
     band = band_ref[0]
     if special:
-        nyquist_ref, out_ref, mid_ref, xs_ref, ys_ref, x_ref, u_ref, fh_ref, fl_ref, ih_ref, il_ref, sems = rest
+        nyquist_ref, *rest = rest
         lane = lax.broadcasted_iota(jnp.int32, (16, MINOR), 1)
         own = (lane == 0) & (band == 0)
-    else:
-        out_ref, mid_ref, xs_ref, ys_ref, x_ref, u_ref, fh_ref, fl_ref, ih_ref, il_ref, sems = rest
+    near_ref, far_ref, mid_ref, xs_ref, ys_ref, x_ref, u_ref, fh_ref, fl_ref, ih_ref, il_ref, sems = rest
 
     fetches = []
-    height = MAJOR // (bands * parts)
+    height = HALF // bands
     for offset in range(bands):
-        for part in range(parts):
-            index = offset * parts + part
-            start = (band ^ offset) * (height * parts) + part * height
-            fetches.append(
-                pltpu.make_async_copy(blocks[index], x_ref.at[pl.ds(start, height)], sems.at[index])
-            )
+        start = (band ^ offset) * height
+        fetches.append(pltpu.make_async_copy(blocks[offset], x_ref.at[pl.ds(start, height)], sems.at[offset]))
     late = []
     for index, (source, target) in enumerate(
         zip([u_hbm] + table_hbms, (u_ref, fh_ref, fl_ref, ih_ref, il_ref))
     ):
-        late.append(pltpu.make_async_copy(source, target, sems.at[bands * parts + index]))
+        late.append(pltpu.make_async_copy(source, target, sems.at[bands + index]))
     for fetch in fetches + late:
         fetch.start()
     for fetch in fetches:
@@ -339,102 +341,125 @@
         start = pl.multiple_of(index * 16, 16)
         rows = pl.ds(start, 16)
         below = pl.ds(pl.multiple_of(start + MINOR, 16), 16)
-        for frame in range(2):
-
-            def load(a, frame=frame):
+        for tile in range(TILES):
+            patch = special and tile == 0
+
+            def load(a, tile=tile, patch=patch):
                 pos_re, pos_im, neg_re, neg_im = [
-                    x_ref[a, rows, MINOR * i : MINOR * (i + 1)].astype(F32) for i in range(4)
+                    x_ref[a, rows, MINOR * i : MINOR * (i + 1)].astype(F32) for i in range(4 * tile, 4 * tile + 4)
                 ]
-                if special:
+                if patch:
                     neg_re = jnp.where(own, pos_re, neg_re)
                     neg_im = jnp.where(own, pos_im, neg_im)
-                if frame == 0:
-                    return pos_re + neg_re, pos_im - neg_im
-                return pos_im + neg_im, neg_re - pos_re
-
-            def store(k, re, im, frame=frame):
-                lanes = slice(MINOR * frame, MINOR * (frame + 1))
-                xs_ref[k, rows, lanes] = re.astype(BF16)
-                xs_ref[k, below, lanes] = im.astype(BF16)
-
-            dft32(load, store, mid_ref)
+                return (pos_re + neg_re, pos_im - neg_im), (pos_im + neg_im, neg_re - pos_re)
+
+            for b in range(8):
+                values = [load(8 * a + b) for a in range(2)]
+                for frame in range(2):
+                    part = dft4_half([value[frame] for value in values])
+                    dft32_first(part, b, mid_ref.at[2 * tile + frame])
+            for frame in range(2):
+
+                def store(k, re, im, tile=tile, frame=frame):
+                    lanes = slice(MINOR * (2 * tile + frame), MINOR * (2 * tile + frame + 1))
+                    xs_ref[k, rows, lanes] = re.astype(BF16)
+                    xs_ref[k, below, lanes] = im.astype(BF16)
+
+                dft32_last(store, mid_ref.at[2 * tile + frame])
         return carry
 
     lax.fori_loop(0, MINOR // 16, forward, 0)
     for fetch in late:
         fetch.wait()
 
-    sin_even_v, cos_even_v, sin_odd_v, cos_odd_v = [v_ref[i : i + 1, :] for i in range(4)]
+    along_v = [[v_ref[tile, i : i + 1, :] for i in range(4)] for tile in range(TILES)]
 
     def middle(k):
         values = xs_ref[k]
         table = jnp.concatenate([fh_ref[k], fl_ref[k]], axis=1)
         spectra = dot(table, jnp.concatenate([values, values], axis=0))
         column = u_ref[k]
-        sin_even = column[:, 0:1] * cos_even_v + column[:, 1:2] * sin_even_v
-        sin_odd = column[:, 2:3] * cos_odd_v + column[:, 3:4] * sin_odd_v
-        scale = 1.0 / (4.0 * (sin_even * sin_even + sin_odd * sin_odd) + 2.0 * alpha_reg)
-        sin_even = sin_even * scale
-        sin_odd = sin_odd * scale
-        phase_re = sin_even * spectra[:MINOR, :MINOR] + sin_odd * spectra[:MINOR, MINOR:]
-        phase_im = sin_even * spectra[MINOR:, :MINOR] + sin_odd * spectra[MINOR:, MINOR:]
-        phase = jnp.concatenate([phase_re.astype(BF16), phase_im.astype(BF16)], axis=0)
+        along_u = [column[:, i : i + 1] for i in range(4)]
+        parts_re, parts_im = [], []
+        for tile in range(TILES):
+            sin_even = along_u[0] * along_v[tile][1] + along_u[1] * along_v[tile][0]
+            sin_odd = along_u[2] * along_v[tile][3] + along_u[3] * along_v[tile][2]
+            scale = 1.0 / (4.0 * (sin_even * sin_even + sin_odd * sin_odd) + 2.0 * alpha_reg)
+            sin_even = sin_even * scale
+            sin_odd = sin_odd * scale
+            even = slice(2 * MINOR * tile, 2 * MINOR * tile + MINOR)
+            odd = slice(2 * MINOR * tile + MINOR, 2 * MINOR * (tile + 1))
+            phase_re = sin_even * spectra[:MINOR, even] + sin_odd * spectra[:MINOR, odd]
+            phase_im = sin_even * spectra[MINOR:, even] + sin_odd * spectra[MINOR:, odd]
+            parts_re.append(phase_re.astype(BF16))
+            parts_im.append(phase_im.astype(BF16))
+        phase = jnp.concatenate([jnp.concatenate(parts_re, axis=1), jnp.concatenate(parts_im, axis=1)], axis=0)
         table = jnp.concatenate([ih_ref[k], il_ref[k]], axis=1)
         ys_ref[k] = dot(table, jnp.concatenate([phase, phase], axis=0))
 
     def middles(index, carry):
-        for step in range(4):
-            middle(4 * index + step)
+        for step in range(2):
+            middle(2 * index + step)
         return carry
 
-    lax.fori_loop(0, MAJOR // 4, middles, 0)
+    lax.fori_loop(0, MAJOR // 2, middles, 0)
 
     def inverse(index, carry):
         start = pl.multiple_of(index * 16, 16)
         rows = pl.ds(start, 16)
         below = pl.ds(pl.multiple_of(start + MINOR, 16), 16)
-
-        def load(k):
-            return ys_ref[k, below, :], ys_ref[k, rows, :]
-
-        def store(a, im, re):
-            if special:
-                im = jnp.where(own, nyquist_ref[rows, a : a + 1], im)
-            out_ref[a, rows, :MINOR] = re.astype(BF16)
-            out_ref[a, rows, MINOR:] = im.astype(BF16)
-
-        dft32(load, store, mid_ref)
+        for tile in range(TILES):
+            lanes = slice(MINOR * tile, MINOR * (tile + 1))
+            patch = special and tile == 0
+
+            def load(k, lanes=lanes):
+                return ys_ref[k, below, lanes], ys_ref[k, rows, lanes]
+
+            def store(a, im, re, tile=tile, patch=patch):
+                if patch:
+                    im = jnp.where(own, nyquist_ref[rows, a : a + 1], im)
+                first = slice(2 * MINOR * tile, 2 * MINOR * tile + MINOR)
+                second = slice(2 * MINOR * tile + MINOR, 2 * MINOR * (tile + 1))
+                if a < HALF:
+                    near_ref[a, rows, first] = re
+                    near_ref[a, rows, second] = im
+                else:
+                    far_ref[a - HALF, rows, first] = re.astype(BF16)
+                    far_ref[a - HALF, rows, second] = im.astype(BF16)
+
+            dft32(load, store, mid_ref.at[tile])
         return carry
 
     lax.fori_loop(0, MINOR // 16, inverse, 0)
 
 
-def columns(blocks, band, along_u, along_v, nyquist, bands, parts):
+def columns(blocks, band, along_u, along_v, nyquist):
     (fh, fl), (ih, il) = column_tables()
     special = nyquist is not None
-    count = bands * parts
+    bands = len(blocks)
     operands = [band, along_v, *blocks, along_u] + [jnp.asarray(t) for t in (fh, fl, ih, il)]
-    in_specs = [pl.BlockSpec(memory_space=pltpu.SMEM), whole_spec()] + [any_spec()] * (count + 5)
+    in_specs = [pl.BlockSpec(memory_space=pltpu.SMEM), whole_spec()] + [any_spec()] * (bands + 5)
     if special:
         operands.append(nyquist)
         in_specs.append(whole_spec())
+    shape = (HALF, MINOR, TILES * 2 * MINOR)
     return pl.pallas_call(
-        functools.partial(column_kernel, special, bands, parts),
+        functools.partial(column_kernel, special, bands),
         in_specs=in_specs,
-        out_specs=whole_spec(),
-        out_shape=jax.ShapeDtypeStruct((MAJOR, MINOR, 2 * MINOR), BF16),
+        out_specs=[whole_spec()] * 2,
+        out_shape=[jax.ShapeDtypeStruct(shape, F32), jax.ShapeDtypeStruct(shape, BF16)],
         scratch_shapes=[
-            pltpu.VMEM((64, 16, MINOR), F32),
-            pltpu.VMEM((MAJOR, 2 * MINOR, 2 * MINOR), BF16),
-            pltpu.VMEM((MAJOR, 2 * MINOR, MINOR), F32),
-            pltpu.VMEM((MAJOR, MINOR, 4 * MINOR), BF16),
+            pltpu.VMEM((2 * TILES, 64, 16, MINOR), F32),
+            pltpu.VMEM((MAJOR, 2 * MINOR, TILES * 2 * MINOR), BF16),
+            pltpu.VMEM((MAJOR, 2 * MINOR, TILES * MINOR), F32),
+            pltpu.VMEM((HALF, MINOR, TILES * 4 * MINOR), BF16),
             pltpu.VMEM(along_u.shape, F32),
         ]
         + [pltpu.VMEM(fh.shape, BF16)] * 4
-        + [pltpu.SemaphoreType.DMA((count + 5,))],
+        + [pltpu.SemaphoreType.DMA((bands + 5,))],
         compiler_params=pltpu.CompilerParams(vmem_limit_bytes=58 * MIB),
         cost_estimate=pl.CostEstimate(
-            flops=64 * 32 * 8 * 256 * 256 * 256, bytes_accessed=24 * MIB, transcendentals=0
+            flops=128 * 32 * 8 * 256 * 256 * 256, bytes_accessed=30 * MIB, transcendentals=0
         ),
         name="columns",
     )(*operands)
@@ -444,10 +469,12 @@
     ins, (high_ref, low_ref, out_ref, xs_ref, zs_ref) = rest[:chunks], rest[chunks:]
     place = place_ref[...]
     count = place.shape[0]
+    width = 2 * MINOR
     for chunk in range(chunks):
-        for band in range(bands):
-            values = ins[chunk][band].reshape(count, 2 * MINOR)
-            xs_ref[chunk * bands + band] = dot(place, values).astype(BF16)
+        for tile in range(TILES):
+            for band in range(bands):
+                values = ins[chunk][band, :, :, width * tile : width * (tile + 1)].reshape(count, width)
+                xs_ref[(chunk * TILES + tile) * bands + band] = dot(place, values).astype(BF16)
 
     for t in range(HALF):
         partner = (HALF - t) % HALF
@@ -542,20 +569,16 @@
 
 def on_device(intensities, dist_index, fresnel_table, proj_order):
     rows = intensities.shape[2]
-    bands = lax.axis_size("band")
+    halves = lax.axis_size("half")
+    bands = lax.axis_size("inner")
     projections = lax.axis_size("proj")
-    band = lax.axis_index("band")
-    chunks = HALF // bands
-    totals = lax.psum(frame_sums(intensities), "band")
-    scale = (rows * bands * LENGTH) / totals
+    band = lax.axis_index("inner")
+    chunks = HALF // (bands * TILES)
+    totals = lax.psum(frame_sums(intensities), ("half", "inner"))
+    scale = (rows * bands * halves * LENGTH) / totals
 
     here = jnp.asarray(band, jnp.int32).reshape(1)
-    parts = 2
-    firsts, others = [], []
-    for part in range(parts):
-        outs = rows_forward(intensities, scale, here, bands, chunks, part, parts, others)
-        firsts.append(outs[:bands])
-        others = outs[bands:]
+    spectra = rows_forward(intensities, scale, here, bands, chunks)
 
     table_size = fresnel_table.shape[0]
     onehot = (dist_index[0][:, None] == jnp.arange(table_size, dtype=jnp.int32)[None, :]).astype(F32)
@@ -564,42 +587,44 @@
     s_index = lax.broadcasted_iota(jnp.int32, (MAJOR, MINOR), 1)
     angle_u = math.pi * coefficient[:, None, None] * folded_square(k_index + MAJOR * s_index, LENGTH)
     along_u = jnp.stack([jnp.sin(angle_u[0]), jnp.cos(angle_u[0]), jnp.sin(angle_u[1]), jnp.cos(angle_u[1])], axis=-1)
-    tile = jnp.arange(chunks, dtype=jnp.int32)[:, None] * bands + band
+    tile = jnp.arange(chunks * TILES, dtype=jnp.int32)[:, None] * bands + band
     lane = jnp.arange(MINOR, dtype=jnp.int32)[None, :]
     first_tile = jnp.where(lane < MINOR // 2, MAJOR * lane, HALF + MAJOR * (lane - MINOR // 2))
     position_v = jnp.where(tile == 0, first_tile, tile + MAJOR * lane)
     angle_v = math.pi * coefficient[:, None, None] * folded_square(position_v, LENGTH)
     along_v = jnp.stack([jnp.sin(angle_v[0]), jnp.cos(angle_v[0]), jnp.sin(angle_v[1]), jnp.cos(angle_v[1])], axis=1)
 
+    rows_to = LENGTH // (halves * bands * projections)
     received = []
     for chunk in range(chunks):
         blocks = []
         for offset in range(bands):
-            pairs = [(source, source ^ offset) for source in range(bands)]
-            if chunk == 0:
-                sources = [first[offset] for first in firsts]
-            else:
-                sources = [others[(chunk - 1) * bands + offset]]
-            for block in sources:
-                blocks.append(lax.ppermute(block, "band", pairs) if offset else block)
+            block = spectra[chunk * bands + offset]
+            if offset:
+                block = lax.ppermute(block, "inner", [(source, source ^ offset) for source in range(bands)])
+            blocks.append(block)
         nyquist = None
         if chunk == 0:
-            sent = jnp.stack([block[:, 2 * MINOR :: MINOR] for block in blocks]).astype(F32)
-            sent = sent.reshape(bands, rows, 2)[jnp.arange(bands, dtype=jnp.int32) ^ band]
-            nyquist = nyquist_column(sent[:, :, 0], sent[:, :, 1], coefficient)
-        blocks = [block.reshape(-1, MINOR, 4 * MINOR) for block in blocks]
-        phase = columns(blocks, here, along_u, along_v[chunk], nyquist, bands, len(blocks) // bands)
-        rows_to = LENGTH // (bands * projections)
-        phase = phase.reshape(bands * projections, rows_to, 2 * MINOR)
-        back = lax.all_to_all(phase, ("band", "proj"), split_axis=0, concat_axis=0, tiled=True)
-        received.append(back.reshape(bands, projections, rows_to, 2 * MINOR))
+            sent = jnp.stack([block[:, 2 * MINOR : 4 * MINOR : MINOR] for block in blocks]).astype(F32)
+            sent = sent[jnp.arange(bands, dtype=jnp.int32) ^ band].reshape(bands * rows, 2)
+            sent = jnp.pad(sent, ((0, bands * rows), (0, 0)))
+            nyquist = nyquist_column(sent[:, 0], sent[:, 1], coefficient)
+        blocks = [block.reshape(-1, MINOR, TILES * 4 * MINOR) for block in blocks]
+        near, far = columns(blocks, here, along_u, along_v[chunk * TILES : (chunk + 1) * TILES], nyquist)
+        from_other = lax.ppermute(far, "half", [(0, 1), (1, 0)])
+        phase = (near + from_other.astype(F32)).astype(BF16)
+        phase = phase.reshape(bands * projections, rows_to, TILES * 2 * MINOR)
+        back = lax.all_to_all(phase, ("inner", "proj"), split_axis=0, concat_axis=0, tiled=True)
+        received.append(back.reshape(bands, projections, rows_to, TILES * 2 * MINOR))
 
     return rows_inverse(received, proj_order, bands)
 
 
 def solution(mesh):
-    in_specs = (P("proj", None, "band", None), P("proj", None), P(), P())
-    out_specs = P(("band", "proj"), None, None)
+    proj, band = mesh.devices.shape
+    split = jax.sharding.Mesh(mesh.devices.reshape(proj, 2, band // 2), ("proj", "half", "inner"))
+    in_specs = (P("proj", None, ("half", "inner"), None), P("proj", None), P(), P())
+    out_specs = P(("half", "inner", "proj"), None, None)
     return jax.shard_map(
-        on_device, mesh=mesh, in_specs=in_specs, out_specs=out_specs, check_vma=False
+        on_device, mesh=split, in_specs=in_specs, out_specs=out_specs, check_vma=False
     )

time: 421 us -> 483 us (1.15)
  Pallas kernels: 156 us -> 185 us
  waiting for transfers between devices: 199 us -> 222 us
  other arithmetic: 6.99 us -> 24.5 us
    ppermute x15 -> x8, waiting for transfers between devices: 74.3 us -> 181 us  [the longest x4 180 us: on_device(): from_other = lax.ppermute(far, 'half', [(0, 1), (1, 0)])]
    all_to_all x4, waiting for transfers between devices: 125 us -> 41.2 us  [on_device(): lax.all_to_all(phase, ('inner', 'proj'), split_axis=0, concat_axis=0, til...]
    pallas_call x6 -> x5, Pallas kernels: 125 us -> 154 us  [the longest x4 116 us: columns(): pl.pallas_call(functools.partial(column_kernel, special, bands), in_specs...]
    convert_element_type x0 -> x5, other arithmetic: none -> 17.4 us  [the longest x4 17.4 us: on_device(): phase = (near + from_other.astype(F32)).astype(BF16)]
    ppermute x15 -> x8, starting transfers between devices: 11.2 us -> 2.74 us  [the longest x4 2.15 us: on_device(): from_other = lax.ppermute(far, 'half', [(0, 1), (1, 0)])]
    slice x9 -> x4, local copies, waits for them, and re-layouts: 10.2 us -> 7.11 us  [the longest x2 6.45 us: on_device(): block[:, 2 * MINOR:4 * MINOR:MINOR]]
  transfers between devices with their start and end apart: 19 -> 12, of which waited for: 10 -> 6; matrix products, arithmetic and copies ran while one was open for 6% -> 8% of each run, Pallas kernels for 20% -> 18%
where the time goes in v4:
time: 483 us; the launch traced here: 482 us
  waiting for transfers between devices  222 us (46%)
  Pallas kernels  185 us (38%)
  starting transfers between devices  26.2 us (5%)
  other arithmetic  24.5 us (5%)
  local copies, waits for them, and re-layouts  14.5 us (3%)
  blocking collectives  8.48 us (2%)
    ppermute x4, waiting for transfers between devices, on_device(): from_other = lax.ppermute(far, 'half', [(0, 1), (1, 0)])  180 us
    pallas_call x4, Pallas kernels, columns(): pl.pallas_call(functools.partial(column_kernel, special, bands), in_specs...  116 us
    all_to_all x4, waiting for transfers between devices, on_device(): lax.all_to_all(phase, ('inner', 'proj'), split_axis=0, concat_axis=0, til...  41.2 us
    pallas_call x1, Pallas kernels, rows_forward(): pl.pallas_call(functools.partial(row_kernel, chunks, bands), grid=(rows /...  38.4 us
    all_to_all x4, starting transfers between devices, on_device(): lax.all_to_all(phase, ('inner', 'proj'), split_axis=0, concat_axis=0, til...  23.5 us
    pallas_call x1, Pallas kernels, rows_inverse(): pl.pallas_call(functools.partial(final_kernel, chunks, bands), grid=(rows...  21.4 us
    convert_element_type x4, other arithmetic, on_device(): phase = (near + from_other.astype(F32)).astype(BF16)  17.4 us
  transfers between devices with their start and end apart: 12, of which 6 were waited for; matrix products, arithmetic and copies ran while one was open for 8% of the time, Pallas kernels for 18%

profile of v4, /device:TPU:0, one launch (start us, length us, event | category | flops | bytes accessed | tf_op | source)
XLA Modules:
  0.0 482.4 jit_solution(15595925886311536959)
XLA Ops:
  0.0 9.3 %frame_sums.1 = f32[1,2]{1,0:T(1,128)} custom-call(bf16[1,2,1024,4096]{3,2,1,0:T(8,128)(2,1)} %x_ref.3), custom_call_target="tpu_custom_call" | custom-call | tf_op jit(solution)/shard_map/frame_sums/pallas_call | solution.py:188
  9.3 8.5 %psum.7 = f32[1,2]{1,0:T(1,128)S(1)} all-reduce(f32[1,2]{1,0:T(1,128)} %frame_sums.1), channel_id=1, replica_groups=mesh['proj'=8,'half'=2,'inner'=2] {'half','inner'}, use_global_device_ids=true, to_apply=%region_1.0 | all-reduce | flops 2 | bytes 16 | tf_op jit(solution)/shard_map/psum | solution.py:577
  17.8 0.6 broadcast_divide_fusion.scale_ref
  18.4 38.4 %rows_forward.1 = (bf16[1024,1024]{1,0:T(8,128)(2,1)}, bf16[1024,1024]{1,0:T(8,128)(2,1)}, bf16[1024,1024]{1,0:T(8,128)(2,1)}, bf16[1024,1024]{1,0:T(8,128)(2,1)...) custom-call(s32[1]{0:T(128)} %bitcast.9.band_ref, ...), custom_call_target="tpu_custom_call" | custom-call | flops 876173328384 | bytes 42991616 | tf_op jit(solution)/shard_map/rows_forward/pallas_call | solution.py:287
  56.8 0.2 fusion.25
  57.3 2.1 copy.81.rest_2_
  59.6 0.6 fusion.33
  60.2 1.0 collective-permute-done.6
  61.2 1.3 copy-done.11
  62.5 28.9 %columns.7 = (f32[16,128,512]{2,1,0:T(8,128)}, bf16[16,128,512]{2,1,0:T(8,128)(2,1)}) custom-call(s32[1]{0:T(128)} %bitcast.9.band_ref, f32[2,4,128]{2,1,0:T(4,128)} %get-tuple-element.49.v_ref, bf16[8,128,1024]{2,1,0:T(8,128)(2,1)} %bitcast.91, bf16[8,128,1024]{2,1,0:T(8,128)(2,1)} %bitcast.87, f32[32,128,4]{2,1,0:T(8,128)} %copy.81.rest_2_, ...), custom_call_target="tpu_custom_call" | custom-call | flops 549755813888 | bytes 31457280 | tf_op jit(solution)/shard_map/columns/pallas_call | solution.py:446
  91.4 0.4 collective-permute-start.7
  91.9 47.5 %collective-permute-done.7 = bf16[16,128,512]{2,1,0:T(8,128)(2,1)S(1)} collective-permute-done((bf16[16,128,512]{2,1,0:T(8,128)(2,1)}, bf16[16,128,512]{2,1,0:T(8,128)(2,1)S(1)}, u32[]{:S(2)}, u32[]{:S(2)}) %collective-permute-start.7) | collective-permute-done | bytes 2097184 | tf_op jit(solution)/shard_map/ppermute | solution.py:614
  139.4 4.4 add_convert_fusion
  143.8 6.0 %all-to-all-start.3 = ((bf16[16,128,512]{2,1,0:T(8,128)(2,1)}), bf16[16,128,512]{2,1,0:T(8,128)(2,1)}, u32[]{:S(2)}, u32[]{:S(2)}) async-start(bf16[16,128,512]{2,1,0:T(8,128)(2,1)} %add_convert_fusion), calls=%async_computation.3 | async-start | bytes 4194304 | tf_op jit(solution)/shard_map/all_to_all | solution.py:617
  149.8 29.0 %columns.6 = (f32[16,128,512]{2,1,0:T(8,128)}, bf16[16,128,512]{2,1,0:T(8,128)(2,1)}) custom-call(s32[1]{0:T(128)} %bitcast.9.band_ref, f32[2,4,128]{2,1,0:T(4,128)} %get-tuple-element.50.v_ref, bf16[8,128,1024]{2,1,0:T(8,128)(2,1)} %bitcast.90, bf16[8,128,1024]{2,1,0:T(8,128)(2,1)} %bitcast.48.rest_1_, f32[32,128,4]{2,1,0:T(8,128)} %copy.81.rest_2_, ...), custom_call_target="tpu_custom_call" | custom-call | flops 549755813888 | bytes 31457280 | tf_op jit(solution)/shard_map/columns/pallas_call | solution.py:446
  178.8 0.6 collective-permute-start.5
  179.4 0.4 collective-permute-start
  179.8 47.1 %collective-permute-done.5 = bf16[16,128,512]{2,1,0:T(8,128)(2,1)S(1)} collective-permute-done((bf16[16,128,512]{2,1,0:T(8,128)(2,1)}, bf16[16,128,512]{2,1,0:T(8,128)(2,1)S(1)}, u32[]{:S(2)}, u32[]{:S(2)}) %collective-permute-start.5) | collective-permute-done | bytes 2097184 | tf_op jit(solution)/shard_map/ppermute | solution.py:614
  226.9 4.4 add_convert_fusion.1
  231.3 5.8 %all-to-all-start.2 = ((bf16[16,128,512]{2,1,0:T(8,128)(2,1)}), bf16[16,128,512]{2,1,0:T(8,128)(2,1)}, u32[]{:S(2)}, u32[]{:S(2)}) async-start(bf16[16,128,512]{2,1,0:T(8,128)(2,1)} %add_convert_fusion.1), calls=%async_computation.2 | async-start | bytes 4194304 | tf_op jit(solution)/shard_map/all_to_all | solution.py:617
  237.1 28.8 %columns.5 = (f32[16,128,512]{2,1,0:T(8,128)}, bf16[16,128,512]{2,1,0:T(8,128)(2,1)}) custom-call(s32[1]{0:T(128)} %bitcast.9.band_ref, f32[2,4,128]{2,1,0:T(4,128)} %get-tuple-element.51.v_ref, bf16[8,128,1024]{2,1,0:T(8,128)(2,1)} %bitcast.89, bf16[8,128,1024]{2,1,0:T(8,128)(2,1)} %bitcast.45.rest_1_, f32[32,128,4]{2,1,0:T(8,128)} %copy.81.rest_2_, ...), custom_call_target="tpu_custom_call" | custom-call | flops 549755813888 | bytes 31457280 | tf_op jit(solution)/shard_map/columns/pallas_call | solution.py:446
  265.9 0.6 collective-permute-start.3
  266.5 3.2 slice.82
  269.7 0.1 copy.77
  269.9 0.3 multiply_sine_fusion
  270.2 3.2 slice.83
  273.5 0.1 copy.78
  273.7 0.6 gather_fusion
  274.4 0.3 convolution_bitcast_fusion.2
  274.8 0.3 convolution_bitcast_fusion.1
  275.1 0.3 convolution_bitcast_fusion
  275.4 0.2 convolution_bitcast_fusion.3
  275.8 0.7 copy.80
  276.5 37.6 %collective-permute-done.3 = bf16[16,128,512]{2,1,0:T(8,128)(2,1)S(1)} collective-permute-done((bf16[16,128,512]{2,1,0:T(8,128)(2,1)}, bf16[16,128,512]{2,1,0:T(8,128)(2,1)S(1)}, u32[]{:S(2)}, u32[]{:S(2)}) %collective-permute-start.3) | collective-permute-done | bytes 2097184 | tf_op jit(solution)/shard_map/ppermute | solution.py:614
  314.1 4.3 add_convert_fusion.2
  318.4 5.8 %all-to-all-start.1 = ((bf16[16,128,512]{2,1,0:T(8,128)(2,1)}), bf16[16,128,512]{2,1,0:T(8,128)(2,1)}, u32[]{:S(2)}, u32[]{:S(2)}) async-start(bf16[16,128,512]{2,1,0:T(8,128)(2,1)} %add_convert_fusion.2), calls=%async_computation.1 | async-start | bytes 4194304 | tf_op jit(solution)/shard_map/all_to_all | solution.py:617
  324.2 29.4 %columns.4 = (f32[16,128,512]{2,1,0:T(8,128)}, bf16[16,128,512]{2,1,0:T(8,128)(2,1)}) custom-call(s32[1]{0:T(128)} %bitcast.9.band_ref, f32[2,4,128]{2,1,0:T(4,128)} %get-tuple-element.52.v_ref, bf16[8,128,1024]{2,1,0:T(8,128)(2,1)} %bitcast.81, bf16[8,128,1024]{2,1,0:T(8,128)(2,1)} %bitcast.19.rest_1_, f32[32,128,4]{2,1,0:T(8,128)} %copy.81.rest_2_, ...), custom_call_target="tpu_custom_call" | custom-call | flops 549755813888 | bytes 31457280 | tf_op jit(solution)/shard_map/columns/pallas_call | solution.py:446
  353.6 0.6 collective-permute-start.1
  354.2 47.6 %collective-permute-done.1 = bf16[16,128,512]{2,1,0:T(8,128)(2,1)S(1)} collective-permute-done((bf16[16,128,512]{2,1,0:T(8,128)(2,1)}, bf16[16,128,512]{2,1,0:T(8,128)(2,1)S(1)}, u32[]{:S(2)}, u32[]{:S(2)}) %collective-permute-start.1) | collective-permute-done | bytes 2097184 | tf_op jit(solution)/shard_map/ppermute | solution.py:614
  401.8 4.4 add_convert_fusion.3
  406.2 5.9 %all-to-all-start = ((bf16[16,128,512]{2,1,0:T(8,128)(2,1)}), bf16[16,128,512]{2,1,0:T(8,128)(2,1)S(1)}, u32[]{:S(2)}, u32[]{:S(2)}) async-start(bf16[16,128,512]{2,1,0:T(8,128)(2,1)} %add_convert_fusion.3), calls=%async_computation | async-start | bytes 4194304 | tf_op jit(solution)/shard_map/all_to_all | solution.py:617
  412.1 0.7 fusion.34
  412.8 4.3 compare_select_fusion.1
  417.1 0.7 fusion.24
  417.7 0.7 fusion.place_ref
  418.4 41.2 %all-to-all-done = bf16[16,128,512]{2,1,0:T(8,128)(2,1)S(1)} async-done(((bf16[16,128,512]{2,1,0:T(8,128)(2,1)}), bf16[16,128,512]{2,1,0:T(8,128)(2,1)S(1)}, u32[]{:S(2)}, u32[]{:S(2)}) %all-to-all-start) | async-done | bytes 2097184 | tf_op jit(solution)/shard_map/all_to_all | solution.py:617
  459.6 1.3 copy-done
  460.9 21.4 %rows_inverse.1 = f32[1024,4096]{1,0:T(8,128)} custom-call(bf16[256,256]{1,0:T(8,128)(2,1)} %fusion.place_ref, bf16[2,8,128,512]{3,2,1,0:T(8,128)(2,1)} %bitcast.77, bf16[2,8,128,512]{3,2,1,0:T(8,128)(2,1)} %bitcast.46.rest_1_, bf16[2,8,128,512]{3,2,1,0:T(8,128)(2,1)} %bitcast.49.rest_2_, bf16[2,8,128,512]{3,2,1,0:T(8,128)(2,1)} %bitcast.52.rest_3_, ...), custom_call_target="tpu_custom_call" | custom-call | flops 10737418240 | bytes 33554432 | tf_op jit(solution)/shard_map/rows_inverse/pallas_call | solution.py:506
  (60 shorter events, 1.1 us)
Async XLA Ops:
  18.4 38.5 %copy-start.12 = (f32[8]{0:T(128)S(1)}, f32[8]{0:T(128)}, u32[]{:S(2)}) copy-start(f32[8]{0:T(128)} %param.20) | copy-start | bytes 100
  18.4 38.5 %copy-start.13 = (s32[1,2]{1,0:T(1,128)S(1)}, s32[1,2]{1,0:T(1,128)}, u32[]{:S(2)}) copy-start(s32[1,2]{1,0:T(1,128)} %param.19) | copy-start | bytes 28
  56.7 4.4 collective-permute-start.6
  57.0 34.4 %copy-start.7 = (f32[2]{0:T(128)}, f32[2]{0:T(128)S(1)}, u32[]{:S(2)}) copy-start(f32[2]{0:T(128)S(1)} %broadcast_multiply_fusion.2) | copy-start | bytes 28
  61.2 1.3 copy-start.11
  62.5 29.4 %copy-start.10 = (bf16[1024,1024]{1,0:T(8,128)(2,1)S(1)}, bf16[1024,1024]{1,0:T(8,128)(2,1)}, u32[]{:S(2)}) copy-start(bf16[1024,1024]{1,0:T(8,128)(2,1)} %get-tuple-element.30) | copy-start | bytes 6291460
  91.4 48.0 %collective-permute-start.7 = (bf16[16,128,512]{2,1,0:T(8,128)(2,1)}, bf16[16,128,512]{2,1,0:T(8,128)(2,1)S(1)}, u32[]{:S(2)}, u32[]{:S(2)}) collective-permute-start(bf16[16,128,512]{2,1,0:T(8,128)(2,1)} %get-tuple-element.36), channel_id=1, source_target_pairs={{0,2},{2,0},{1,3},{3,1},{4,6},{6,4},{5,7},{7,5},{8,10},{10,8},{9,1... | collective-permute-start | bytes 6291464 | tf_op jit(solution)/shard_map/ppermute | solution.py:614
  91.9 57.9 %collective-permute-start.4 = (bf16[1024,1024]{1,0:T(8,128)(2,1)S(1)}, bf16[1024,1024]{1,0:T(8,128)(2,1)}, u32[]{:S(2)}, u32[]{:S(2)}) collective-permute-start(bf16[1024,1024]{1,0:T(8,128)(2,1)S(1)} %copy-done.10), channel_id=1, source_target_pairs={{0,1},{1,0},{2,3},{3,2},{4,5},{5,4},{6,7},{7,6},{8,9},{9,8},{10,11... | collective-permute-start | bytes 6291464 | tf_op jit(solution)/shard_map/ppermute | solution.py:604
  143.8 87.5 %all-to-all-start.3 = ((bf16[16,128,512]{2,1,0:T(8,128)(2,1)}), bf16[16,128,512]{2,1,0:T(8,128)(2,1)}, u32[]{:S(2)}, u32[]{:S(2)}) async-start(bf16[16,128,512]{2,1,0:T(8,128)(2,1)} %add_convert_fusion), calls=%async_computation.3 | async-start | bytes 4194304 | tf_op jit(solution)/shard_map/all_to_all | solution.py:617
  149.8 29.5 %copy-start.9 = (bf16[1024,1024]{1,0:T(8,128)(2,1)S(1)}, bf16[1024,1024]{1,0:T(8,128)(2,1)}, u32[]{:S(2)}) copy-start(bf16[1024,1024]{1,0:T(8,128)(2,1)} %get-tuple-element.26) | copy-start | bytes 6291460
  178.8 48.2 %collective-permute-start.5 = (bf16[16,128,512]{2,1,0:T(8,128)(2,1)}, bf16[16,128,512]{2,1,0:T(8,128)(2,1)S(1)}, u32[]{:S(2)}, u32[]{:S(2)}) collective-permute-start(bf16[16,128,512]{2,1,0:T(8,128)(2,1)} %get-tuple-element.32), channel_id=1, source_target_pairs={{0,2},{2,0},{1,3},{3,1},{4,6},{6,4},{5,7},{7,5},{8,10},{10,8},{9,1... | collective-permute-start | bytes 6291464 | tf_op jit(solution)/shard_map/ppermute | solution.py:614
  179.3 57.8 %collective-permute-start.2 = (bf16[1024,1024]{1,0:T(8,128)(2,1)S(1)}, bf16[1024,1024]{1,0:T(8,128)(2,1)}, u32[]{:S(2)}, u32[]{:S(2)}) collective-permute-start(bf16[1024,1024]{1,0:T(8,128)(2,1)S(1)} %copy-done.9), channel_id=1, source_target_pairs={{0,1},{1,0},{2,3},{3,2},{4,5},{5,4},{6,7},{7,6},{8,9},{9,8},{10,11... | collective-permute-start | bytes 6291464 | tf_op jit(solution)/shard_map/ppermute | solution.py:604
  179.4 90.8 %collective-permute-start = (bf16[1024,1024]{1,0:T(8,128)(2,1)}, bf16[1024,1024]{1,0:T(8,128)(2,1)}, u32[]{:S(2)}, u32[]{:S(2)}) collective-permute-start(bf16[1024,1024]{1,0:T(8,128)(2,1)} %get-tuple-element.22), channel_id=1, source_target_pairs={{0,1},{1,0},{2,3},{3,2},{4,5},{5,4},{6,7},{7,6},{8,9},{9,8},{10,11... | collective-permute-start | bytes 6291464 | tf_op jit(solution)/shard_map/ppermute | solution.py:604
  231.3 87.1 %all-to-all-start.2 = ((bf16[16,128,512]{2,1,0:T(8,128)(2,1)}), bf16[16,128,512]{2,1,0:T(8,128)(2,1)}, u32[]{:S(2)}, u32[]{:S(2)}) async-start(bf16[16,128,512]{2,1,0:T(8,128)(2,1)} %add_convert_fusion.1), calls=%async_computation.2 | async-start | bytes 4194304 | tf_op jit(solution)/shard_map/all_to_all | solution.py:617
  237.1 32.8 %copy-start.8 = (f32[2]{0:T(128)S(1)}, f32[2]{0:T(128)}, u32[]{:S(2)}) copy-start(f32[2]{0:T(128)} %copy-done.7) | copy-start | bytes 28
  265.9 8.5 %copy-start.1 = (f32[2,64,2,64]{1,3,0,2:T(8,128)S(1)}, f32[2,64,2,64]{1,3,0,2:T(8,128)}, u32[]{:S(2)}) copy-start(f32[2,64,2,64]{1,3,0,2:T(8,128)} %constant.108.clone) | copy-start | bytes 196612
  265.9 48.2 %collective-permute-start.3 = (bf16[16,128,512]{2,1,0:T(8,128)(2,1)}, bf16[16,128,512]{2,1,0:T(8,128)(2,1)S(1)}, u32[]{:S(2)}, u32[]{:S(2)}) collective-permute-start(bf16[16,128,512]{2,1,0:T(8,128)(2,1)} %get-tuple-element.28), channel_id=1, source_target_pairs={{0,2},{2,0},{1,3},{3,1},{4,6},{6,4},{5,7},{7,5},{8,10},{10,8},{9,1... | collective-permute-start | bytes 6291464 | tf_op jit(solution)/shard_map/ppermute | solution.py:614
  266.5 8.2 %copy-start.3 = (f32[1,64,64]{2,1,0:T(8,128)S(1)}, f32[1,64,64]{2,1,0:T(8,128)}, u32[]{:S(2)}) copy-start(f32[1,64,64]{2,1,0:T(8,128)} %constant.123) | copy-start | bytes 49156
  266.5 8.3 %copy-start.4 = (f32[1,64,64]{2,1,0:T(8,128)S(1)}, f32[1,64,64]{2,1,0:T(8,128)}, u32[]{:S(2)}) copy-start(f32[1,64,64]{2,1,0:T(8,128)} %constant.124) | copy-start | bytes 49156
  269.9 5.3 %copy-start.2 = (f32[2,64,2,64]{3,1,0,2:T(8,128)S(1)}, f32[2,64,2,64]{3,1,0,2:T(8,128)}, u32[]{:S(2)}) copy-start(f32[2,64,2,64]{3,1,0,2:T(8,128)} %constant.111.clone) | copy-start | bytes 196612
  270.2 5.2 %copy-start.5 = (f32[2,64,64]{1,2,0:T(8,128)S(1)}, f32[2,64,64]{1,2,0:T(8,128)}, u32[]{:S(2)}) copy-start(f32[2,64,64]{1,2,0:T(8,128)} %constant.112.clone) | copy-start | bytes 98308
  318.4 87.8 %all-to-all-start.1 = ((bf16[16,128,512]{2,1,0:T(8,128)(2,1)}), bf16[16,128,512]{2,1,0:T(8,128)(2,1)}, u32[]{:S(2)}, u32[]{:S(2)}) async-start(bf16[16,128,512]{2,1,0:T(8,128)(2,1)} %add_convert_fusion.2), calls=%async_computation.1 | async-start | bytes 4194304 | tf_op jit(solution)/shard_map/all_to_all | solution.py:617
  353.6 48.2 %collective-permute-start.1 = (bf16[16,128,512]{2,1,0:T(8,128)(2,1)}, bf16[16,128,512]{2,1,0:T(8,128)(2,1)S(1)}, u32[]{:S(2)}, u32[]{:S(2)}) collective-permute-start(bf16[16,128,512]{2,1,0:T(8,128)(2,1)} %get-tuple-element.24), channel_id=1, source_target_pairs={{0,2},{2,0},{1,3},{3,1},{4,6},{6,4},{5,7},{7,5},{8,10},{10,8},{9,1... | collective-permute-start | bytes 6291464 | tf_op jit(solution)/shard_map/ppermute | solution.py:614
  406.2 5.9 %copy-start.6 = (s32[8]{0:T(128)S(1)}, s32[8]{0:T(128)}, u32[]{:S(2)}) copy-start(s32[8]{0:T(128)} %param.21) | copy-start | bytes 100
  406.2 53.5 %all-to-all-start = ((bf16[16,128,512]{2,1,0:T(8,128)(2,1)}), bf16[16,128,512]{2,1,0:T(8,128)(2,1)S(1)}, u32[]{:S(2)}, u32[]{:S(2)}) async-start(bf16[16,128,512]{2,1,0:T(8,128)(2,1)} %add_convert_fusion.3), calls=%async_computation | async-start | bytes 4194304 | tf_op jit(solution)/shard_map/all_to_all | solution.py:617
  459.6 1.3 copy-start

commit v5 on v4

--- a/solution.py
+++ b/solution.py
@@ -14,7 +14,6 @@
 MAJOR = 32
 MINOR = 128
 HALF = MAJOR // 2
-TILES = 2
 F32 = jnp.float32
 BF16 = jnp.bfloat16
 MIB = 1 << 20
@@ -197,9 +196,9 @@
     )(intensities)
 
 
-def row_kernel(chunks, bands, band_ref, scale_ref, x_ref, high_hbm, low_hbm, *rest):
-    outs = rest[: chunks * bands]
-    mid_ref, xs_ref, high_ref, low_ref, sems = rest[chunks * bands :]
+def row_kernel(plan, bands, band_ref, scale_ref, x_ref, high_hbm, low_hbm, *rest):
+    outs = rest[: len(plan) * bands]
+    mid_ref, xs_ref, high_ref, low_ref, sems = rest[len(plan) * bands :]
     rows_here = x_ref.shape[2]
     band = band_ref[0]
     scale_even, scale_odd = scale_ref[0, 0], scale_ref[0, 1]
@@ -248,22 +247,34 @@
         return dot(whole, jnp.concatenate([high, high, low_ref[table]], axis=0))
 
     width = 2 * MINOR
-    for chunk in range(chunks):
-        for place in range(TILES):
+    for chunk, slots in enumerate(plan):
+        for place, slot in enumerate(slots):
             start = 2 * width * place
             for offset in range(bands):
-                t = (chunk * TILES + place) * bands + (band ^ offset)
+                t = slot * bands + (band ^ offset)
                 out_ref = outs[chunk * bands + offset]
                 out_ref[:, start : start + width] = apply(t, 2 * t).astype(BF16)
                 out_ref[:, start + width : start + 2 * width] = apply(
                     lax.rem(MAJOR - t, MAJOR), 2 * t + 1
                 ).astype(BF16)
+    chunk = special_chunk(plan)
     for offset in range(bands):
 
         @pl.when(band == offset)
-        def _(offset=offset):
-            outs[offset][:, :width] = (apply(0, 0) + apply(HALF, 32)).astype(BF16)
-            outs[offset][:, width : 2 * width] = (apply(0, 1) + apply(HALF, 33)).astype(BF16)
+        def _(out_ref=outs[chunk * bands + offset]):
+            out_ref[:, :width] = (apply(0, 0) + apply(HALF, 32)).astype(BF16)
+            out_ref[:, width : 2 * width] = (apply(0, 1) + apply(HALF, 33)).astype(BF16)
+
+
+def chunk_plan(count):
+    if count < 4:
+        return [[slot] for slot in range(1, count)] + [[0]]
+    order = [1, 2, 3, 0] + list(range(4, count))
+    return [order[:1]] + [order[i : i + 2] for i in range(1, count - 1, 2)] + [order[count - 1 :]]
+
+
+def special_chunk(plan):
+    return next(chunk for chunk, slots in enumerate(plan) if slots[0] == 0)
 
 
 def whole_spec():
@@ -278,14 +289,13 @@
     return pl.BlockSpec(shape, lambda *_: (0,) * len(shape), pipeline_mode=pl.Buffered(1))
 
 
-def rows_forward(intensities, scale, band, bands, chunks):
+def rows_forward(intensities, scale, band, bands, plan):
     rows = intensities.shape[2]
     block = min(256, rows)
     high, low = row_tables()
-    width = TILES * 4 * MINOR
-    count = chunks * bands
+    widths = [len(slots) * 4 * MINOR for slots in plan for _ in range(bands)]
     return pl.pallas_call(
-        functools.partial(row_kernel, chunks, bands),
+        functools.partial(row_kernel, plan, bands),
         grid=(rows // block,),
         in_specs=[
             pl.BlockSpec(memory_space=pltpu.SMEM),
@@ -294,8 +304,8 @@
             any_spec(),
             any_spec(),
         ],
-        out_specs=[pl.BlockSpec((block, width), lambda i: (i, 0))] * count,
-        out_shape=[jax.ShapeDtypeStruct((rows, width), BF16)] * count,
+        out_specs=[pl.BlockSpec((block, width), lambda i: (i, 0)) for width in widths],
+        out_shape=[jax.ShapeDtypeStruct((rows, width), BF16) for width in widths],
         scratch_shapes=[
             pltpu.VMEM((64, 16, MINOR), F32),
             pltpu.VMEM((MAJOR, block, 4 * MINOR), BF16),
@@ -311,10 +321,10 @@
     )(band, scale, intensities, jnp.asarray(high), jnp.asarray(low))
 
 
-def column_kernel(special, bands, band_ref, v_ref, *rest):
+def column_kernel(special, tiles, bands, waits, band_ref, v_ref, *rest):
     blocks = rest[:bands]
     u_hbm, *table_hbms = rest[bands : bands + 5]
-    rest = rest[bands + 5 :]
+    rest = rest[bands + 5 + waits :]
     band = band_ref[0]
     if special:
         nyquist_ref, *rest = rest
@@ -341,7 +351,7 @@
         start = pl.multiple_of(index * 16, 16)
         rows = pl.ds(start, 16)
         below = pl.ds(pl.multiple_of(start + MINOR, 16), 16)
-        for tile in range(TILES):
+        for tile in range(tiles):
             patch = special and tile == 0
 
             def load(a, tile=tile, patch=patch):
@@ -372,7 +382,7 @@
     for fetch in late:
         fetch.wait()
 
-    along_v = [[v_ref[tile, i : i + 1, :] for i in range(4)] for tile in range(TILES)]
+    along_v = [[v_ref[tile, i : i + 1, :] for i in range(4)] for tile in range(tiles)]
 
     def middle(k):
         values = xs_ref[k]
@@ -381,7 +391,7 @@
         column = u_ref[k]
         along_u = [column[:, i : i + 1] for i in range(4)]
         parts_re, parts_im = [], []
-        for tile in range(TILES):
+        for tile in range(tiles):
             sin_even = along_u[0] * along_v[tile][1] + along_u[1] * along_v[tile][0]
             sin_odd = along_u[2] * along_v[tile][3] + along_u[3] * along_v[tile][2]
             scale = 1.0 / (4.0 * (sin_even * sin_even + sin_odd * sin_odd) + 2.0 * alpha_reg)
@@ -408,7 +418,7 @@
         start = pl.multiple_of(index * 16, 16)
         rows = pl.ds(start, 16)
         below = pl.ds(pl.multiple_of(start + MINOR, 16), 16)
-        for tile in range(TILES):
+        for tile in range(tiles):
             lanes = slice(MINOR * tile, MINOR * (tile + 1))
             patch = special and tile == 0
 
@@ -433,48 +443,67 @@
     lax.fori_loop(0, MINOR // 16, inverse, 0)
 
 
-def columns(blocks, band, along_u, along_v, nyquist):
+def columns(blocks, band, along_u, along_v, nyquist, after):
+    tiles = along_v.shape[0]
     (fh, fl), (ih, il) = column_tables()
     special = nyquist is not None
     bands = len(blocks)
-    operands = [band, along_v, *blocks, along_u] + [jnp.asarray(t) for t in (fh, fl, ih, il)]
-    in_specs = [pl.BlockSpec(memory_space=pltpu.SMEM), whole_spec()] + [any_spec()] * (bands + 5)
+    operands = [band, along_v, *blocks, along_u] + [jnp.asarray(t) for t in (fh, fl, ih, il)] + after
+    in_specs = [pl.BlockSpec(memory_space=pltpu.SMEM), whole_spec()] + [any_spec()] * (bands + 5 + len(after))
     if special:
         operands.append(nyquist)
         in_specs.append(whole_spec())
-    shape = (HALF, MINOR, TILES * 2 * MINOR)
+    shape = (HALF, MINOR, tiles * 2 * MINOR)
     return pl.pallas_call(
-        functools.partial(column_kernel, special, bands),
+        functools.partial(column_kernel, special, tiles, bands, len(after)),
         in_specs=in_specs,
         out_specs=[whole_spec()] * 2,
         out_shape=[jax.ShapeDtypeStruct(shape, F32), jax.ShapeDtypeStruct(shape, BF16)],
         scratch_shapes=[
-            pltpu.VMEM((2 * TILES, 64, 16, MINOR), F32),
-            pltpu.VMEM((MAJOR, 2 * MINOR, TILES * 2 * MINOR), BF16),
-            pltpu.VMEM((MAJOR, 2 * MINOR, TILES * MINOR), F32),
-            pltpu.VMEM((HALF, MINOR, TILES * 4 * MINOR), BF16),
+            pltpu.VMEM((2 * tiles, 64, 16, MINOR), F32),
+            pltpu.VMEM((MAJOR, 2 * MINOR, tiles * 2 * MINOR), BF16),
+            pltpu.VMEM((MAJOR, 2 * MINOR, tiles * MINOR), F32),
+            pltpu.VMEM((HALF, MINOR, tiles * 4 * MINOR), BF16),
             pltpu.VMEM(along_u.shape, F32),
         ]
         + [pltpu.VMEM(fh.shape, BF16)] * 4
         + [pltpu.SemaphoreType.DMA((bands + 5,))],
         compiler_params=pltpu.CompilerParams(vmem_limit_bytes=58 * MIB),
         cost_estimate=pl.CostEstimate(
-            flops=128 * 32 * 8 * 256 * 256 * 256, bytes_accessed=30 * MIB, transcendentals=0
+            flops=tiles * 64 * 32 * 8 * 256 * 256 * 256, bytes_accessed=30 * MIB, transcendentals=0
         ),
         name="columns",
     )(*operands)
 
 
-def final_kernel(chunks, bands, place_ref, *rest):
-    ins, (high_ref, low_ref, out_ref, xs_ref, zs_ref) = rest[:chunks], rest[chunks:]
+def share_kernel(near_ref, far_ref, *rest):
+    rest[-1][...] = (near_ref[...] + far_ref[...].astype(F32)).astype(BF16)
+
+
+def add_shares(near, far, after):
+    block = (4,) + near.shape[1:]
+    spec = pl.BlockSpec(block, lambda i: (i, 0, 0))
+    return pl.pallas_call(
+        share_kernel,
+        grid=(near.shape[0] // 4,),
+        in_specs=[spec, spec] + [any_spec()] * len(after),
+        out_specs=spec,
+        out_shape=jax.ShapeDtypeStruct(near.shape, BF16),
+        compiler_params=pltpu.CompilerParams(vmem_limit_bytes=58 * MIB),
+        name="add_shares",
+    )(near, far, *after)
+
+
+def final_kernel(plan, bands, place_ref, *rest):
+    ins, (high_ref, low_ref, out_ref, xs_ref, zs_ref) = rest[: len(plan)], rest[len(plan) :]
     place = place_ref[...]
     count = place.shape[0]
     width = 2 * MINOR
-    for chunk in range(chunks):
-        for tile in range(TILES):
+    for chunk, slots in enumerate(plan):
+        for tile, slot in enumerate(slots):
             for band in range(bands):
                 values = ins[chunk][band, :, :, width * tile : width * (tile + 1)].reshape(count, width)
-                xs_ref[(chunk * TILES + tile) * bands + band] = dot(place, values).astype(BF16)
+                xs_ref[slot * bands + band] = dot(place, values).astype(BF16)
 
     for t in range(HALF):
         partner = (HALF - t) % HALF
@@ -494,9 +523,8 @@
     lax.fori_loop(0, count // 16, group, 0)
 
 
-def rows_inverse(received, proj_order, bands):
-    chunks = len(received)
-    _, projections, rows, width = received[0].shape
+def rows_inverse(received, proj_order, bands, plan):
+    _, projections, rows, _ = received[0].shape
     block = min(256 // projections, rows)
     count = block * projections
     high, low = final_tables()
@@ -504,10 +532,10 @@
     slot = proj_order[to // block]
     place = (to[:, None] == ((to % block) * projections + slot)[None, :]).astype(BF16)
     result = pl.pallas_call(
-        functools.partial(final_kernel, chunks, bands),
+        functools.partial(final_kernel, plan, bands),
         grid=(rows // block,),
         in_specs=[fixed_spec((count, count))]
-        + [pl.BlockSpec((bands, projections, block, width), lambda i: (0, 0, i, 0))] * chunks
+        + [pl.BlockSpec((bands, projections, block, each.shape[3]), lambda i: (0, 0, i, 0)) for each in received]
         + [fixed_spec(high.shape), fixed_spec(low.shape)],
         out_specs=pl.BlockSpec((count, LENGTH), lambda i: (i, 0)),
         out_shape=jax.ShapeDtypeStruct((rows * projections, LENGTH), F32),
@@ -573,12 +601,13 @@
     bands = lax.axis_size("inner")
     projections = lax.axis_size("proj")
     band = lax.axis_index("inner")
-    chunks = HALF // (bands * TILES)
+    slots = HALF // bands
+    plan = chunk_plan(slots)
     totals = lax.psum(frame_sums(intensities), ("half", "inner"))
     scale = (rows * bands * halves * LENGTH) / totals
 
     here = jnp.asarray(band, jnp.int32).reshape(1)
-    spectra = rows_forward(intensities, scale, here, bands, chunks)
+    spectra = rows_forward(intensities, scale, here, bands, plan)
 
     table_size = fresnel_table.shape[0]
     onehot = (dist_index[0][:, None] == jnp.arange(table_size, dtype=jnp.int32)[None, :]).astype(F32)
@@ -587,7 +616,7 @@
     s_index = lax.broadcasted_iota(jnp.int32, (MAJOR, MINOR), 1)
     angle_u = math.pi * coefficient[:, None, None] * folded_square(k_index + MAJOR * s_index, LENGTH)
     along_u = jnp.stack([jnp.sin(angle_u[0]), jnp.cos(angle_u[0]), jnp.sin(angle_u[1]), jnp.cos(angle_u[1])], axis=-1)
-    tile = jnp.arange(chunks * TILES, dtype=jnp.int32)[:, None] * bands + band
+    tile = jnp.asarray(sum(plan, []), jnp.int32)[:, None] * bands + band
     lane = jnp.arange(MINOR, dtype=jnp.int32)[None, :]
     first_tile = jnp.where(lane < MINOR // 2, MAJOR * lane, HALF + MAJOR * (lane - MINOR // 2))
     position_v = jnp.where(tile == 0, first_tile, tile + MAJOR * lane)
@@ -595,8 +624,8 @@
     along_v = jnp.stack([jnp.sin(angle_v[0]), jnp.cos(angle_v[0]), jnp.sin(angle_v[1]), jnp.cos(angle_v[1])], axis=1)
 
     rows_to = LENGTH // (halves * bands * projections)
-    received = []
-    for chunk in range(chunks):
+    phases, pending, after = [], [], []
+    for chunk, members in enumerate(plan):
         blocks = []
         for offset in range(bands):
             block = spectra[chunk * bands + offset]
@@ -604,20 +633,28 @@
                 block = lax.ppermute(block, "inner", [(source, source ^ offset) for source in range(bands)])
             blocks.append(block)
         nyquist = None
-        if chunk == 0:
+        if chunk == special_chunk(plan):
             sent = jnp.stack([block[:, 2 * MINOR : 4 * MINOR : MINOR] for block in blocks]).astype(F32)
             sent = sent[jnp.arange(bands, dtype=jnp.int32) ^ band].reshape(bands * rows, 2)
             sent = jnp.pad(sent, ((0, bands * rows), (0, 0)))
             nyquist = nyquist_column(sent[:, 0], sent[:, 1], coefficient)
-        blocks = [block.reshape(-1, MINOR, TILES * 4 * MINOR) for block in blocks]
-        near, far = columns(blocks, here, along_u, along_v[chunk * TILES : (chunk + 1) * TILES], nyquist)
-        from_other = lax.ppermute(far, "half", [(0, 1), (1, 0)])
-        phase = (near + from_other.astype(F32)).astype(BF16)
-        phase = phase.reshape(bands * projections, rows_to, TILES * 2 * MINOR)
+        width = len(members) * 4 * MINOR
+        start = sum(len(each) for each in plan[:chunk])
+        blocks = [block.reshape(-1, MINOR, width) for block in blocks]
+        near, far = columns(blocks, here, along_u, along_v[start : start + len(members)], nyquist, after)
+        if pending:
+            phases.append(add_shares(*pending.pop(), [far]))
+        pending.append((near, lax.ppermute(far, "half", [(0, 1), (1, 0)])))
+        after = [far] if chunk == 0 else [phases[-1]]
+    phases.append(add_shares(*pending.pop(), []))
+
+    received = []
+    for phase in phases:
+        phase = phase.reshape(bands * projections, rows_to, phase.shape[2])
         back = lax.all_to_all(phase, ("inner", "proj"), split_axis=0, concat_axis=0, tiled=True)
-        received.append(back.reshape(bands, projections, rows_to, TILES * 2 * MINOR))
-
-    return rows_inverse(received, proj_order, bands)
+        received.append(back.reshape(bands, projections, rows_to, phase.shape[2]))
+
+    return rows_inverse(received, proj_order, bands, plan)
 
 
 def solution(mesh):

time: 483 us -> 506 us (1.048)
  waiting for transfers between devices: 222 us -> 128 us
  blocking collectives: 8.48 us -> 94.6 us
  Pallas kernels: 185 us -> 229 us
  other arithmetic: 24.5 us -> 8.99 us
    ppermute x4 -> x5, waiting for transfers between devices: 180 us -> 87.3 us  [on_device(): pending.append((near, lax.ppermute(far, 'half', [(0, 1), (1, 0)])))]
    all_to_all x0 -> x2, blocking collectives: none -> 86.2 us  [on_device(): lax.all_to_all(phase, ('inner', 'proj'), split_axis=0, concat_axis=0, til...]
    pallas_call x6 -> x12, Pallas kernels: 176 us -> 219 us  [the longest x5 138 us: columns(): pl.pallas_call(functools.partial(column_kernel, special, tiles, bands, le...]
    convert_element_type x4 -> x0, other arithmetic: 17.4 us -> none  [on_device(): phase = (near + from_other.astype(F32)).astype(BF16)]
    all_to_all x4 -> x3, starting transfers between devices: 23.5 us -> 16.5 us  [on_device(): lax.all_to_all(phase, ('inner', 'proj'), split_axis=0, concat_axis=0, til...]
    all_to_all x4 -> x3, waiting for transfers between devices: 41.2 us -> 41.1 us  [on_device(): lax.all_to_all(phase, ('inner', 'proj'), split_axis=0, concat_axis=0, til...]
  transfers between devices with their start and end apart: 12 -> 13, of which waited for: 6 -> 5; matrix products, arithmetic and copies ran while one was open for 8% -> 5% of each run, Pallas kernels for 18% -> 32%
where the time goes in v5:
time: 506 us; the launch traced here: 504 us
  Pallas kernels  229 us (45%)
  waiting for transfers between devices  128 us (25%)
  blocking collectives  94.6 us (19%)
  starting transfers between devices  23.6 us (5%)
  local copies, waits for them, and re-layouts  18.6 us (4%)
  other arithmetic  8.99 us (2%)
    pallas_call x5, Pallas kernels, columns(): pl.pallas_call(functools.partial(column_kernel, special, tiles, bands, le...  138 us
    ppermute x5, waiting for transfers between devices, on_device(): pending.append((near, lax.ppermute(far, 'half', [(0, 1), (1, 0)])))  87.3 us
    all_to_all x2, blocking collectives, on_device(): lax.all_to_all(phase, ('inner', 'proj'), split_axis=0, concat_axis=0, til...  86.2 us
    all_to_all x3, waiting for transfers between devices, on_device(): lax.all_to_all(phase, ('inner', 'proj'), split_axis=0, concat_axis=0, til...  41.1 us
    pallas_call x1, Pallas kernels, rows_forward(): pl.pallas_call(functools.partial(row_kernel, plan, bands), grid=(rows //...  38.4 us
    pallas_call x5, Pallas kernels, add_shares(): pl.pallas_call(share_kernel, grid=(near.shape[0] // 4,), in_specs=[spec,...  21.5 us
    pallas_call x1, Pallas kernels, rows_inverse(): pl.pallas_call(functools.partial(final_kernel, plan, bands), grid=(rows /...  21.5 us
    all_to_all x3, starting transfers between devices, on_device(): lax.all_to_all(phase, ('inner', 'proj'), split_axis=0, concat_axis=0, til...  16.5 us
  transfers between devices with their start and end apart: 13, of which 5 were waited for; matrix products, arithmetic and copies ran while one was open for 5% of the time, Pallas kernels for 32%

profile of v5, /device:TPU:0, one launch (start us, length us, event | category | flops | bytes accessed | tf_op | source)
XLA Modules:
  0.0 504.5 jit_solution(586926276513242680)
XLA Ops:
  0.0 9.3 %frame_sums.1 = f32[1,2]{1,0:T(1,128)} custom-call(bf16[1,2,1024,4096]{3,2,1,0:T(8,128)(2,1)} %x_ref.3), custom_call_target="tpu_custom_call" | custom-call | tf_op jit(solution)/shard_map/frame_sums/pallas_call | solution.py:187
  9.3 8.5 %psum.7 = f32[1,2]{1,0:T(1,128)S(1)} all-reduce(f32[1,2]{1,0:T(1,128)} %frame_sums.1), channel_id=1, replica_groups=mesh['proj'=8,'half'=2,'inner'=2] {'half','inner'}, use_global_device_ids=true, to_apply=%region_1.0 | all-reduce | flops 2 | bytes 16 | tf_op jit(solution)/shard_map/psum | solution.py:606
  18.3 38.4 %rows_forward.1 = (bf16[1024,512]{1,0:T(8,128)(2,1)}, bf16[1024,512]{1,0:T(8,128)(2,1)}, bf16[1024,1024]{1,0:T(8,128)(2,1)}, bf16[1024,1024]{1,0:T(8,128)(2,1)},...) custom-call(s32[1]{0:T(128)} %bitcast.9.band_ref, ...), custom_call_target="tpu_custom_call" | custom-call | flops 876173328384 | bytes 42991616 | tf_op jit(solution)/shard_map/rows_forward/pallas_call | solution.py:297
  58.6 3.2 slice.87
  61.9 0.7 copy.81
  62.6 2.0 copy.79.rest_2_
  64.6 0.6 pad_clamp_fusion
  65.2 0.6 pad_maximum_fusion.2
  65.8 0.6 fusion.33
  66.5 0.9 multiply_sine_fusion
  67.4 1.0 copy-done.15
  68.4 25.4 %columns.5 = (f32[16,128,256]{2,1,0:T(8,128)}, bf16[16,128,256]{2,1,0:T(8,128)(2,1)}) custom-call(s32[1]{0:T(128)} %bitcast.9.band_ref, f32[1,4,128]{2,1,0:T(4,128)} %get-tuple-element.58.v_ref, bf16[8,128,512]{2,1,0:T(8,128)(2,1)} %bitcast.101, bf16[8,128,512]{2,1,0:T(8,128)(2,1)} %bitcast.96, f32[32,128,4]{2,1,0:T(8,128)} %copy.79.rest_2_, ...), custom_call_target="tpu_custom_call" | custom-call | flops 274877906944 | bytes 31457280 | tf_op jit(solution)/shard_map/columns/pallas_call | solution.py:457
  94.3 3.2 slice.88
  97.7 0.7 gather_fusion
  98.4 0.7 stack.58
  99.1 0.7 stack.59
  99.9 28.9 %columns.6 = (f32[16,128,512]{2,1,0:T(8,128)}, bf16[16,128,512]{2,1,0:T(8,128)(2,1)}) custom-call(s32[1]{0:T(128)} %bitcast.9.band_ref, f32[2,4,128]{2,1,0:T(4,128)} %get-tuple-element.61.v_ref, bf16[8,128,1024]{2,1,0:T(8,128)(2,1)} %bitcast.99, bf16[8,128,1024]{2,1,0:T(8,128)(2,1)} %bitcast.25.rest_1_, f32[32,128,4]{2,1,0:T(8,128)} %copy.79.rest_2_, ...), custom_call_target="tpu_custom_call" | custom-call | flops 549755813888 | bytes 31457280 | tf_op jit(solution)/shard_map/columns/pallas_call | solution.py:457
  130.2 0.7 copy.84
  130.9 1.7 collective-permute-start.3
  132.6 3.8 add_shares.5.rest_7_
  136.3 6.0 %all-to-all-start = ((bf16[16,128,256]{2,1,0:T(8,128)(2,1)}), bf16[16,128,256]{2,1,0:T(8,128)(2,1)}, u32[]{:S(2)}, u32[]{:S(2)}) async-start(bf16[16,128,256]{2,1,0:T(8,128)(2,1)} %add_shares.5.rest_7_), calls=%async_computation | async-start | bytes 2097152 | tf_op jit(solution)/shard_map/all_to_all | solution.py:654
  142.4 29.4 %columns.7 = (f32[16,128,512]{2,1,0:T(8,128)}, bf16[16,128,512]{2,1,0:T(8,128)(2,1)}) custom-call(s32[1]{0:T(128)} %bitcast.9.band_ref, f32[2,4,128]{2,1,0:T(4,128)} %get-tuple-element.60.v_ref, bf16[8,128,1024]{2,1,0:T(8,128)(2,1)} %bitcast.94, bf16[8,128,1024]{2,1,0:T(8,128)(2,1)} %bitcast.28.rest_1_, f32[32,128,4]{2,1,0:T(8,128)} %copy.79.rest_2_, ...), custom_call_target="tpu_custom_call" | custom-call | flops 549755813888 | bytes 31457280 | tf_op jit(solution)/shard_map/columns/pallas_call | solution.py:457
  171.8 0.6 collective-permute-start.5
  172.3 7.4 %collective-permute-done.3.far_ref = bf16[16,128,512]{2,1,0:T(8,128)(2,1)} collective-permute-done((bf16[16,128,512]{2,1,0:T(8,128)(2,1)}, bf16[16,128,512]{2,1,0:T(8,128)(2,1)}, u32[]{:S(2)}, u32[]{:S(2)}) %collective-permute-start.3) | collective-permute-done | bytes 2097184 | tf_op jit(solution)/shard_map/ppermute | solution.py:647
  179.7 4.7 add_shares.6.rest_7_
  184.3 28.8 %columns.8 = (f32[16,128,512]{2,1,0:T(8,128)}, bf16[16,128,512]{2,1,0:T(8,128)(2,1)}) custom-call(s32[1]{0:T(128)} %bitcast.9.band_ref, f32[2,4,128]{2,1,0:T(4,128)} %get-tuple-element.59.v_ref, bf16[8,128,1024]{2,1,0:T(8,128)(2,1)} %bitcast.98, bf16[8,128,1024]{2,1,0:T(8,128)(2,1)} %bitcast.50.rest_1_, f32[32,128,4]{2,1,0:T(8,128)} %copy.79.rest_2_, ...), custom_call_target="tpu_custom_call" | custom-call | flops 549755813888 | bytes 31457280 | tf_op jit(solution)/shard_map/columns/pallas_call | solution.py:457
  213.2 10.7 %collective-permute-done.5.far_ref = bf16[16,128,512]{2,1,0:T(8,128)(2,1)} collective-permute-done((bf16[16,128,512]{2,1,0:T(8,128)(2,1)}, bf16[16,128,512]{2,1,0:T(8,128)(2,1)}, u32[]{:S(2)}, u32[]{:S(2)}) %collective-permute-start.5) | collective-permute-done | bytes 2097184 | tf_op jit(solution)/shard_map/ppermute | solution.py:647
  223.9 4.7 add_shares.7.rest_7_
  228.5 25.5 %columns.9 = (f32[16,128,256]{2,1,0:T(8,128)}, bf16[16,128,256]{2,1,0:T(8,128)(2,1)}) custom-call(s32[1]{0:T(128)} %bitcast.9.band_ref, f32[1,4,128]{2,1,0:T(4,128)} %get-tuple-element.57.v_ref, bf16[8,128,512]{2,1,0:T(8,128)(2,1)} %bitcast.100, bf16[8,128,512]{2,1,0:T(8,128)(2,1)} %bitcast.53.rest_1_, f32[32,128,4]{2,1,0:T(8,128)} %copy.79.rest_2_, ...), custom_call_target="tpu_custom_call" | custom-call | flops 274877906944 | bytes 31457280 | tf_op jit(solution)/shard_map/columns/pallas_call | solution.py:457
  254.1 1.7 collective-permute-start.9
  255.8 22.9 %collective-permute-done.9.far_ref = bf16[16,128,256]{2,1,0:T(8,128)(2,1)S(1)} collective-permute-done((bf16[16,128,256]{2,1,0:T(8,128)(2,1)}, bf16[16,128,256]{2,1,0:T(8,128)(2,1)S(1)}, u32[]{:S(2)}, u32[]{:S(2)}) %collective-permute-start.9) | collective-permute-done | bytes 1048608 | tf_op jit(solution)/shard_map/ppermute | solution.py:647
  278.7 1.0 copy-done.4
  279.7 3.8 add_shares.9
  283.5 33.4 %all_to_all.25 = bf16[16,128,256]{2,1,0:T(8,128)(2,1)} all-to-all(bf16[16,128,256]{2,1,0:T(8,128)(2,1)} %add_shares.9), channel_id=1, replica_groups=mesh['proj'=8,'half'=2,'inner'=2] {'inner','proj'}, dimensions={0} | all-to-all | bytes 2097152 | tf_op jit(solution)/shard_map/all_to_all | solution.py:654
  316.9 52.8 %all_to_all.26 = bf16[16,128,512]{2,1,0:T(8,128)(2,1)} all-to-all(bf16[16,128,512]{2,1,0:T(8,128)(2,1)S(1)} %copy-done), channel_id=1, replica_groups=mesh['proj'=8,'half'=2,'inner'=2] {'inner','proj'}, dimensions={0} | all-to-all | bytes 4194304 | tf_op jit(solution)/shard_map/all_to_all | solution.py:654
  369.7 4.6 all-to-all-start.1
  374.2 1.6 collective-permute-start.7
  375.8 46.3 %collective-permute-done.7.far_ref = bf16[16,128,512]{2,1,0:T(8,128)(2,1)S(1)} collective-permute-done((bf16[16,128,512]{2,1,0:T(8,128)(2,1)S(1)}, bf16[16,128,512]{2,1,0:T(8,128)(2,1)S(1)}, u32[]{:S(2)}, u32[]{:S(2)}) %collective-permute-start.7) | collective-permute-done | bytes 2097184 | tf_op jit(solution)/shard_map/ppermute | solution.py:647
  422.1 1.4 copy-done.3
  423.5 4.6 add_shares.8
  428.2 5.9 %all-to-all-start.3 = ((bf16[16,128,512]{2,1,0:T(8,128)(2,1)}), bf16[16,128,512]{2,1,0:T(8,128)(2,1)S(1)}, u32[]{:S(2)}, u32[]{:S(2)}) async-start(bf16[16,128,512]{2,1,0:T(8,128)(2,1)} %add_shares.8), calls=%async_computation.3 | async-start | bytes 4194304 | tf_op jit(solution)/shard_map/all_to_all | solution.py:654
  434.1 0.7 fusion.34
  434.8 4.4 compare_select_fusion.1
  439.2 0.7 fusion.24
  439.9 0.7 fusion.place_ref
  440.6 41.1 %all-to-all-done.3 = bf16[16,128,512]{2,1,0:T(8,128)(2,1)S(1)} async-done(((bf16[16,128,512]{2,1,0:T(8,128)(2,1)}), bf16[16,128,512]{2,1,0:T(8,128)(2,1)S(1)}, u32[]{:S(2)}, u32[]{:S(2)}) %all-to-all-start.3) | async-done | bytes 2097184 | tf_op jit(solution)/shard_map/all_to_all | solution.py:654
  481.7 1.4 copy-done.2
  483.0 21.5 %rows_inverse.1 = f32[1024,4096]{1,0:T(8,128)} custom-call(bf16[256,256]{1,0:T(8,128)(2,1)} %fusion.place_ref, bf16[2,8,128,256]{3,2,1,0:T(8,128)(2,1)} %bitcast.26.rest_0_, bf16[2,8,128,512]{3,2,1,0:T(8,128)(2,1)} %bitcast.48.rest_1_, bf16[2,8,128,512]{3,2,1,0:T(8,128)(2,1)} %bitcast.80, bf16[2,8,128,512]{3,2,1,0:T(8,128)(2,1)} %bitcast.81, ...), custom_call_target="tpu_custom_call" | custom-call | flops 10737418240 | bytes 33554432 | tf_op jit(solution)/shard_map/rows_inverse/pallas_call | solution.py:534
  (77 shorter events, 4.4 us)
Async XLA Ops:
  18.3 39.6 %copy-start.18 = (s32[8]{0:T(128)S(1)}, s32[8]{0:T(128)}, u32[]{:S(2)}) copy-start(s32[8]{0:T(128)} %constant.126) | copy-start | bytes 100
  18.3 39.6 %copy-start.16 = (f32[8]{0:T(128)S(1)}, f32[8]{0:T(128)}, u32[]{:S(2)}) copy-start(f32[8]{0:T(128)} %param.21) | copy-start | bytes 100
  18.3 39.6 %copy-start.17 = (s32[1,2]{1,0:T(1,128)S(1)}, s32[1,2]{1,0:T(1,128)}, u32[]{:S(2)}) copy-start(s32[1,2]{1,0:T(1,128)} %param.20) | copy-start | bytes 28
  56.8 37.5 %collective-permute-start.4 = (bf16[1024,1024]{1,0:T(8,128)(2,1)}, bf16[1024,1024]{1,0:T(8,128)(2,1)}, u32[]{:S(2)}, u32[]{:S(2)}) collective-permute-start(bf16[1024,1024]{1,0:T(8,128)(2,1)} %get-tuple-element.34), channel_id=1, source_target_pairs={{0,1},{1,0},{2,3},{3,2},{4,5},{5,4},{6,7},{7,6},{8,9},{9,8},{10,11... | collective-permute-start | bytes 6291464 | tf_op jit(solution)/shard_map/ppermute | solution.py:633
  56.9 10.5 %collective-permute-start = (bf16[1024,512]{1,0:T(8,128)(2,1)}, bf16[1024,512]{1,0:T(8,128)(2,1)S(1)}, u32[]{:S(2)}, u32[]{:S(2)}) collective-permute-start(bf16[1024,512]{1,0:T(8,128)(2,1)} %get-tuple-element.26), channel_id=1, source_target_pairs={{0,1},{1,0},{2,3},{3,2},{4,5},{5,4},{6,7},{7,6},{8,9},{9,8},{10,11... | collective-permute-start | bytes 3145736 | tf_op jit(solution)/shard_map/ppermute | solution.py:633
  57.3 42.5 %collective-permute-start.2 = (bf16[1024,1024]{1,0:T(8,128)(2,1)}, bf16[1024,1024]{1,0:T(8,128)(2,1)}, u32[]{:S(2)}, u32[]{:S(2)}) collective-permute-start(bf16[1024,1024]{1,0:T(8,128)(2,1)} %get-tuple-element.30), channel_id=1, source_target_pairs={{0,1},{1,0},{2,3},{3,2},{4,5},{5,4},{6,7},{7,6},{8,9},{9,8},{10,11... | collective-permute-start | bytes 6291464 | tf_op jit(solution)/shard_map/ppermute | solution.py:633
  57.4 126.9 %collective-permute-start.6 = (bf16[1024,1024]{1,0:T(8,128)(2,1)}, bf16[1024,1024]{1,0:T(8,128)(2,1)}, u32[]{:S(2)}, u32[]{:S(2)}) collective-permute-start(bf16[1024,1024]{1,0:T(8,128)(2,1)} %get-tuple-element.38), channel_id=1, source_target_pairs={{0,1},{1,0},{2,3},{3,2},{4,5},{5,4},{6,7},{7,6},{8,9},{9,8},{10,11... | collective-permute-start | bytes 6291464 | tf_op jit(solution)/shard_map/ppermute | solution.py:633
  57.9 170.7 %collective-permute-start.8 = (bf16[1024,512]{1,0:T(8,128)(2,1)}, bf16[1024,512]{1,0:T(8,128)(2,1)}, u32[]{:S(2)}, u32[]{:S(2)}) collective-permute-start(bf16[1024,512]{1,0:T(8,128)(2,1)} %get-tuple-element.42), channel_id=1, source_target_pairs={{0,1},{1,0},{2,3},{3,2},{4,5},{5,4},{6,7},{7,6},{8,9},{9,8},{10,11... | collective-permute-start | bytes 3145736 | tf_op jit(solution)/shard_map/ppermute | solution.py:633
  67.4 1.0 copy-start.15
  68.4 29.2 %copy-start.14 = (bf16[1,1024,2]{1,2,0:T(2,128)(2,1)S(1)}, bf16[1,1024,2]{1,2,0:T(2,128)(2,1)}, u32[]{:S(2)}) copy-start(bf16[1,1024,2]{1,2,0:T(2,128)(2,1)} %copy.81) | copy-start | bytes 12292
  93.9 38.7 %collective-permute-start.1 = (bf16[16,128,256]{2,1,0:T(8,128)(2,1)}, bf16[16,128,256]{2,1,0:T(8,128)(2,1)}, u32[]{:S(2)}, u32[]{:S(2)}) collective-permute-start(bf16[16,128,256]{2,1,0:T(8,128)(2,1)} %get-tuple-element.28.rest_7_), channel_id=1, source_target_pairs={{0,2},{2,0},{1,3},{3,1},{4,6},{6,4},{5,7},{7,5},{8,10},{10,8},{9,1... | collective-permute-start | bytes 3145736 | tf_op jit(solution)/shard_map/ppermute | solution.py:647
  99.8 29.0 %copy-start.5 = (f32[2,64,2,64]{1,3,0,2:T(8,128)S(1)}, f32[2,64,2,64]{1,3,0,2:T(8,128)}, u32[]{:S(2)}) copy-start(f32[2,64,2,64]{1,3,0,2:T(8,128)} %constant.115.clone) | copy-start | bytes 196612
  99.8 29.0 %copy-start.10 = (f32[1,64,64]{2,1,0:T(8,128)S(1)}, f32[1,64,64]{2,1,0:T(8,128)}, u32[]{:S(2)}) copy-start(f32[1,64,64]{2,1,0:T(8,128)} %stack.58) | copy-start | bytes 49156
  99.8 29.0 %copy-start.11 = (f32[1,64,64]{2,1,0:T(8,128)S(1)}, f32[1,64,64]{2,1,0:T(8,128)}, u32[]{:S(2)}) copy-start(f32[1,64,64]{2,1,0:T(8,128)} %stack.59) | copy-start | bytes 49156
  99.8 29.3 %copy-start.8 = (f32[1,64,64]{2,1,0:T(8,128)S(1)}, f32[1,64,64]{2,1,0:T(8,128)}, u32[]{:S(2)}) copy-start(f32[1,64,64]{2,1,0:T(8,128)} %constant.127) | copy-start | bytes 49156
  99.8 29.3 %copy-start.9 = (f32[1,64,64]{2,1,0:T(8,128)S(1)}, f32[1,64,64]{2,1,0:T(8,128)}, u32[]{:S(2)}) copy-start(f32[1,64,64]{2,1,0:T(8,128)} %constant.128) | copy-start | bytes 49156
  99.9 29.7 %copy-start.6 = (f32[2,64,64]{2,1,0:T(8,128)S(1)}, f32[2,64,64]{2,1,0:T(8,128)}, u32[]{:S(2)}) copy-start(f32[2,64,64]{2,1,0:T(8,128)} %multiply_sine_fusion) | copy-start | bytes 98308
  99.9 29.7 %copy-start.7 = (f32[2,64,2,64]{3,1,0,2:T(8,128)S(1)}, f32[2,64,2,64]{3,1,0,2:T(8,128)}, u32[]{:S(2)}) copy-start(f32[2,64,2,64]{3,1,0,2:T(8,128)} %constant.118.clone) | copy-start | bytes 196612
  99.9 30.0 %copy-start.12 = (f32[2,64,64]{1,2,0:T(8,128)S(1)}, f32[2,64,64]{1,2,0:T(8,128)}, u32[]{:S(2)}) copy-start(f32[2,64,64]{1,2,0:T(8,128)} %constant.119.clone) | copy-start | bytes 98308
  130.9 48.8 %collective-permute-start.3 = (bf16[16,128,512]{2,1,0:T(8,128)(2,1)}, bf16[16,128,512]{2,1,0:T(8,128)(2,1)}, u32[]{:S(2)}, u32[]{:S(2)}) collective-permute-start(bf16[16,128,512]{2,1,0:T(8,128)(2,1)} %get-tuple-element.31.rest_0_), channel_id=1, source_target_pairs={{0,2},{2,0},{1,3},{3,1},{4,6},{6,4},{5,7},{7,5},{8,10},{10,8},{9,1... | collective-permute-start | bytes 6291464 | tf_op jit(solution)/shard_map/ppermute | solution.py:647
  136.3 147.2 %all-to-all-start = ((bf16[16,128,256]{2,1,0:T(8,128)(2,1)}), bf16[16,128,256]{2,1,0:T(8,128)(2,1)}, u32[]{:S(2)}, u32[]{:S(2)}) async-start(bf16[16,128,256]{2,1,0:T(8,128)(2,1)} %add_shares.5.rest_7_), calls=%async_computation | async-start | bytes 2097152 | tf_op jit(solution)/shard_map/all_to_all | solution.py:654
  171.8 52.1 %collective-permute-start.5 = (bf16[16,128,512]{2,1,0:T(8,128)(2,1)}, bf16[16,128,512]{2,1,0:T(8,128)(2,1)}, u32[]{:S(2)}, u32[]{:S(2)}) collective-permute-start(bf16[16,128,512]{2,1,0:T(8,128)(2,1)} %get-tuple-element.35.rest_0_), channel_id=1, source_target_pairs={{0,2},{2,0},{1,3},{3,1},{4,6},{6,4},{5,7},{7,5},{8,10},{10,8},{9,1... | collective-permute-start | bytes 6291464 | tf_op jit(solution)/shard_map/ppermute | solution.py:647
  254.1 24.7 %collective-permute-start.9 = (bf16[16,128,256]{2,1,0:T(8,128)(2,1)}, bf16[16,128,256]{2,1,0:T(8,128)(2,1)S(1)}, u32[]{:S(2)}, u32[]{:S(2)}) collective-permute-start(bf16[16,128,256]{2,1,0:T(8,128)(2,1)} %get-tuple-element.43.rest_0_), channel_id=1, source_target_pairs={{0,2},{2,0},{1,3},{3,1},{4,6},{6,4},{5,7},{7,5},{8,10},{10,8},{9,1... | collective-permute-start | bytes 3145736 | tf_op jit(solution)/shard_map/ppermute | solution.py:647
  278.7 1.0 copy-start.4
  283.5 33.4 %copy-start = (bf16[16,128,512]{2,1,0:T(8,128)(2,1)S(1)}, bf16[16,128,512]{2,1,0:T(8,128)(2,1)}, u32[]{:S(2)}) copy-start(bf16[16,128,512]{2,1,0:T(8,128)(2,1)} %add_shares.7.rest_7_) | copy-start | bytes 6291460
  369.7 4.6 copy-start.1
  369.7 58.5 %all-to-all-start.1 = ((bf16[16,128,512]{2,1,0:T(8,128)(2,1)}), bf16[16,128,512]{2,1,0:T(8,128)(2,1)}, u32[]{:S(2)}, u32[]{:S(2)}) async-start(bf16[16,128,512]{2,1,0:T(8,128)(2,1)} %add_shares.6.rest_7_), calls=%async_computation.1 | async-start | bytes 4194304 | tf_op jit(solution)/shard_map/all_to_all | solution.py:654
  374.2 47.9 %collective-permute-start.7 = (bf16[16,128,512]{2,1,0:T(8,128)(2,1)S(1)}, bf16[16,128,512]{2,1,0:T(8,128)(2,1)S(1)}, u32[]{:S(2)}, u32[]{:S(2)}) collective-permute-start(bf16[16,128,512]{2,1,0:T(8,128)(2,1)S(1)} %copy-done.1), channel_id=1, source_target_pairs={{0,2},{2,0},{1,3},{3,1},{4,6},{6,4},{5,7},{7,5},{8,10},{10,8},{9,1... | collective-permute-start | bytes 6291464 | tf_op jit(solution)/shard_map/ppermute | solution.py:647
  422.1 1.4 copy-start.3
  428.2 5.9 %copy-start.13 = (s32[8]{0:T(128)S(1)}, s32[8]{0:T(128)}, u32[]{:S(2)}) copy-start(s32[8]{0:T(128)} %param.22) | copy-start | bytes 100
  428.2 53.5 %all-to-all-start.3 = ((bf16[16,128,512]{2,1,0:T(8,128)(2,1)}), bf16[16,128,512]{2,1,0:T(8,128)(2,1)S(1)}, u32[]{:S(2)}, u32[]{:S(2)}) async-start(bf16[16,128,512]{2,1,0:T(8,128)(2,1)} %add_shares.8), calls=%async_computation.3 | async-start | bytes 4194304 | tf_op jit(solution)/shard_map/all_to_all | solution.py:654
  481.6 1.4 copy-start.2

commit v6 on v5

--- a/solution.py
+++ b/solution.py
@@ -172,8 +172,13 @@
 
     rows = x_ref.shape[2]
     for frame in range(2):
-        values = x_ref[0, frame].astype(F32).reshape(rows // 8, 8, LENGTH)
-        total_ref[frame] += jnp.sum(values, axis=0)
+        for start in range(0, LENGTH, 8 * MINOR):
+            lanes = slice(start, start + 8 * MINOR)
+            total = total_ref[frame, :, lanes]
+            for row in range(0, rows, 16):
+                values = x_ref[0, frame, row : row + 16, lanes].astype(F32)
+                total = total + (values[:8] + values[8:])
+            total_ref[frame, :, lanes] = total
 
     @pl.when(pl.program_id(0) == pl.num_programs(0) - 1)
     def _():
@@ -267,10 +272,10 @@
 
 
 def chunk_plan(count):
-    if count < 4:
+    if count < 8:
         return [[slot] for slot in range(1, count)] + [[0]]
-    order = [1, 2, 3, 0] + list(range(4, count))
-    return [order[:1]] + [order[i : i + 2] for i in range(1, count - 1, 2)] + [order[count - 1 :]]
+    order = [1, 2, 3, 4, 0] + list(range(5, count))
+    return [order[i : i + 2] for i in range(0, count, 2)]
 
 
 def special_chunk(plan):
@@ -624,7 +629,15 @@
     along_v = jnp.stack([jnp.sin(angle_v[0]), jnp.cos(angle_v[0]), jnp.sin(angle_v[1]), jnp.cos(angle_v[1])], axis=1)
 
     rows_to = LENGTH // (halves * bands * projections)
-    phases, pending, after = [], [], []
+    received, pending, after = [], [], []
+
+    def deliver(near, from_other, earlier):
+        phase = add_shares(near, from_other, earlier)
+        send = phase.reshape(bands * projections, rows_to, phase.shape[2])
+        back = lax.all_to_all(send, ("inner", "proj"), split_axis=0, concat_axis=0, tiled=True)
+        received.append(back.reshape(bands, projections, rows_to, phase.shape[2]))
+        return phase
+
     for chunk, members in enumerate(plan):
         blocks = []
         for offset in range(bands):
@@ -642,17 +655,11 @@
         start = sum(len(each) for each in plan[:chunk])
         blocks = [block.reshape(-1, MINOR, width) for block in blocks]
         near, far = columns(blocks, here, along_u, along_v[start : start + len(members)], nyquist, after)
+        after = [far]
         if pending:
-            phases.append(add_shares(*pending.pop(), [far]))
+            after = received[-1:] + [deliver(*pending.pop(), [far])]
         pending.append((near, lax.ppermute(far, "half", [(0, 1), (1, 0)])))
-        after = [far] if chunk == 0 else [phases[-1]]
-    phases.append(add_shares(*pending.pop(), []))
-
-    received = []
-    for phase in phases:
-        phase = phase.reshape(bands * projections, rows_to, phase.shape[2])
-        back = lax.all_to_all(phase, ("inner", "proj"), split_axis=0, concat_axis=0, tiled=True)
-        received.append(back.reshape(bands, projections, rows_to, phase.shape[2]))
+    deliver(*pending.pop(), received[-1:])
 
     return rows_inverse(received, proj_order, bands, plan)
 

time: 506 us -> 431 us (0.85)
  blocking collectives: 94.6 us -> 64 us
  Pallas kernels: 229 us -> 203 us
  waiting for transfers between devices: 128 us -> 115 us
    all_to_all x2 -> x1, blocking collectives: 86.2 us -> 55.6 us  [deliver(): lax.all_to_all(send, ('inner', 'proj'), split_axis=0, concat_axis=0, tile...]
    pallas_call x5 -> x4, Pallas kernels: 138 us -> 116 us  [columns(): pl.pallas_call(functools.partial(column_kernel, special, tiles, bands, le...]
    ppermute x5 -> x4, waiting for transfers between devices: 87.3 us -> 65.3 us  [on_device(): pending.append((near, lax.ppermute(far, 'half', [(0, 1), (1, 0)])))]
    all_to_all x3, waiting for transfers between devices: 41.1 us -> 49.8 us  [deliver(): lax.all_to_all(send, ('inner', 'proj'), split_axis=0, concat_axis=0, tile...]
    pallas_call x5 -> x4, Pallas kernels: 21.5 us -> 18.6 us  [add_shares(): pl.pallas_call(share_kernel, grid=(near.shape[0] // 4,), in_specs=[spec,...]
  transfers between devices with their start and end apart: 13 -> 11, of which waited for: 5 -> 7; matrix products, arithmetic and copies ran while one was open for 5% -> 5% of each run, Pallas kernels for 32% -> 30%
where the time goes in v6:
time: 431 us; the launch traced here: 430 us
  Pallas kernels  203 us (47%)
  waiting for transfers between devices  115 us (27%)
  blocking collectives  64 us (15%)
  starting transfers between devices  20.8 us (5%)
  local copies, waits for them, and re-layouts  16.6 us (4%)
  other arithmetic  8.45 us (2%)
    pallas_call x4, Pallas kernels, columns(): pl.pallas_call(functools.partial(column_kernel, special, tiles, bands, le...  116 us
    ppermute x4, waiting for transfers between devices, on_device(): pending.append((near, lax.ppermute(far, 'half', [(0, 1), (1, 0)])))  65.3 us
    all_to_all x1, blocking collectives, deliver(): lax.all_to_all(send, ('inner', 'proj'), split_axis=0, concat_axis=0, tile...  55.6 us
    all_to_all x3, waiting for transfers between devices, deliver(): lax.all_to_all(send, ('inner', 'proj'), split_axis=0, concat_axis=0, tile...  49.8 us
    pallas_call x1, Pallas kernels, rows_forward(): pl.pallas_call(functools.partial(row_kernel, plan, bands), grid=(rows //...  38.4 us
    pallas_call x1, Pallas kernels, rows_inverse(): pl.pallas_call(functools.partial(final_kernel, plan, bands), grid=(rows /...  21.4 us
    pallas_call x4, Pallas kernels, add_shares(): pl.pallas_call(share_kernel, grid=(near.shape[0] // 4,), in_specs=[spec,...  18.6 us
    all_to_all x3, starting transfers between devices, deliver(): lax.all_to_all(send, ('inner', 'proj'), split_axis=0, concat_axis=0, tile...  16.5 us
  transfers between devices with their start and end apart: 11, of which 7 were waited for; matrix products, arithmetic and copies ran while one was open for 5% of the time, Pallas kernels for 30%

profile of v6, /device:TPU:0, one launch (start us, length us, event | category | flops | bytes accessed | tf_op | source)
XLA Modules:
  0.0 430.1 jit_solution(4481170320554929835)
XLA Ops:
  0.0 9.3 %frame_sums.1 = f32[1,2]{1,0:T(1,128)} custom-call(bf16[1,2,1024,4096]{3,2,1,0:T(8,128)(2,1)} %x_ref.3), custom_call_target="tpu_custom_call" | custom-call | tf_op jit(solution)/shard_map/frame_sums/pallas_call | solution.py:192
  9.3 8.5 %psum.7 = f32[1,2]{1,0:T(1,128)S(1)} all-reduce(f32[1,2]{1,0:T(1,128)} %frame_sums.1), channel_id=1, replica_groups=mesh['proj'=8,'half'=2,'inner'=2] {'half','inner'}, use_global_device_ids=true, to_apply=%region_1.0 | all-reduce | flops 2 | bytes 16 | tf_op jit(solution)/shard_map/psum | solution.py:611
  17.8 0.6 broadcast_divide_fusion.scale_ref
  18.4 38.4 %rows_forward.1 = (bf16[1024,1024]{1,0:T(8,128)(2,1)}, bf16[1024,1024]{1,0:T(8,128)(2,1)}, bf16[1024,1024]{1,0:T(8,128)(2,1)}, bf16[1024,1024]{1,0:T(8,128)(2,1)...) custom-call(s32[1]{0:T(128)} %bitcast.9.band_ref, ...), custom_call_target="tpu_custom_call" | custom-call | flops 876173328384 | bytes 42991616 | tf_op jit(solution)/shard_map/rows_forward/pallas_call | solution.py:302
  56.8 0.5 collective-permute-start
  57.4 0.4 collective-permute-start.6
  57.9 3.2 slice.84
  61.1 0.7 copy.80
  62.2 2.0 copy.78.rest_2_
  64.2 0.6 pad_clamp_fusion
  65.0 0.6 fusion.33
  65.7 0.9 multiply_sine_fusion
  66.8 1.3 copy-done.11
  68.2 28.8 %columns.4 = (f32[16,128,512]{2,1,0:T(8,128)}, bf16[16,128,512]{2,1,0:T(8,128)(2,1)}) custom-call(s32[1]{0:T(128)} %bitcast.9.band_ref, f32[2,4,128]{2,1,0:T(4,128)} %get-tuple-element.52.v_ref, bf16[8,128,1024]{2,1,0:T(8,128)(2,1)} %bitcast.93, bf16[8,128,1024]{2,1,0:T(8,128)(2,1)} %bitcast.89, f32[32,128,4]{2,1,0:T(8,128)} %copy.78.rest_2_, ...), custom_call_target="tpu_custom_call" | custom-call | flops 549755813888 | bytes 31457280 | tf_op jit(solution)/shard_map/columns/pallas_call | solution.py:462
  97.0 0.4 collective-permute-start.1
  97.5 28.7 %columns.5 = (f32[16,128,512]{2,1,0:T(8,128)}, bf16[16,128,512]{2,1,0:T(8,128)(2,1)}) custom-call(s32[1]{0:T(128)} %bitcast.9.band_ref, f32[2,4,128]{2,1,0:T(4,128)} %get-tuple-element.51.v_ref, bf16[8,128,1024]{2,1,0:T(8,128)(2,1)} %bitcast.92, bf16[8,128,1024]{2,1,0:T(8,128)(2,1)} %bitcast.25.rest_1_, f32[32,128,4]{2,1,0:T(8,128)} %copy.78.rest_2_, ...), custom_call_target="tpu_custom_call" | custom-call | flops 549755813888 | bytes 31457280 | tf_op jit(solution)/shard_map/columns/pallas_call | solution.py:462
  126.3 3.3 slice.85
  129.8 0.7 gather_fusion
  130.7 0.3 convolution_bitcast_fusion.2
  131.0 0.3 convolution_bitcast_fusion.1
  131.4 0.3 convolution_bitcast_fusion
  132.0 0.7 copy.83
  132.7 1.7 collective-permute-start.3
  134.4 11.5 %collective-permute-done.1.far_ref = bf16[16,128,512]{2,1,0:T(8,128)(2,1)} collective-permute-done((bf16[16,128,512]{2,1,0:T(8,128)(2,1)}, bf16[16,128,512]{2,1,0:T(8,128)(2,1)}, u32[]{:S(2)}, u32[]{:S(2)}) %collective-permute-start.1) | collective-permute-done | bytes 2097184 | tf_op jit(solution)/shard_map/ppermute | solution.py:661
  145.9 4.7 %add_shares.4.rest_7_ = bf16[16,128,512]{2,1,0:T(8,128)(2,1)} custom-call(f32[16,128,512]{2,1,0:T(8,128)} %get-tuple-element.23.near_ref, bf16[16,128,512]{2,1,0:T(8,128)(2,1)} %collective-permute-done.1.far_ref, bf16[16,128,512]{2,1,0:T(8,128)(2,1)} %get-tuple-element.27.rest_0_), custom_call_target="tpu_custom_call" | custom-call | tf_op jit(solution)/shard_map/add_shares/pallas_call | solution.py:491
  150.6 6.0 %all-to-all-start = ((bf16[16,128,512]{2,1,0:T(8,128)(2,1)}), bf16[16,128,512]{2,1,0:T(8,128)(2,1)}, u32[]{:S(2)}, u32[]{:S(2)}) async-start(bf16[16,128,512]{2,1,0:T(8,128)(2,1)} %add_shares.4.rest_7_), calls=%async_computation | async-start | bytes 4194304 | tf_op jit(solution)/shard_map/all_to_all | solution.py:637
  156.6 29.4 %columns.6 = (f32[16,128,512]{2,1,0:T(8,128)}, bf16[16,128,512]{2,1,0:T(8,128)(2,1)}) custom-call(s32[1]{0:T(128)} %bitcast.9.band_ref, f32[2,4,128]{2,1,0:T(4,128)} %get-tuple-element.50.v_ref, bf16[8,128,1024]{2,1,0:T(8,128)(2,1)} %bitcast.83, bf16[8,128,1024]{2,1,0:T(8,128)(2,1)} %bitcast.28.rest_1_, f32[32,128,4]{2,1,0:T(8,128)} %copy.78.rest_2_, ...), custom_call_target="tpu_custom_call" | custom-call | flops 549755813888 | bytes 31457280 | tf_op jit(solution)/shard_map/columns/pallas_call | solution.py:462
  186.0 0.6 collective-permute-start.5
  186.6 4.2 collective-permute-done.3.far_ref
  190.8 4.6 %add_shares.5.rest_8_ = bf16[16,128,512]{2,1,0:T(8,128)(2,1)} custom-call(f32[16,128,512]{2,1,0:T(8,128)} %get-tuple-element.28.near_ref, bf16[16,128,512]{2,1,0:T(8,128)(2,1)} %collective-permute-done.3.far_ref, bf16[16,128,512]{2,1,0:T(8,128)(2,1)} %get-tuple-element.31.rest_0_), custom_call_target="tpu_custom_call" | custom-call | tf_op jit(solution)/shard_map/add_shares/pallas_call | solution.py:491
  195.4 8.7 %all-to-all-done = bf16[16,128,512]{2,1,0:T(8,128)(2,1)} async-done(((bf16[16,128,512]{2,1,0:T(8,128)(2,1)}), bf16[16,128,512]{2,1,0:T(8,128)(2,1)}, u32[]{:S(2)}, u32[]{:S(2)}) %all-to-all-start) | async-done | bytes 2097184 | tf_op jit(solution)/shard_map/all_to_all | solution.py:637
  204.2 28.7 %columns.7 = (f32[16,128,512]{2,1,0:T(8,128)}, bf16[16,128,512]{2,1,0:T(8,128)(2,1)}) custom-call(s32[1]{0:T(128)} %bitcast.9.band_ref, f32[2,4,128]{2,1,0:T(4,128)} %get-tuple-element.49.v_ref, bf16[8,128,1024]{2,1,0:T(8,128)(2,1)} %bitcast.91, bf16[8,128,1024]{2,1,0:T(8,128)(2,1)} %bitcast.50.rest_1_, f32[32,128,4]{2,1,0:T(8,128)} %copy.78.rest_2_, ...), custom_call_target="tpu_custom_call" | custom-call | flops 549755813888 | bytes 31457280 | tf_op jit(solution)/shard_map/columns/pallas_call | solution.py:462
  232.9 2.3 collective-permute-done.5.far_ref
  235.2 4.7 %add_shares.6 = bf16[16,128,512]{2,1,0:T(8,128)(2,1)} custom-call(f32[16,128,512]{2,1,0:T(8,128)} %get-tuple-element.32.near_ref, bf16[16,128,512]{2,1,0:T(8,128)(2,1)} %collective-permute-done.5.far_ref, bf16[16,128,512]{2,1,0:T(8,128)(2,1)} %get-tuple-element.35.rest_0_), custom_call_target="tpu_custom_call" | custom-call | tf_op jit(solution)/shard_map/add_shares/pallas_call | solution.py:491
  239.9 55.6 %all_to_all.20 = bf16[16,128,512]{2,1,0:T(8,128)(2,1)} all-to-all(bf16[16,128,512]{2,1,0:T(8,128)(2,1)} %add_shares.6), channel_id=1, replica_groups=mesh['proj'=8,'half'=2,'inner'=2] {'inner','proj'}, dimensions={0} | all-to-all | bytes 4194304 | tf_op jit(solution)/shard_map/all_to_all | solution.py:637
  295.4 4.6 %all-to-all-start.1 = ((bf16[16,128,512]{2,1,0:T(8,128)(2,1)}), bf16[16,128,512]{2,1,0:T(8,128)(2,1)}, u32[]{:S(2)}, u32[]{:S(2)}) async-start(bf16[16,128,512]{2,1,0:T(8,128)(2,1)} %add_shares.5.rest_8_), calls=%async_computation.1 | async-start | bytes 4194304 | tf_op jit(solution)/shard_map/all_to_all | solution.py:637
  300.0 0.6 collective-permute-start.7
  300.6 47.3 %collective-permute-done.7.far_ref = bf16[16,128,512]{2,1,0:T(8,128)(2,1)S(1)} collective-permute-done((bf16[16,128,512]{2,1,0:T(8,128)(2,1)S(1)}, bf16[16,128,512]{2,1,0:T(8,128)(2,1)S(1)}, u32[]{:S(2)}, u32[]{:S(2)}) %collective-permute-start.7) | collective-permute-done | bytes 2097184 | tf_op jit(solution)/shard_map/ppermute | solution.py:661
  347.9 1.3 copy-done.1
  349.2 4.6 %add_shares.7 = bf16[16,128,512]{2,1,0:T(8,128)(2,1)} custom-call(f32[16,128,512]{2,1,0:T(8,128)} %get-tuple-element.36.near_ref, bf16[16,128,512]{2,1,0:T(8,128)(2,1)} %copy-done.1, bf16[2,8,128,512]{3,2,1,0:T(8,128)(2,1)} %bitcast.77), custom_call_target="tpu_custom_call" | custom-call | tf_op jit(solution)/shard_map/add_shares/pallas_call | solution.py:491
  353.9 5.9 %all-to-all-start.3 = ((bf16[16,128,512]{2,1,0:T(8,128)(2,1)}), bf16[16,128,512]{2,1,0:T(8,128)(2,1)S(1)}, u32[]{:S(2)}, u32[]{:S(2)}) async-start(bf16[16,128,512]{2,1,0:T(8,128)(2,1)} %add_shares.7), calls=%async_computation.3 | async-start | bytes 4194304 | tf_op jit(solution)/shard_map/all_to_all | solution.py:637
  359.8 0.7 fusion.34
  360.5 4.4 %compare_select_fusion.1 = s32[256,1]{0,1:T(1,128)S(1)} fusion(s32[]{:T(128)} %bitcast.1, s32[]{:T(128)} %bitcast.2, s32[]{:T(128)} %bitcast.3, s32[]{:T(128)} %bitcast.4, s32[]{:T(128)} %bitcast.5, s32[]{:T(128)} %bitcast.7, s32[]{:T(128)} %bitcast.6), kind=kLoop, calls=%fused_computation.56 | loop fusion | flops 5888 | bytes 1052 | tf_op jit(solution)/shard_map/gather | solution.py:537
  365.0 0.7 fusion.24
  365.6 0.7 fusion.place_ref
  366.3 41.1 %all-to-all-done.3 = bf16[16,128,512]{2,1,0:T(8,128)(2,1)S(1)} async-done(((bf16[16,128,512]{2,1,0:T(8,128)(2,1)}), bf16[16,128,512]{2,1,0:T(8,128)(2,1)S(1)}, u32[]{:S(2)}, u32[]{:S(2)}) %all-to-all-start.3) | async-done | bytes 2097184 | tf_op jit(solution)/shard_map/all_to_all | solution.py:637
  407.4 1.3 copy-done.2
  408.7 21.4 %rows_inverse.1 = f32[1024,4096]{1,0:T(8,128)} custom-call(bf16[256,256]{1,0:T(8,128)(2,1)} %fusion.place_ref, bf16[2,8,128,512]{3,2,1,0:T(8,128)(2,1)} %bitcast.26.rest_7_.rest_0_, bf16[2,8,128,512]{3,2,1,0:T(8,128)(2,1)} %bitcast.48.rest_1_, bf16[2,8,128,512]{3,2,1,0:T(8,128)(2,1)} %bitcast.78, bf16[2,8,128,512]{3,2,1,0:T(8,128)(2,1)} %bitcast.79, ...), custom_call_target="tpu_custom_call" | custom-call | flops 10737418240 | bytes 33554432 | tf_op jit(solution)/shard_map/rows_inverse/pallas_call | solution.py:539
  (61 shorter events, 1.9 us)
Async XLA Ops:
  18.3 43.5 %copy-start.12 = (f32[8]{0:T(128)S(1)}, f32[8]{0:T(128)}, u32[]{:S(2)}) copy-start(f32[8]{0:T(128)} %param.21) | copy-start | bytes 100
  18.4 43.5 %copy-start.13 = (s32[1,2]{1,0:T(1,128)S(1)}, s32[1,2]{1,0:T(1,128)}, u32[]{:S(2)}) copy-start(s32[1,2]{1,0:T(1,128)} %param.20) | copy-start | bytes 28
  56.8 8.0 %copy-start.14 = (s32[8]{0:T(128)S(1)}, s32[8]{0:T(128)}, u32[]{:S(2)}) copy-start(s32[8]{0:T(128)} %constant.126) | copy-start | bytes 100
  56.8 69.5 %collective-permute-start.4 = (bf16[1024,1024]{1,0:T(8,128)(2,1)}, bf16[1024,1024]{1,0:T(8,128)(2,1)}, u32[]{:S(2)}, u32[]{:S(2)}) collective-permute-start(bf16[1024,1024]{1,0:T(8,128)(2,1)} %get-tuple-element.30), channel_id=1, source_target_pairs={{0,1},{1,0},{2,3},{3,2},{4,5},{5,4},{6,7},{7,6},{8,9},{9,8},{10,11... | collective-permute-start | bytes 6291464 | tf_op jit(solution)/shard_map/ppermute | solution.py:646
  56.8 10.0 %collective-permute-start = (bf16[1024,1024]{1,0:T(8,128)(2,1)}, bf16[1024,1024]{1,0:T(8,128)(2,1)S(1)}, u32[]{:S(2)}, u32[]{:S(2)}) collective-permute-start(bf16[1024,1024]{1,0:T(8,128)(2,1)} %get-tuple-element.22), channel_id=1, source_target_pairs={{0,1},{1,0},{2,3},{3,2},{4,5},{5,4},{6,7},{7,6},{8,9},{9,8},{10,11... | collective-permute-start | bytes 6291464 | tf_op jit(solution)/shard_map/ppermute | solution.py:646
  57.3 40.1 %collective-permute-start.2 = (bf16[1024,1024]{1,0:T(8,128)(2,1)}, bf16[1024,1024]{1,0:T(8,128)(2,1)}, u32[]{:S(2)}, u32[]{:S(2)}) collective-permute-start(bf16[1024,1024]{1,0:T(8,128)(2,1)} %get-tuple-element.26), channel_id=1, source_target_pairs={{0,1},{1,0},{2,3},{3,2},{4,5},{5,4},{6,7},{7,6},{8,9},{9,8},{10,11... | collective-permute-start | bytes 6291464 | tf_op jit(solution)/shard_map/ppermute | solution.py:646
  57.4 138.0 %collective-permute-start.6 = (bf16[1024,1024]{1,0:T(8,128)(2,1)}, bf16[1024,1024]{1,0:T(8,128)(2,1)}, u32[]{:S(2)}, u32[]{:S(2)}) collective-permute-start(bf16[1024,1024]{1,0:T(8,128)(2,1)} %get-tuple-element.34), channel_id=1, source_target_pairs={{0,1},{1,0},{2,3},{3,2},{4,5},{5,4},{6,7},{7,6},{8,9},{9,8},{10,11... | collective-permute-start | bytes 6291464 | tf_op jit(solution)/shard_map/ppermute | solution.py:646
  66.8 1.3 copy-start.11
  97.0 48.8 %collective-permute-start.1 = (bf16[16,128,512]{2,1,0:T(8,128)(2,1)}, bf16[16,128,512]{2,1,0:T(8,128)(2,1)}, u32[]{:S(2)}, u32[]{:S(2)}) collective-permute-start(bf16[16,128,512]{2,1,0:T(8,128)(2,1)} %get-tuple-element.24.rest_7_), channel_id=1, source_target_pairs={{0,2},{2,0},{1,3},{3,1},{4,6},{6,4},{5,7},{7,5},{8,10},{10,8},{9,1... | collective-permute-start | bytes 6291464 | tf_op jit(solution)/shard_map/ppermute | solution.py:661
  97.5 32.3 %copy-start.10 = (bf16[1,1024,2]{1,2,0:T(2,128)(2,1)S(1)}, bf16[1,1024,2]{1,2,0:T(2,128)(2,1)}, u32[]{:S(2)}) copy-start(bf16[1,1024,2]{1,2,0:T(2,128)(2,1)} %copy.80) | copy-start | bytes 12292
  126.2 4.5 %copy-start.3 = (f32[2,64,2,64]{1,3,0,2:T(8,128)S(1)}, f32[2,64,2,64]{1,3,0,2:T(8,128)}, u32[]{:S(2)}) copy-start(f32[2,64,2,64]{1,3,0,2:T(8,128)} %constant.115.clone) | copy-start | bytes 196612
  126.2 4.8 %copy-start.6 = (f32[1,64,64]{2,1,0:T(8,128)S(1)}, f32[1,64,64]{2,1,0:T(8,128)}, u32[]{:S(2)}) copy-start(f32[1,64,64]{2,1,0:T(8,128)} %constant.127) | copy-start | bytes 49156
  126.2 4.8 %copy-start.7 = (f32[1,64,64]{2,1,0:T(8,128)S(1)}, f32[1,64,64]{2,1,0:T(8,128)}, u32[]{:S(2)}) copy-start(f32[1,64,64]{2,1,0:T(8,128)} %constant.128) | copy-start | bytes 49156
  126.2 5.1 %copy-start.4 = (f32[2,64,64]{2,1,0:T(8,128)S(1)}, f32[2,64,64]{2,1,0:T(8,128)}, u32[]{:S(2)}) copy-start(f32[2,64,64]{2,1,0:T(8,128)} %multiply_sine_fusion) | copy-start | bytes 98308
  126.2 5.1 %copy-start.5 = (f32[2,64,2,64]{3,1,0,2:T(8,128)S(1)}, f32[2,64,2,64]{3,1,0,2:T(8,128)}, u32[]{:S(2)}) copy-start(f32[2,64,2,64]{3,1,0,2:T(8,128)} %constant.118.clone) | copy-start | bytes 196612
  126.3 5.4 %copy-start.8 = (f32[2,64,64]{1,2,0:T(8,128)S(1)}, f32[2,64,64]{1,2,0:T(8,128)}, u32[]{:S(2)}) copy-start(f32[2,64,64]{1,2,0:T(8,128)} %constant.119.clone) | copy-start | bytes 98308
  132.7 58.1 %collective-permute-start.3 = (bf16[16,128,512]{2,1,0:T(8,128)(2,1)}, bf16[16,128,512]{2,1,0:T(8,128)(2,1)}, u32[]{:S(2)}, u32[]{:S(2)}) collective-permute-start(bf16[16,128,512]{2,1,0:T(8,128)(2,1)} %get-tuple-element.27.rest_0_), channel_id=1, source_target_pairs={{0,2},{2,0},{1,3},{3,1},{4,6},{6,4},{5,7},{7,5},{8,10},{10,8},{9,1... | collective-permute-start | bytes 6291464 | tf_op jit(solution)/shard_map/ppermute | solution.py:661
  150.6 53.6 %all-to-all-start = ((bf16[16,128,512]{2,1,0:T(8,128)(2,1)}), bf16[16,128,512]{2,1,0:T(8,128)(2,1)}, u32[]{:S(2)}, u32[]{:S(2)}) async-start(bf16[16,128,512]{2,1,0:T(8,128)(2,1)} %add_shares.4.rest_7_), calls=%async_computation | async-start | bytes 4194304 | tf_op jit(solution)/shard_map/all_to_all | solution.py:637
  186.0 49.2 %collective-permute-start.5 = (bf16[16,128,512]{2,1,0:T(8,128)(2,1)}, bf16[16,128,512]{2,1,0:T(8,128)(2,1)}, u32[]{:S(2)}, u32[]{:S(2)}) collective-permute-start(bf16[16,128,512]{2,1,0:T(8,128)(2,1)} %get-tuple-element.31.rest_0_), channel_id=1, source_target_pairs={{0,2},{2,0},{1,3},{3,1},{4,6},{6,4},{5,7},{7,5},{8,10},{10,8},{9,1... | collective-permute-start | bytes 6291464 | tf_op jit(solution)/shard_map/ppermute | solution.py:661
  295.4 4.6 %copy-start = (bf16[16,128,512]{2,1,0:T(8,128)(2,1)S(1)}, bf16[16,128,512]{2,1,0:T(8,128)(2,1)}, u32[]{:S(2)}) copy-start(bf16[16,128,512]{2,1,0:T(8,128)(2,1)} %get-tuple-element.35.rest_0_) | copy-start | bytes 6291460
  295.4 58.4 %all-to-all-start.1 = ((bf16[16,128,512]{2,1,0:T(8,128)(2,1)}), bf16[16,128,512]{2,1,0:T(8,128)(2,1)}, u32[]{:S(2)}, u32[]{:S(2)}) async-start(bf16[16,128,512]{2,1,0:T(8,128)(2,1)} %add_shares.5.rest_8_), calls=%async_computation.1 | async-start | bytes 4194304 | tf_op jit(solution)/shard_map/all_to_all | solution.py:637
  300.0 47.9 %collective-permute-start.7 = (bf16[16,128,512]{2,1,0:T(8,128)(2,1)S(1)}, bf16[16,128,512]{2,1,0:T(8,128)(2,1)S(1)}, u32[]{:S(2)}, u32[]{:S(2)}) collective-permute-start(bf16[16,128,512]{2,1,0:T(8,128)(2,1)S(1)} %copy-done), channel_id=1, source_target_pairs={{0,2},{2,0},{1,3},{3,1},{4,6},{6,4},{5,7},{7,5},{8,10},{10,8},{9,1... | collective-permute-start | bytes 6291464 | tf_op jit(solution)/shard_map/ppermute | solution.py:661
  347.9 1.3 copy-start.1
  353.9 5.9 %copy-start.9 = (s32[8]{0:T(128)S(1)}, s32[8]{0:T(128)}, u32[]{:S(2)}) copy-start(s32[8]{0:T(128)} %param.22) | copy-start | bytes 100
  353.9 53.5 %all-to-all-start.3 = ((bf16[16,128,512]{2,1,0:T(8,128)(2,1)}), bf16[16,128,512]{2,1,0:T(8,128)(2,1)S(1)}, u32[]{:S(2)}, u32[]{:S(2)}) async-start(bf16[16,128,512]{2,1,0:T(8,128)(2,1)} %add_shares.7), calls=%async_computation.3 | async-start | bytes 4194304 | tf_op jit(solution)/shard_map/all_to_all | solution.py:637
  407.4 1.3 copy-start.2

commit v7 on v6

--- a/solution.py
+++ b/solution.py
@@ -657,7 +657,8 @@
         near, far = columns(blocks, here, along_u, along_v[start : start + len(members)], nyquist, after)
         after = [far]
         if pending:
-            after = received[-1:] + [deliver(*pending.pop(), [far])]
+            earlier = received[-1:]
+            after = earlier + [deliver(*pending.pop(), [far] + (earlier if chunk > 2 else []))]
         pending.append((near, lax.ppermute(far, "half", [(0, 1), (1, 0)])))
     deliver(*pending.pop(), received[-1:])
 

time: 431 us -> 398 us (0.923)
  blocking collectives: 64 us -> 8.48 us
  waiting for transfers between devices: 115 us -> 132 us
  starting transfers between devices: 20.8 us -> 26.4 us
    all_to_all x1 -> x0, blocking collectives: 55.6 us -> none  [deliver(): lax.all_to_all(send, ('inner', 'proj'), split_axis=0, concat_axis=0, tile...]
    all_to_all x3 -> x4, waiting for transfers between devices: 49.8 us -> 68.7 us  [deliver(): lax.all_to_all(send, ('inner', 'proj'), split_axis=0, concat_axis=0, tile...]
    all_to_all x3 -> x4, starting transfers between devices: 16.5 us -> 22.1 us  [deliver(): lax.all_to_all(send, ('inner', 'proj'), split_axis=0, concat_axis=0, tile...]
  transfers between devices with their start and end apart: 11 -> 12, of which waited for: 7 -> 7; matrix products, arithmetic and copies ran while one was open for 5% -> 5% of each run, Pallas kernels for 30% -> 31%
where the time goes in v7:
time: 398 us; the launch traced here: 397 us
  Pallas kernels  203 us (51%)
  waiting for transfers between devices  132 us (33%)
  starting transfers between devices  26.4 us (7%)
  local copies, waits for them, and re-layouts  16.7 us (4%)
  blocking collectives  8.48 us (2%)
  other arithmetic  8.32 us (2%)
    pallas_call x4, Pallas kernels, columns(): pl.pallas_call(functools.partial(column_kernel, special, tiles, bands, le...  116 us
    all_to_all x4, waiting for transfers between devices, deliver(): lax.all_to_all(send, ('inner', 'proj'), split_axis=0, concat_axis=0, tile...  68.7 us
    ppermute x4, waiting for transfers between devices, on_device(): pending.append((near, lax.ppermute(far, 'half', [(0, 1), (1, 0)])))  63.4 us
    pallas_call x1, Pallas kernels, rows_forward(): pl.pallas_call(functools.partial(row_kernel, plan, bands), grid=(rows //...  38.4 us
    all_to_all x4, starting transfers between devices, deliver(): lax.all_to_all(send, ('inner', 'proj'), split_axis=0, concat_axis=0, tile...  22.1 us
    pallas_call x1, Pallas kernels, rows_inverse(): pl.pallas_call(functools.partial(final_kernel, plan, bands), grid=(rows /...  21.4 us
    pallas_call x4, Pallas kernels, add_shares(): pl.pallas_call(share_kernel, grid=(near.shape[0] // 4,), in_specs=[spec,...  18.6 us
    pallas_call x1, Pallas kernels, frame_sums(): pl.pallas_call(sum_kernel, grid=(rows // block,), in_specs=[pl.BlockSpec(...  9.31 us
  transfers between devices with their start and end apart: 12, of which 7 were waited for; matrix products, arithmetic and copies ran while one was open for 5% of the time, Pallas kernels for 31%

profile of v7, /device:TPU:0, one launch (start us, length us, event | category | flops | bytes accessed | tf_op | source)
XLA Modules:
  0.0 397.2 jit_solution(5868372882773489646)
XLA Ops:
  0.0 9.3 %frame_sums.1 = f32[1,2]{1,0:T(1,128)} custom-call(bf16[1,2,1024,4096]{3,2,1,0:T(8,128)(2,1)} %x_ref.3), custom_call_target="tpu_custom_call" | custom-call | tf_op jit(solution)/shard_map/frame_sums/pallas_call | solution.py:192
  9.3 8.5 %psum.7 = f32[1,2]{1,0:T(1,128)S(1)} all-reduce(f32[1,2]{1,0:T(1,128)} %frame_sums.1), channel_id=1, replica_groups=mesh['proj'=8,'half'=2,'inner'=2] {'half','inner'}, use_global_device_ids=true, to_apply=%region_1.0 | all-reduce | flops 2 | bytes 16 | tf_op jit(solution)/shard_map/psum | solution.py:611
  17.8 0.6 broadcast_divide_fusion.scale_ref
  18.4 38.4 %rows_forward.1 = (bf16[1024,1024]{1,0:T(8,128)(2,1)}, bf16[1024,1024]{1,0:T(8,128)(2,1)}, bf16[1024,1024]{1,0:T(8,128)(2,1)}, bf16[1024,1024]{1,0:T(8,128)(2,1)...) custom-call(s32[1]{0:T(128)} %bitcast.9.band_ref, ...), custom_call_target="tpu_custom_call" | custom-call | flops 876173328384 | bytes 42991616 | tf_op jit(solution)/shard_map/rows_forward/pallas_call | solution.py:302
  56.9 0.5 collective-permute-start
  57.4 0.4 collective-permute-start.6
  57.9 3.2 slice.84
  61.1 0.7 copy.80
  62.3 2.0 copy.78.rest_2_
  64.2 0.6 pad_clamp_fusion
  65.1 0.6 fusion.33
  65.7 0.9 multiply_sine_fusion
  66.8 1.4 copy-done.10
  68.2 28.8 %columns.4 = (f32[16,128,512]{2,1,0:T(8,128)}, bf16[16,128,512]{2,1,0:T(8,128)(2,1)}) custom-call(s32[1]{0:T(128)} %bitcast.9.band_ref, f32[2,4,128]{2,1,0:T(4,128)} %get-tuple-element.52.v_ref, bf16[8,128,1024]{2,1,0:T(8,128)(2,1)} %bitcast.93, bf16[8,128,1024]{2,1,0:T(8,128)(2,1)} %bitcast.89, f32[32,128,4]{2,1,0:T(8,128)} %copy.78.rest_2_, ...), custom_call_target="tpu_custom_call" | custom-call | flops 549755813888 | bytes 31457280 | tf_op jit(solution)/shard_map/columns/pallas_call | solution.py:462
  97.0 0.4 collective-permute-start.1
  97.5 28.7 %columns.5 = (f32[16,128,512]{2,1,0:T(8,128)}, bf16[16,128,512]{2,1,0:T(8,128)(2,1)}) custom-call(s32[1]{0:T(128)} %bitcast.9.band_ref, f32[2,4,128]{2,1,0:T(4,128)} %get-tuple-element.51.v_ref, bf16[8,128,1024]{2,1,0:T(8,128)(2,1)} %bitcast.92, bf16[8,128,1024]{2,1,0:T(8,128)(2,1)} %bitcast.25.rest_1_, f32[32,128,4]{2,1,0:T(8,128)} %copy.78.rest_2_, ...), custom_call_target="tpu_custom_call" | custom-call | flops 549755813888 | bytes 31457280 | tf_op jit(solution)/shard_map/columns/pallas_call | solution.py:462
  126.3 3.3 slice.85
  129.8 0.7 gather_fusion
  130.7 0.3 convolution_bitcast_fusion.2
  131.0 0.3 convolution_bitcast_fusion.1
  131.4 0.3 convolution_bitcast_fusion
  132.0 0.7 copy.83
  132.7 1.7 collective-permute-start.3
  134.4 11.5 %collective-permute-done.1.far_ref = bf16[16,128,512]{2,1,0:T(8,128)(2,1)} collective-permute-done((bf16[16,128,512]{2,1,0:T(8,128)(2,1)}, bf16[16,128,512]{2,1,0:T(8,128)(2,1)}, u32[]{:S(2)}, u32[]{:S(2)}) %collective-permute-start.1) | collective-permute-done | bytes 2097184 | tf_op jit(solution)/shard_map/ppermute | solution.py:662
  145.9 4.7 %add_shares.4.rest_7_ = bf16[16,128,512]{2,1,0:T(8,128)(2,1)} custom-call(f32[16,128,512]{2,1,0:T(8,128)} %get-tuple-element.23.near_ref, bf16[16,128,512]{2,1,0:T(8,128)(2,1)} %collective-permute-done.1.far_ref, bf16[16,128,512]{2,1,0:T(8,128)(2,1)} %get-tuple-element.27.rest_0_), custom_call_target="tpu_custom_call" | custom-call | tf_op jit(solution)/shard_map/add_shares/pallas_call | solution.py:491
  150.6 6.0 %all-to-all-start = ((bf16[16,128,512]{2,1,0:T(8,128)(2,1)}), bf16[16,128,512]{2,1,0:T(8,128)(2,1)}, u32[]{:S(2)}, u32[]{:S(2)}) async-start(bf16[16,128,512]{2,1,0:T(8,128)(2,1)} %add_shares.4.rest_7_), calls=%async_computation | async-start | bytes 4194304 | tf_op jit(solution)/shard_map/all_to_all | solution.py:637
  156.6 29.4 %columns.6 = (f32[16,128,512]{2,1,0:T(8,128)}, bf16[16,128,512]{2,1,0:T(8,128)(2,1)}) custom-call(s32[1]{0:T(128)} %bitcast.9.band_ref, f32[2,4,128]{2,1,0:T(4,128)} %get-tuple-element.50.v_ref, bf16[8,128,1024]{2,1,0:T(8,128)(2,1)} %bitcast.83, bf16[8,128,1024]{2,1,0:T(8,128)(2,1)} %bitcast.28.rest_1_, f32[32,128,4]{2,1,0:T(8,128)} %copy.78.rest_2_, ...), custom_call_target="tpu_custom_call" | custom-call | flops 549755813888 | bytes 31457280 | tf_op jit(solution)/shard_map/columns/pallas_call | solution.py:462
  186.0 0.6 collective-permute-start.5
  186.6 4.2 %collective-permute-done.3.far_ref = bf16[16,128,512]{2,1,0:T(8,128)(2,1)} collective-permute-done((bf16[16,128,512]{2,1,0:T(8,128)(2,1)}, bf16[16,128,512]{2,1,0:T(8,128)(2,1)}, u32[]{:S(2)}, u32[]{:S(2)}) %collective-permute-start.3) | collective-permute-done | bytes 2097184 | tf_op jit(solution)/shard_map/ppermute | solution.py:662
  190.8 4.6 %add_shares.5.rest_8_ = bf16[16,128,512]{2,1,0:T(8,128)(2,1)} custom-call(f32[16,128,512]{2,1,0:T(8,128)} %get-tuple-element.28.near_ref, bf16[16,128,512]{2,1,0:T(8,128)(2,1)} %collective-permute-done.3.far_ref, bf16[16,128,512]{2,1,0:T(8,128)(2,1)} %get-tuple-element.31.rest_0_), custom_call_target="tpu_custom_call" | custom-call | tf_op jit(solution)/shard_map/add_shares/pallas_call | solution.py:491
  195.5 8.7 %all-to-all-done = bf16[16,128,512]{2,1,0:T(8,128)(2,1)} async-done(((bf16[16,128,512]{2,1,0:T(8,128)(2,1)}), bf16[16,128,512]{2,1,0:T(8,128)(2,1)}, u32[]{:S(2)}, u32[]{:S(2)}) %all-to-all-start) | async-done | bytes 2097184 | tf_op jit(solution)/shard_map/all_to_all | solution.py:637
  204.2 5.2 %all-to-all-start.1 = ((bf16[16,128,512]{2,1,0:T(8,128)(2,1)}), bf16[16,128,512]{2,1,0:T(8,128)(2,1)}, u32[]{:S(2)}, u32[]{:S(2)}) async-start(bf16[16,128,512]{2,1,0:T(8,128)(2,1)} %add_shares.5.rest_8_), calls=%async_computation.1 | async-start | bytes 4194304 | tf_op jit(solution)/shard_map/all_to_all | solution.py:637
  209.4 28.8 %columns.7 = (f32[16,128,512]{2,1,0:T(8,128)}, bf16[16,128,512]{2,1,0:T(8,128)(2,1)}) custom-call(s32[1]{0:T(128)} %bitcast.9.band_ref, f32[2,4,128]{2,1,0:T(4,128)} %get-tuple-element.49.v_ref, bf16[8,128,1024]{2,1,0:T(8,128)(2,1)} %bitcast.91, bf16[8,128,1024]{2,1,0:T(8,128)(2,1)} %bitcast.50.rest_1_, f32[32,128,4]{2,1,0:T(8,128)} %copy.78.rest_2_, ...), custom_call_target="tpu_custom_call" | custom-call | flops 549755813888 | bytes 31457280 | tf_op jit(solution)/shard_map/columns/pallas_call | solution.py:462
  238.2 18.8 %all-to-all-done.1 = bf16[16,128,512]{2,1,0:T(8,128)(2,1)} async-done(((bf16[16,128,512]{2,1,0:T(8,128)(2,1)}), bf16[16,128,512]{2,1,0:T(8,128)(2,1)}, u32[]{:S(2)}, u32[]{:S(2)}) %all-to-all-start.1) | async-done | bytes 2097184 | tf_op jit(solution)/shard_map/all_to_all | solution.py:637
  257.0 4.6 %add_shares.6 = bf16[16,128,512]{2,1,0:T(8,128)(2,1)} custom-call(f32[16,128,512]{2,1,0:T(8,128)} %get-tuple-element.32.near_ref, bf16[16,128,512]{2,1,0:T(8,128)(2,1)} %collective-permute-done.5.far_ref, bf16[16,128,512]{2,1,0:T(8,128)(2,1)} %get-tuple-element.35.rest_0_, bf16[2,8,128,512]{3,2,1,0:T(8,128)(2,1)} %bitcast.48.rest_1_), custom_call_target="tpu_custom_call" | custom-call | tf_op jit(solution)/shard_map/add_shares/pallas_call | solution.py:491
  261.6 5.1 %all-to-all-start.2 = ((bf16[16,128,512]{2,1,0:T(8,128)(2,1)}), bf16[16,128,512]{2,1,0:T(8,128)(2,1)S(1)}, u32[]{:S(2)}, u32[]{:S(2)}) async-start(bf16[16,128,512]{2,1,0:T(8,128)(2,1)} %add_shares.6), calls=%async_computation.2 | async-start | bytes 4194304 | tf_op jit(solution)/shard_map/all_to_all | solution.py:637
  266.7 0.6 collective-permute-start.7
  267.3 47.7 %collective-permute-done.7.far_ref = bf16[16,128,512]{2,1,0:T(8,128)(2,1)} collective-permute-done((bf16[16,128,512]{2,1,0:T(8,128)(2,1)}, bf16[16,128,512]{2,1,0:T(8,128)(2,1)}, u32[]{:S(2)}, u32[]{:S(2)}) %collective-permute-start.7) | collective-permute-done | bytes 2097184 | tf_op jit(solution)/shard_map/ppermute | solution.py:662
  315.0 1.4 copy-done
  316.3 4.6 %add_shares.7 = bf16[16,128,512]{2,1,0:T(8,128)(2,1)} custom-call(f32[16,128,512]{2,1,0:T(8,128)} %get-tuple-element.36.near_ref, bf16[16,128,512]{2,1,0:T(8,128)(2,1)} %collective-permute-done.7.far_ref, bf16[2,8,128,512]{3,2,1,0:T(8,128)(2,1)} %bitcast.77), custom_call_target="tpu_custom_call" | custom-call | tf_op jit(solution)/shard_map/add_shares/pallas_call | solution.py:491
  321.0 5.9 %all-to-all-start.3 = ((bf16[16,128,512]{2,1,0:T(8,128)(2,1)}), bf16[16,128,512]{2,1,0:T(8,128)(2,1)S(1)}, u32[]{:S(2)}, u32[]{:S(2)}) async-start(bf16[16,128,512]{2,1,0:T(8,128)(2,1)} %add_shares.7), calls=%async_computation.3 | async-start | bytes 4194304 | tf_op jit(solution)/shard_map/all_to_all | solution.py:637
  326.9 0.7 fusion.34
  327.6 4.3 %compare_select_fusion.1 = s32[256,1]{0,1:T(1,128)S(1)} fusion(s32[]{:T(128)} %bitcast.1, s32[]{:T(128)} %bitcast.2, s32[]{:T(128)} %bitcast.3, s32[]{:T(128)} %bitcast.4, s32[]{:T(128)} %bitcast.5, s32[]{:T(128)} %bitcast.7, s32[]{:T(128)} %bitcast.6), kind=kLoop, calls=%fused_computation.56 | loop fusion | flops 5888 | bytes 1052 | tf_op jit(solution)/shard_map/gather | solution.py:537
  331.9 0.6 fusion.24
  332.6 0.7 fusion.place_ref
  333.3 41.2 %all-to-all-done.3 = bf16[16,128,512]{2,1,0:T(8,128)(2,1)S(1)} async-done(((bf16[16,128,512]{2,1,0:T(8,128)(2,1)}), bf16[16,128,512]{2,1,0:T(8,128)(2,1)S(1)}, u32[]{:S(2)}, u32[]{:S(2)}) %all-to-all-start.3) | async-done | bytes 2097184 | tf_op jit(solution)/shard_map/all_to_all | solution.py:637
  374.4 1.3 copy-done.1
  375.8 21.4 %rows_inverse.1 = f32[1024,4096]{1,0:T(8,128)} custom-call(bf16[256,256]{1,0:T(8,128)(2,1)} %fusion.place_ref, bf16[2,8,128,512]{3,2,1,0:T(8,128)(2,1)} %bitcast.26.rest_7_.rest_0_, bf16[2,8,128,512]{3,2,1,0:T(8,128)(2,1)} %bitcast.48.rest_1_, bf16[2,8,128,512]{3,2,1,0:T(8,128)(2,1)} %bitcast.78, bf16[2,8,128,512]{3,2,1,0:T(8,128)(2,1)} %bitcast.79, ...), custom_call_target="tpu_custom_call" | custom-call | flops 10737418240 | bytes 33554432 | tf_op jit(solution)/shard_map/rows_inverse/pallas_call | solution.py:539
  (60 shorter events, 1.9 us)
Async XLA Ops:
  18.4 43.5 %copy-start.11 = (f32[8]{0:T(128)S(1)}, f32[8]{0:T(128)}, u32[]{:S(2)}) copy-start(f32[8]{0:T(128)} %param.21) | copy-start | bytes 100
  18.4 43.5 %copy-start.12 = (s32[1,2]{1,0:T(1,128)S(1)}, s32[1,2]{1,0:T(1,128)}, u32[]{:S(2)}) copy-start(s32[1,2]{1,0:T(1,128)} %param.20) | copy-start | bytes 28
  56.8 8.1 %copy-start.13 = (s32[8]{0:T(128)S(1)}, s32[8]{0:T(128)}, u32[]{:S(2)}) copy-start(s32[8]{0:T(128)} %constant.126) | copy-start | bytes 100
  56.8 69.5 %collective-permute-start.4 = (bf16[1024,1024]{1,0:T(8,128)(2,1)}, bf16[1024,1024]{1,0:T(8,128)(2,1)}, u32[]{:S(2)}, u32[]{:S(2)}) collective-permute-start(bf16[1024,1024]{1,0:T(8,128)(2,1)} %get-tuple-element.30), channel_id=1, source_target_pairs={{0,1},{1,0},{2,3},{3,2},{4,5},{5,4},{6,7},{7,6},{8,9},{9,8},{10,11... | collective-permute-start | bytes 6291464 | tf_op jit(solution)/shard_map/ppermute | solution.py:646
  56.9 10.0 %collective-permute-start = (bf16[1024,1024]{1,0:T(8,128)(2,1)}, bf16[1024,1024]{1,0:T(8,128)(2,1)S(1)}, u32[]{:S(2)}, u32[]{:S(2)}) collective-permute-start(bf16[1024,1024]{1,0:T(8,128)(2,1)} %get-tuple-element.22), channel_id=1, source_target_pairs={{0,1},{1,0},{2,3},{3,2},{4,5},{5,4},{6,7},{7,6},{8,9},{9,8},{10,11... | collective-permute-start | bytes 6291464 | tf_op jit(solution)/shard_map/ppermute | solution.py:646
  57.4 40.1 %collective-permute-start.2 = (bf16[1024,1024]{1,0:T(8,128)(2,1)}, bf16[1024,1024]{1,0:T(8,128)(2,1)}, u32[]{:S(2)}, u32[]{:S(2)}) collective-permute-start(bf16[1024,1024]{1,0:T(8,128)(2,1)} %get-tuple-element.26), channel_id=1, source_target_pairs={{0,1},{1,0},{2,3},{3,2},{4,5},{5,4},{6,7},{7,6},{8,9},{9,8},{10,11... | collective-permute-start | bytes 6291464 | tf_op jit(solution)/shard_map/ppermute | solution.py:646
  57.4 151.9 %collective-permute-start.6 = (bf16[1024,1024]{1,0:T(8,128)(2,1)}, bf16[1024,1024]{1,0:T(8,128)(2,1)}, u32[]{:S(2)}, u32[]{:S(2)}) collective-permute-start(bf16[1024,1024]{1,0:T(8,128)(2,1)} %get-tuple-element.34), channel_id=1, source_target_pairs={{0,1},{1,0},{2,3},{3,2},{4,5},{5,4},{6,7},{7,6},{8,9},{9,8},{10,11... | collective-permute-start | bytes 6291464 | tf_op jit(solution)/shard_map/ppermute | solution.py:646
  66.8 1.4 copy-start.10
  97.0 48.8 %collective-permute-start.1 = (bf16[16,128,512]{2,1,0:T(8,128)(2,1)}, bf16[16,128,512]{2,1,0:T(8,128)(2,1)}, u32[]{:S(2)}, u32[]{:S(2)}) collective-permute-start(bf16[16,128,512]{2,1,0:T(8,128)(2,1)} %get-tuple-element.24.rest_7_), channel_id=1, source_target_pairs={{0,2},{2,0},{1,3},{3,1},{4,6},{6,4},{5,7},{7,5},{8,10},{10,8},{9,1... | collective-permute-start | bytes 6291464 | tf_op jit(solution)/shard_map/ppermute | solution.py:662
  97.5 32.3 %copy-start.9 = (bf16[1,1024,2]{1,2,0:T(2,128)(2,1)S(1)}, bf16[1,1024,2]{1,2,0:T(2,128)(2,1)}, u32[]{:S(2)}) copy-start(bf16[1,1024,2]{1,2,0:T(2,128)(2,1)} %copy.80) | copy-start | bytes 12292
  126.2 4.5 %copy-start.2 = (f32[2,64,2,64]{1,3,0,2:T(8,128)S(1)}, f32[2,64,2,64]{1,3,0,2:T(8,128)}, u32[]{:S(2)}) copy-start(f32[2,64,2,64]{1,3,0,2:T(8,128)} %constant.115.clone) | copy-start | bytes 196612
  126.2 4.8 %copy-start.5 = (f32[1,64,64]{2,1,0:T(8,128)S(1)}, f32[1,64,64]{2,1,0:T(8,128)}, u32[]{:S(2)}) copy-start(f32[1,64,64]{2,1,0:T(8,128)} %constant.127) | copy-start | bytes 49156
  126.2 4.8 %copy-start.6 = (f32[1,64,64]{2,1,0:T(8,128)S(1)}, f32[1,64,64]{2,1,0:T(8,128)}, u32[]{:S(2)}) copy-start(f32[1,64,64]{2,1,0:T(8,128)} %constant.128) | copy-start | bytes 49156
  126.2 5.1 %copy-start.3 = (f32[2,64,64]{2,1,0:T(8,128)S(1)}, f32[2,64,64]{2,1,0:T(8,128)}, u32[]{:S(2)}) copy-start(f32[2,64,64]{2,1,0:T(8,128)} %multiply_sine_fusion) | copy-start | bytes 98308
  126.2 5.1 %copy-start.4 = (f32[2,64,2,64]{3,1,0,2:T(8,128)S(1)}, f32[2,64,2,64]{3,1,0,2:T(8,128)}, u32[]{:S(2)}) copy-start(f32[2,64,2,64]{3,1,0,2:T(8,128)} %constant.118.clone) | copy-start | bytes 196612
  126.2 5.4 %copy-start.7 = (f32[2,64,64]{1,2,0:T(8,128)S(1)}, f32[2,64,64]{1,2,0:T(8,128)}, u32[]{:S(2)}) copy-start(f32[2,64,64]{1,2,0:T(8,128)} %constant.119.clone) | copy-start | bytes 98308
  132.7 58.1 %collective-permute-start.3 = (bf16[16,128,512]{2,1,0:T(8,128)(2,1)}, bf16[16,128,512]{2,1,0:T(8,128)(2,1)}, u32[]{:S(2)}, u32[]{:S(2)}) collective-permute-start(bf16[16,128,512]{2,1,0:T(8,128)(2,1)} %get-tuple-element.27.rest_0_), channel_id=1, source_target_pairs={{0,2},{2,0},{1,3},{3,1},{4,6},{6,4},{5,7},{7,5},{8,10},{10,8},{9,1... | collective-permute-start | bytes 6291464 | tf_op jit(solution)/shard_map/ppermute | solution.py:662
  150.6 53.6 %all-to-all-start = ((bf16[16,128,512]{2,1,0:T(8,128)(2,1)}), bf16[16,128,512]{2,1,0:T(8,128)(2,1)}, u32[]{:S(2)}, u32[]{:S(2)}) async-start(bf16[16,128,512]{2,1,0:T(8,128)(2,1)} %add_shares.4.rest_7_), calls=%async_computation | async-start | bytes 4194304 | tf_op jit(solution)/shard_map/all_to_all | solution.py:637
  186.0 52.2 %collective-permute-start.5 = (bf16[16,128,512]{2,1,0:T(8,128)(2,1)}, bf16[16,128,512]{2,1,0:T(8,128)(2,1)}, u32[]{:S(2)}, u32[]{:S(2)}) collective-permute-start(bf16[16,128,512]{2,1,0:T(8,128)(2,1)} %get-tuple-element.31.rest_0_), channel_id=1, source_target_pairs={{0,2},{2,0},{1,3},{3,1},{4,6},{6,4},{5,7},{7,5},{8,10},{10,8},{9,1... | collective-permute-start | bytes 6291464 | tf_op jit(solution)/shard_map/ppermute | solution.py:662
  204.2 52.8 %all-to-all-start.1 = ((bf16[16,128,512]{2,1,0:T(8,128)(2,1)}), bf16[16,128,512]{2,1,0:T(8,128)(2,1)}, u32[]{:S(2)}, u32[]{:S(2)}) async-start(bf16[16,128,512]{2,1,0:T(8,128)(2,1)} %add_shares.5.rest_8_), calls=%async_computation.1 | async-start | bytes 4194304 | tf_op jit(solution)/shard_map/all_to_all | solution.py:637
  261.6 53.4 %all-to-all-start.2 = ((bf16[16,128,512]{2,1,0:T(8,128)(2,1)}), bf16[16,128,512]{2,1,0:T(8,128)(2,1)S(1)}, u32[]{:S(2)}, u32[]{:S(2)}) async-start(bf16[16,128,512]{2,1,0:T(8,128)(2,1)} %add_shares.6), calls=%async_computation.2 | async-start | bytes 4194304 | tf_op jit(solution)/shard_map/all_to_all | solution.py:637
  266.7 48.3 %collective-permute-start.7 = (bf16[16,128,512]{2,1,0:T(8,128)(2,1)}, bf16[16,128,512]{2,1,0:T(8,128)(2,1)}, u32[]{:S(2)}, u32[]{:S(2)}) collective-permute-start(bf16[16,128,512]{2,1,0:T(8,128)(2,1)} %get-tuple-element.35.rest_0_), channel_id=1, source_target_pairs={{0,2},{2,0},{1,3},{3,1},{4,6},{6,4},{5,7},{7,5},{8,10},{10,8},{9,1... | collective-permute-start | bytes 6291464 | tf_op jit(solution)/shard_map/ppermute | solution.py:662
  315.0 1.4 copy-start
  321.0 5.9 %copy-start.8 = (s32[8]{0:T(128)S(1)}, s32[8]{0:T(128)}, u32[]{:S(2)}) copy-start(s32[8]{0:T(128)} %param.22) | copy-start | bytes 100
  321.0 53.5 %all-to-all-start.3 = ((bf16[16,128,512]{2,1,0:T(8,128)(2,1)}), bf16[16,128,512]{2,1,0:T(8,128)(2,1)S(1)}, u32[]{:S(2)}, u32[]{:S(2)}) async-start(bf16[16,128,512]{2,1,0:T(8,128)(2,1)} %add_shares.7), calls=%async_computation.3 | async-start | bytes 4194304 | tf_op jit(solution)/shard_map/all_to_all | solution.py:637
  374.4 1.3 copy-start.1
